TPU v7x, 1024 devices: a whole 4x4x32 slice. The times are simulated.
1024 devices in a mesh: row: 32 (over x, z_hi, core), col: 32 (over y, z_lo).
Axes of the slice: x: 4, y: 4, z: 32 (z_hi: 4, z_lo: 8; z = z_hi * 8 + z_lo), core: 2. Of those that a mesh axis runs over, the one named last changes fastest.
Arguments:
- saved_input: float32 [1280, 16384], P('row', 'col'), may hold values from -6 to 6
- out_grad: float32 [1280, 16384], P('col', 'row'), may hold values from -1.2 to 1.2
- weight: bfloat16 [16384, 16384], P('row', 'col'), may hold values from -0.046875 to 0.046875
- history_in: float32 [32, 32, 16], P('row', 'col'), may hold values from 2 to 8
- history_grad: float32 [32, 32, 16], P('row', 'col'), may hold values from 0.4 to 1.6
- slot_in: int32 [32, 32], P('row', 'col'), may hold values from 0 to 15
- slot_grad: int32 [32, 32], P('row', 'col'), may hold values from 0 to 15
- step_count: int32 [1], replicated, may hold values from 1 to 16
Outputs:
- weight_grad: float32 [16384, 16384], P('row', 'col')
- input_grad: bfloat16 [1280, 16384], P('row', 'col')
- new_history_in: float32 [32, 32, 16], P('row', 'col')
- new_history_grad: float32 [32, 32, 16], P('row', 'col')
All inputs are finite; a program needn't handle non-finite values.
Results may differ from a plain program's by a relative error of at most 0.023.
Values may be sent and summed in bfloat16 or wider, within the bound.
No kernel may reach another device: no remote copies, remote signals or barrier semaphores. Data moves between devices by JAX's collectives and lax.ppermute only.
A program may use at most 32 MiB of HBM per device.

v0:
```python
import jax
import jax.numpy as jnp
from jax import lax
from jax.sharding import PartitionSpec as P

code_max = 448.0


def delayed_scale(history, slot, count):
    depth = history.shape[-1]
    entry = jnp.arange(depth)
    age = jnp.mod(slot[..., None] - 1 - entry, depth)
    valid = age < count[0]
    held = jnp.max(jnp.where(valid, history, jnp.float32(0.0)), axis=-1)
    return code_max / held


def updated(history, slot, amax):
    depth = history.shape[-1]
    entry = jnp.arange(depth)
    return jnp.where(entry == slot[..., None], amax.reshape(1, 1, 1), history)


def shards(saved_input, out_grad, weight, history_in, history_grad, slot_in, slot_grad, step_count):
    scale_in = delayed_scale(history_in, slot_in, step_count).reshape(1)
    scale_grad = delayed_scale(history_grad, slot_grad, step_count).reshape(1)
    codes_in = jnp.clip(saved_input * scale_in[0], -code_max, code_max).astype(jnp.bfloat16)
    codes_grad = jnp.clip(out_grad * scale_grad[0], -code_max, code_max).astype(jnp.bfloat16)
    amax_in = jnp.max(jnp.abs(saved_input))
    amax_grad = jnp.max(jnp.abs(out_grad))
    local_in = codes_in.astype(jnp.float32) / scale_in[0]
    local_grad = codes_grad.astype(jnp.float32) / scale_grad[0]
    restored_in = lax.all_gather(local_in.astype(jnp.bfloat16), "row", axis=0, tiled=True).astype(
        local_in.dtype
    )
    restored_grad = lax.all_gather(
        local_grad.astype(jnp.bfloat16), "col", axis=0, tiled=True
    ).astype(local_grad.dtype)
    weight_float = weight.astype(jnp.float32)
    weight_grad = lax.dot_general(
        restored_grad, restored_in, (((0,), (0,)), ((), ())), precision=lax.Precision.HIGHEST
    )
    summed = lax.psum_scatter(
        jnp.dot(restored_grad, weight_float, precision=lax.Precision.HIGHEST).astype(jnp.bfloat16),
        "row",
        scatter_dimension=0,
        tiled=True,
    )
    new_history_in = updated(history_in, slot_in, amax_in)
    new_history_grad = updated(history_grad, slot_grad, amax_grad)
    return (weight_grad, summed, new_history_in, new_history_grad)


def solution(mesh):
    return jax.shard_map(
        shards,
        mesh=mesh,
        in_specs=(
            P("row", "col"),
            P("col", "row"),
            P("row", "col"),
            P("row", "col", None),
            P("row", "col", None),
            P("row", "col"),
            P("row", "col"),
            P(),
        ),
        out_specs=(P("row", "col"), P("row", "col"), P("row", "col", None), P("row", "col", None)),
        check_vma=False,
    )
```

profile of v0, /device:TPU:1, one launch (start us, length us, event | category | flops | bytes accessed | tf_op | source)
XLA Modules:
  0.0 551.8 jit_solution(9332696941706228556)
XLA Ops:
  7.2 0.0 copy-start
  7.2 0.0 all-gather.3.cloned.1.call-start
  9.2 1.4 fusion.2
  11.2 2.1 abs_reduce_fusion
  13.4 0.0 all-gather.3.cloned.1.call-update
  13.4 0.0 all-gather.5.cloned.1.call-start
  14.2 2.1 abs_reduce_fusion.1
  16.3 0.0 all-gather.5.cloned.1.call-update
  16.3 0.0 reduce-scatter.2.cloned.1.call-start
  16.4 218.7 %all-gather.3.cloned.1.call-done = bf16[1280,512]{1,0:T(8,128)(2,1)} async-done(((bf16[40,512]{1,0:T(8,128)(2,1)}), bf16[1280,512]{1,0:T(8,128)(2,1)}) %all-gather.3.cloned.1.call-update) | async-done | bytes 1310736 | tf_op jit(solution)/shard_map/all_gather | solution.py:36
  235.0 0.0 copy-done
  235.0 3.2 convolution_convert_fusion
  238.3 0.0 copy-start.1
  238.3 0.0 copy-start.2
  238.3 0.0 copy-start.3
  238.3 0.0 reduce-scatter.2.cloned.1.call-update
  238.3 0.6 copy-done.1
  238.9 1.1 compare_select_fusion.5
  240.0 0.0 copy-done.2
  240.0 1.1 compare_select_fusion.4
  241.1 135.8 %all-gather.5.cloned.1.call-done = bf16[1280,512]{1,0:T(8,128)(2,1)} async-done(((bf16[40,512]{1,0:T(8,128)(2,1)}), bf16[1280,512]{1,0:T(8,128)(2,1)}) %all-gather.5.cloned.1.call-update) | async-done | bytes 1310736 | tf_op jit(solution)/shard_map/all_gather | solution.py:33
  377.0 0.0 copy-done.3
  377.0 3.2 fusion.4
  380.1 165.1 %reduce-scatter.2.cloned.1.call-done = bf16[40,512]{1,0:T(8,128)(2,1)} async-done(((bf16[1280,512]{1,0:T(8,128)(2,1)}), bf16[40,512]{1,0:T(8,128)(2,1)}) %reduce-scatter.2.cloned.1.call-update) | async-done | bytes 40976 | tf_op jit(solution)/shard_map/reduce_scatter | solution.py:43
Async XLA Ops:
  7.2 227.9 %copy-start = (bf16[512,512]{1,0:T(8,128)(2,1)S(1)}, bf16[512,512]{1,0:T(8,128)(2,1)}, u32[]{:S(2)}) copy-start(bf16[512,512]{1,0:T(8,128)(2,1)} %param.10) | copy-start | bytes 1572868
  7.2 227.9 %all-gather.3.cloned.1.call-start = ((), (), s32[]{:S(2)}) async-start(), calls=%async_computation.1 | async-start | bytes 1351680 | tf_op jit(solution)/shard_map/all_gather | solution.py:36
  13.4 363.6 %all-gather.5.cloned.1.call-start = ((), (), s32[]{:S(2)}) async-start(), calls=%async_computation.2 | async-start | bytes 1351680 | tf_op jit(solution)/shard_map/all_gather | solution.py:33
  16.3 529.0 %reduce-scatter.2.cloned.1.call-start = ((), (), s32[]{:S(2)}) async-start(), calls=%async_computation.3 | async-start | bytes 1351680 | tf_op jit(solution)/shard_map/reduce_scatter | solution.py:43
  238.3 0.7 copy-start.1
  238.3 1.7 copy-start.2
  238.3 138.7 %copy-start.3 = (bf16[1280,512]{1,0:T(8,128)(2,1)S(1)}, bf16[1280,512]{1,0:T(8,128)(2,1)}, u32[]{:S(2)}) copy-start(bf16[1280,512]{1,0:T(8,128)(2,1)} %all-gather.3.cloned.1.call-done) | copy-start | bytes 3932164
Sparse Core Ops, SparseCore 0:
  13.5 221.4 all-gather.2
  239.9 137.0 all-gather.4
  383.1 162.1 reduce-scatter.1
where the time goes:
time: 553 us; the launch traced here: 552 us
  waiting for transfers between devices  520 us (94%)
  between operations  17.1 us (3%)
  other arithmetic  7.81 us (1%)
  matrix products  6.39 us (1%)
    all_gather x1, waiting for transfers between devices, shards(): lax.all_gather(local_grad.astype(jnp.bfloat16), 'col', axis=0, tiled=True)  219 us
    reduce_scatter x1, waiting for transfers between devices, shards(): lax.psum_scatter(jnp.dot(restored_grad, weight_float, precision=lax.Preci...  165 us
    all_gather x1, waiting for transfers between devices, shards(): lax.all_gather(local_in.astype(jnp.bfloat16), 'row', axis=0, tiled=True)  136 us
  transfers between devices with their start and end apart: 3, of which 3 were waited for; matrix products, arithmetic and copies ran while one was open for 2% of the time, Pallas kernels for 0%

commit v1 on v0

v1 whole, which is shorter than its diff:
```python
import jax
import jax.numpy as jnp
from jax import lax
from jax.sharding import PartitionSpec as P

code_max = 448.0
bf16 = jnp.bfloat16
f32 = jnp.float32


def row_of(x, h, c):
    return ((x % 4) * 4 + h % 4) * 2 + c % 2


def col_of(y, l):
    return (y % 4) * 8 + l


def row_pairs(dx, dh, dc):
    return [
        (row_of(x, h, c), row_of(x + dx, h + dh, c + dc)) for x in range(4) for h in range(4) for c in range(2)
    ]


along_x = [[row_of(x, h, c) for x in range(4)] for h in range(4) for c in range(2)]
along_y = [[col_of(y, l) for y in range(4)] for l in range(8)]
quads = [[col_of(y, 4 * s + k) for k in range(4)] for y in range(4) for s in range(2)]
halves = [(col_of(y, l), col_of(y, l ^ 4)) for y in range(4) for l in range(8)]


def delayed_scale(history, slot, count):
    depth = history.shape[-1]
    entry = jnp.arange(depth)
    age = jnp.mod(slot[..., None] - 1 - entry, depth)
    valid = age < count[0]
    held = jnp.max(jnp.where(valid, history, jnp.float32(0.0)), axis=-1)
    return code_max / held


def updated(history, slot, amax):
    depth = history.shape[-1]
    entry = jnp.arange(depth)
    return jnp.where(entry == slot[..., None], amax.reshape(1, 1, 1), history)


def restore(values, history, slot, count):
    scale = delayed_scale(history, slot, count).reshape(1)[0]
    codes = jnp.clip(values * scale, -code_max, code_max).astype(bf16)
    amax = jnp.max(jnp.abs(values))
    return (codes.astype(f32) / scale).astype(bf16), updated(history, slot, amax)


def spread(block, axis_name, groups):
    n = len(groups[0])
    copies = jnp.broadcast_to(block[None], (n, *block.shape))
    return lax.all_to_all(copies, axis_name, 0, 0, axis_index_groups=groups)


def shards(saved_input, out_grad, weight, history_in, history_grad, slot_in, slot_grad, step_count):
    row = lax.axis_index("row")
    col = lax.axis_index("col")
    h = row // 2 % 4
    core = row % 2
    side = col % 8 // 4

    grad, new_history_grad = restore(out_grad, history_grad, slot_grad, step_count)
    kept, new_history_in = restore(saved_input, history_in, slot_in, step_count)

    with jax.named_scope("grad_z"):
        far = lax.ppermute(grad, "col", halves)
        first = side == 0
        pair = jnp.stack([jnp.where(first, grad, far), jnp.where(first, far, grad)])
        line = spread(pair.reshape(80, 512), "col", quads)
    with jax.named_scope("in_z"):
        moved = [lax.ppermute(kept, "row", row_pairs(0, d, 0)) for d in (2, 1, 3)]
    with jax.named_scope("grad_y"):
        grads = spread(line.reshape(320, 512), "col", along_y)
    grads = grads.reshape(4, 2, 2, 80, 512)
    own = lax.dynamic_index_in_dim(grads, core, 2, keepdims=False).reshape(640, 512)
    other = lax.dynamic_index_in_dim(grads, 1 - core, 2, keepdims=False).reshape(640, 512)

    with jax.named_scope("sum_core"):
        sent = jnp.dot(other, weight, preferred_element_type=f32).astype(bf16)
        got = lax.ppermute(sent, "row", row_pairs(0, 0, 1))
        part = jnp.dot(own, weight, preferred_element_type=f32) + got.astype(f32)
    with jax.named_scope("sum_x"):
        across = lax.all_to_all(
            part.astype(bf16).reshape(4, 160, 512), "row", 0, 0, axis_index_groups=along_x
        )
        part = jnp.sum(across.astype(f32), axis=0).reshape(2, 2, 40, 512)
    with jax.named_scope("sum_z"):

        def block_of(at):
            at = at % 4
            return lax.dynamic_index_in_dim(
                lax.dynamic_index_in_dim(part, at % 2, 0, keepdims=False), at // 2, 0, keepdims=False
            )

        total = block_of(h)
        for d in (2, 1, 3):
            total += lax.ppermute(block_of(h + d).astype(bf16), "row", row_pairs(0, d, 0)).astype(f32)
        input_grad = total.astype(bf16)

    with jax.named_scope("in_x"):
        by_distance = dict(zip((2, 1, 3), moved)) | {0: kept}
        stacked = jnp.stack([by_distance[d] for d in range(4)])
        order = [lax.dynamic_index_in_dim(stacked, (h - p) % 4, 0, keepdims=False) for p in (0, 2, 1, 3)]
        lines = jnp.concatenate(order, axis=0)
        own_in = lax.all_gather(lines, "row", axis=0, tiled=True, axis_index_groups=along_x)
    with jax.named_scope("in_core"):
        other_in = lax.ppermute(own_in, "row", row_pairs(0, 0, 1))
    with jax.named_scope("outer"):
        contract = (((0,), (0,)), ((), ()))
        weight_grad = lax.dot_general(own, own_in, contract, preferred_element_type=f32)
        weight_grad += lax.dot_general(other, other_in, contract, preferred_element_type=f32)
    return (weight_grad, input_grad, new_history_in, new_history_grad)


def solution(mesh):
    return jax.shard_map(
        shards,
        mesh=mesh,
        in_specs=(
            P("row", "col"),
            P("col", "row"),
            P("row", "col"),
            P("row", "col", None),
            P("row", "col", None),
            P("row", "col"),
            P("row", "col"),
            P(),
        ),
        out_specs=(P("row", "col"), P("row", "col"), P("row", "col", None), P("row", "col", None)),
        check_vma=False,
    )
```

time: 553 us -> 159 us (0.29)
  waiting for transfers between devices: 520 us -> 18.2 us
  starting transfers between devices: 0.12 us -> 98.5 us
  blocking collectives: 0 us -> 23.3 us
  between operations: 17.1 us -> 4.29 us
    all_gather x2 -> x0, waiting for transfers between devices: 355 us -> none  [the longest x1 219 us: shards(): lax.all_gather(local_grad.astype(jnp.bfloat16), 'col', axis=0, tiled=True)]
    reduce_scatter x1 -> x0, waiting for transfers between devices: 165 us -> none  [shards(): lax.psum_scatter(jnp.dot(restored_grad, weight_float, precision=lax.Preci...]
    ppermute x0 -> x9, starting transfers between devices: none -> 87.9 us  [the longest x3 35.4 us: shards(): moved = [lax.ppermute(kept, 'row', row_pairs(0, d, 0)) for d in (2, 1, 3)]]
    all_to_all x0 -> x1, blocking collectives: none -> 12.7 us  [spread(): return lax.all_to_all(copies, axis_name, 0, 0, axis_index_groups=groups)]
    all_to_all x0 -> x2, starting transfers between devices: none -> 10.6 us  [the longest x1 7.09 us: spread(): return lax.all_to_all(copies, axis_name, 0, 0, axis_index_groups=groups)]
    all_gather x0 -> x1, blocking collectives: none -> 10.5 us  [shards(): lax.all_gather(lines, 'row', axis=0, tiled=True, axis_index_groups=along_x)]
    all_to_all x0 -> x2, waiting for transfers between devices: none -> 9.2 us  [the longest x1 9.19 us: shards(): lax.all_to_all(part.astype(bf16).reshape(4, 160, 512), 'row', 0, 0, axis_...]
    ppermute x0 -> x9, waiting for transfers between devices: none -> 8.97 us  [the longest x3 7.62 us: shards(): lax.ppermute(block_of(h + d).astype(bf16), 'row', row_pairs(0, d, 0))]
  transfers between devices with their start and end apart: 3 -> 11, of which waited for: 3 -> 4; matrix products, arithmetic and copies ran while one was open for 2% -> 5% of each run, Pallas kernels for 0% -> 0%
where the time goes in v1:
time: 159 us; the launch traced here: 158 us
  starting transfers between devices  98.5 us (62%)
  blocking collectives  23.3 us (15%)
  waiting for transfers between devices  18.2 us (11%)
  other arithmetic  6.6 us (4%)
  matrix products  5.11 us (3%)
  between operations  4.29 us (3%)
  local copies, waits for them, and re-layouts  2.22 us (1%)
    ppermute x3, starting transfers between devices, shards(): moved = [lax.ppermute(kept, 'row', row_pairs(0, d, 0)) for d in (2, 1, 3)]  35.4 us
    ppermute x3, starting transfers between devices, shards(): lax.ppermute(block_of(h + d).astype(bf16), 'row', row_pairs(0, d, 0))  26.9 us
    all_to_all x1, blocking collectives, spread(): return lax.all_to_all(copies, axis_name, 0, 0, axis_index_groups=groups)  12.7 us
    all_gather x1, blocking collectives, shards(): lax.all_gather(lines, 'row', axis=0, tiled=True, axis_index_groups=along_x)  10.5 us
    ppermute x1, starting transfers between devices, shards(): far = lax.ppermute(grad, 'col', halves)  9.63 us
    all_to_all x1, waiting for transfers between devices, shards(): lax.all_to_all(part.astype(bf16).reshape(4, 160, 512), 'row', 0, 0, axis_...  9.19 us
    ppermute x1, starting transfers between devices, shards(): other_in = lax.ppermute(own_in, 'row', row_pairs(0, 0, 1))  8.5 us
    ppermute x3, waiting for transfers between devices, shards(): lax.ppermute(block_of(h + d).astype(bf16), 'row', row_pairs(0, d, 0))  7.62 us
  transfers between devices with their start and end apart: 11, of which 4 were waited for; matrix products, arithmetic and copies ran while one was open for 5% of the time, Pallas kernels for 0%

profile of v1, /device:TPU:1, one launch (start us, length us, event | category | flops | bytes accessed | tf_op | source)
XLA Modules:
  0.0 158.1 jit_solution(14198562919075488091)
XLA Ops:
  2.6 1.4 fusion.8
  4.7 1.5 abs_reduce_fusion
  6.2 9.6 %collective-permute-start = (bf16[40,512]{1,0:T(8,128)(2,1)S(1)}, bf16[40,512]{1,0:T(8,128)(2,1)S(1)}, u32[]{:S(2)}, u32[]{:S(2)}) collective-permute-start(bf16[40,512]{1,0:T(8,128)(2,1)S(1)} %get-tuple-element.14), channel_id=1, source_target_pairs={{0,4},{1,5},{2,6},{3,7},{4,0},{5,1},{6,2},{7,3},{8,12},{9,13},{10,... | collective-permute-start | bytes 122888 | tf_op jit(solution)/shard_map/grad_z/ppermute | solution.py:70
  15.8 1.3 collective-permute-done
  17.3 12.7 %all_to_all.15 = bf16[4,80,512]{2,1,0:T(8,128)(2,1)S(1)} all-to-all(bf16[4,80,512]{2,1,0:T(8,128)(2,1)S(1)} %broadcast_in_dim.42), channel_id=1, replica_groups={{0,1,2,3},{4,5,6,7},{8,9,10,11},{12,13,14,15},{16,17,18,19},{20,21,22,2..., dimensions={0} | all-to-all | bytes 655360 | tf_op jit(solution)/shard_map/grad_z/all_to_all | solution.py:56
  30.0 1.2 broadcast_in_dim.44
  31.2 7.1 %all-to-all-start.1 = ((bf16[4,320,512]{2,1,0:T(8,128)(2,1)}), bf16[4,320,512]{2,1,0:T(8,128)(2,1)S(1)}, u32[]{:S(2)}, u32[]{:S(2)}) async-start(bf16[4,320,512]{2,1,0:T(8,128)(2,1)} %broadcast_in_dim.44), calls=%async_computation.1 | async-start | bytes 2621440 | tf_op jit(solution)/shard_map/grad_y/all_to_all | solution.py:56
  39.6 15.4 %collective-permute-start.1 = (bf16[40,512]{1,0:T(8,128)(2,1)S(1)}, bf16[40,512]{1,0:T(8,128)(2,1)S(1)}, u32[]{:S(2)}, u32[]{:S(2)}) collective-permute-start(bf16[40,512]{1,0:T(8,128)(2,1)S(1)} %get-tuple-element.16), channel_id=1, source_target_pairs={{0,64},{32,96},{64,128},{96,160},{128,192},{160,224},{192,0},{224,... | collective-permute-start | bytes 122888 | tf_op jit(solution)/shard_map/in_z/ppermute | solution.py:75
  55.0 11.8 %collective-permute-start.2 = (bf16[40,512]{1,0:T(8,128)(2,1)S(1)}, bf16[40,512]{1,0:T(8,128)(2,1)S(1)}, u32[]{:S(2)}, u32[]{:S(2)}) collective-permute-start(bf16[40,512]{1,0:T(8,128)(2,1)S(1)} %get-tuple-element.16), channel_id=1, source_target_pairs={{0,128},{32,160},{64,192},{96,224},{128,0},{160,32},{192,64},{224,... | collective-permute-start | bytes 122888 | tf_op jit(solution)/shard_map/in_z/ppermute | solution.py:75
  66.8 8.2 %collective-permute-start.3 = (bf16[40,512]{1,0:T(8,128)(2,1)S(1)}, bf16[40,512]{1,0:T(8,128)(2,1)S(1)}, u32[]{:S(2)}, u32[]{:S(2)}) collective-permute-start(bf16[40,512]{1,0:T(8,128)(2,1)S(1)} %get-tuple-element.16), channel_id=1, source_target_pairs={{0,192},{32,224},{64,0},{96,32},{128,64},{160,96},{192,128},{224,1... | collective-permute-start | bytes 122888 | tf_op jit(solution)/shard_map/in_z/ppermute | solution.py:75
  75.2 0.8 copy-done.1
  76.5 7.4 %collective-permute-start.5 = (bf16[640,512]{1,0:T(8,128)(2,1)S(1)}, bf16[640,512]{1,0:T(8,128)(2,1)S(1)}, u32[]{:S(2)}, u32[]{:S(2)}) collective-permute-start(bf16[640,512]{1,0:T(8,128)(2,1)S(1)} %convolution_convert_fusion), channel_id=1, source_target_pairs={{0,32},{32,0},{64,96},{96,64},{128,160},{160,128},{192,224},{224,1... | collective-permute-start | bytes 1966088 | tf_op jit(solution)/shard_map/sum_core/ppermute | solution.py:84
  84.0 1.2 compare_select_fusion.4
  85.2 10.5 %all_gather.3 = bf16[640,512]{1,0:T(8,128)(2,1)S(1)} all-gather(bf16[160,512]{1,0:T(8,128)(2,1)S(1)} %pad_maximum_fusion.1), channel_id=1, replica_groups={{0,256,512,768},{32,288,544,800},{64,320,576,832},{96,352,608,864},{128..., dimensions={0}, use_global_device_ids=true | all-gather | bytes 819200 | tf_op jit(solution)/shard_map/in_x/all_gather | solution.py:109
  95.8 8.5 %collective-permute-start.4 = (bf16[640,512]{1,0:T(8,128)(2,1)S(1)}, bf16[640,512]{1,0:T(8,128)(2,1)}, u32[]{:S(2)}, u32[]{:S(2)}) collective-permute-start(bf16[640,512]{1,0:T(8,128)(2,1)S(1)} %all_gather.3), channel_id=1, source_target_pairs={{0,32},{32,0},{64,96},{96,64},{128,160},{160,128},{192,224},{224,1... | collective-permute-start | bytes 1966088 | tf_op jit(solution)/shard_map/in_core/ppermute | solution.py:111
  104.3 1.4 add_convert_fusion
  105.7 3.5 %all-to-all-start.2 = ((bf16[4,160,512]{2,1,0:T(8,128)(2,1)}), bf16[4,160,512]{2,1,0:T(8,128)(2,1)S(1)}, u32[]{:S(2)}, u32[]{:S(2)}) async-start(bf16[4,160,512]{2,1,0:T(8,128)(2,1)} %bitcast.18), calls=%async_computation.2 | async-start | bytes 1310720 | tf_op jit(solution)/shard_map/sum_x/all_to_all | solution.py:87
  109.2 1.2 compare_select_fusion.5
  110.9 9.2 %all-to-all-done.2 = bf16[4,160,512]{2,1,0:T(8,128)(2,1)S(1)} async-done(((bf16[4,160,512]{2,1,0:T(8,128)(2,1)}), bf16[4,160,512]{2,1,0:T(8,128)(2,1)S(1)}, u32[]{:S(2)}, u32[]{:S(2)}) %all-to-all-start.2) | async-done | bytes 655392 | tf_op jit(solution)/shard_map/sum_x/all_to_all | solution.py:87
  120.2 12.9 %collective-permute-start.6 = (bf16[40,512]{1,0:T(8,128)(2,1)S(1)}, bf16[40,512]{1,0:T(8,128)(2,1)S(1)}, u32[]{:S(2)}, u32[]{:S(2)}) collective-permute-start(bf16[40,512]{1,0:T(8,128)(2,1)S(1)} %get-tuple-element.6), channel_id=1, source_target_pairs={{0,128},{32,160},{64,192},{96,224},{128,0},{160,32},{192,64},{224,... | collective-permute-start | bytes 122888 | tf_op jit(solution)/shard_map/sum_z/ppermute | solution.py:101
  133.2 6.6 %collective-permute-start.7 = (bf16[40,512]{1,0:T(8,128)(2,1)S(1)}, bf16[40,512]{1,0:T(8,128)(2,1)S(1)}, u32[]{:S(2)}, u32[]{:S(2)}) collective-permute-start(bf16[40,512]{1,0:T(8,128)(2,1)S(1)} %get-tuple-element.8), channel_id=1, source_target_pairs={{0,64},{32,96},{64,128},{96,160},{128,192},{160,224},{192,0},{224,... | collective-permute-start | bytes 122888 | tf_op jit(solution)/shard_map/sum_z/ppermute | solution.py:101
  139.7 7.4 %collective-permute-start.8 = (bf16[40,512]{1,0:T(8,128)(2,1)S(1)}, bf16[40,512]{1,0:T(8,128)(2,1)S(1)}, u32[]{:S(2)}, u32[]{:S(2)}) collective-permute-start(bf16[40,512]{1,0:T(8,128)(2,1)S(1)} %get-tuple-element.7), channel_id=1, source_target_pairs={{0,192},{32,224},{64,0},{96,32},{128,64},{160,96},{192,128},{224,1... | collective-permute-start | bytes 122888 | tf_op jit(solution)/shard_map/sum_z/ppermute | solution.py:101
  147.2 2.7 %convolution_add_fusion = f32[512,512]{1,0:T(8,128)} fusion(f32[512,512]{1,0:T(8,128)S(1)} %fusion.10, bf16[640,512]{1,0:T(8,128)(2,1)S(1)} %bitcast.57, bf16[640,512]{1,0:T(8,128)(2,1)} %collective-permute-done.4), kind=kOutput, calls=%fused_computation | convolution fusion | flops 335806464 | bytes 3407872 | tf_op jit(solution)/shard_map/outer/dot_general | solution.py:115
  150.4 7.0 %collective-permute-done.8 = bf16[40,512]{1,0:T(8,128)(2,1)S(1)} collective-permute-done((bf16[40,512]{1,0:T(8,128)(2,1)S(1)}, bf16[40,512]{1,0:T(8,128)(2,1)S(1)}, u32[]{:S(2)}, u32[]{:S(2)}) %collective-permute-start.8) | collective-permute-done | bytes 40992 | tf_op jit(solution)/shard_map/sum_z/ppermute | solution.py:101
  (32 shorter events, 3.3 us)
Async XLA Ops:
  0.6 75.3 %copy-start = (bf16[512,512]{1,0:T(8,128)(2,1)S(1)}, bf16[512,512]{1,0:T(8,128)(2,1)}, u32[]{:S(2)}) copy-start(bf16[512,512]{1,0:T(8,128)(2,1)} %param.10) | copy-start | bytes 1572868
  6.2 11.0 %collective-permute-start = (bf16[40,512]{1,0:T(8,128)(2,1)S(1)}, bf16[40,512]{1,0:T(8,128)(2,1)S(1)}, u32[]{:S(2)}, u32[]{:S(2)}) collective-permute-start(bf16[40,512]{1,0:T(8,128)(2,1)S(1)} %get-tuple-element.14), channel_id=1, source_target_pairs={{0,4},{1,5},{2,6},{3,7},{4,0},{5,1},{6,2},{7,3},{8,12},{9,13},{10,... | collective-permute-start | bytes 122888 | tf_op jit(solution)/shard_map/grad_z/ppermute | solution.py:70
  31.2 7.8 %copy-start.3 = (f32[40,512]{1,0:T(8,128)S(1)}, f32[40,512]{1,0:T(8,128)}, u32[]{:S(2)}) copy-start(f32[40,512]{1,0:T(8,128)} %param.8) | copy-start | bytes 245764
  31.2 43.9 %all-to-all-start.1 = ((bf16[4,320,512]{2,1,0:T(8,128)(2,1)}), bf16[4,320,512]{2,1,0:T(8,128)(2,1)S(1)}, u32[]{:S(2)}, u32[]{:S(2)}) async-start(bf16[4,320,512]{2,1,0:T(8,128)(2,1)} %broadcast_in_dim.44), calls=%async_computation.1 | async-start | bytes 2621440 | tf_op jit(solution)/shard_map/grad_y/all_to_all | solution.py:56
  39.6 45.5 %collective-permute-start.1 = (bf16[40,512]{1,0:T(8,128)(2,1)S(1)}, bf16[40,512]{1,0:T(8,128)(2,1)S(1)}, u32[]{:S(2)}, u32[]{:S(2)}) collective-permute-start(bf16[40,512]{1,0:T(8,128)(2,1)S(1)} %get-tuple-element.16), channel_id=1, source_target_pairs={{0,64},{32,96},{64,128},{96,160},{128,192},{160,224},{192,0},{224,... | collective-permute-start | bytes 122888 | tf_op jit(solution)/shard_map/in_z/ppermute | solution.py:75
  55.0 30.1 %collective-permute-start.2 = (bf16[40,512]{1,0:T(8,128)(2,1)S(1)}, bf16[40,512]{1,0:T(8,128)(2,1)S(1)}, u32[]{:S(2)}, u32[]{:S(2)}) collective-permute-start(bf16[40,512]{1,0:T(8,128)(2,1)S(1)} %get-tuple-element.16), channel_id=1, source_target_pairs={{0,128},{32,160},{64,192},{96,224},{128,0},{160,32},{192,64},{224,... | collective-permute-start | bytes 122888 | tf_op jit(solution)/shard_map/in_z/ppermute | solution.py:75
  66.8 18.3 %collective-permute-start.3 = (bf16[40,512]{1,0:T(8,128)(2,1)S(1)}, bf16[40,512]{1,0:T(8,128)(2,1)S(1)}, u32[]{:S(2)}, u32[]{:S(2)}) collective-permute-start(bf16[40,512]{1,0:T(8,128)(2,1)S(1)} %get-tuple-element.16), channel_id=1, source_target_pairs={{0,192},{32,224},{64,0},{96,32},{128,64},{160,96},{192,128},{224,1... | collective-permute-start | bytes 122888 | tf_op jit(solution)/shard_map/in_z/ppermute | solution.py:75
  75.1 0.8 copy-start.1
  75.2 8.8 %copy-start.4 = (f32[1,1,16]{2,1,0:T(1,128)S(1)}, f32[1,1,16]{2,1,0:T(1,128)}, u32[]{:S(2)}) copy-start(f32[1,1,16]{2,1,0:T(1,128)} %param.12) | copy-start | bytes 196
  76.5 27.8 %collective-permute-start.5 = (bf16[640,512]{1,0:T(8,128)(2,1)S(1)}, bf16[640,512]{1,0:T(8,128)(2,1)S(1)}, u32[]{:S(2)}, u32[]{:S(2)}) collective-permute-start(bf16[640,512]{1,0:T(8,128)(2,1)S(1)} %convolution_convert_fusion), channel_id=1, source_target_pairs={{0,32},{32,0},{64,96},{96,64},{128,160},{160,128},{192,224},{224,1... | collective-permute-start | bytes 1966088 | tf_op jit(solution)/shard_map/sum_core/ppermute | solution.py:84
  95.8 51.4 %collective-permute-start.4 = (bf16[640,512]{1,0:T(8,128)(2,1)S(1)}, bf16[640,512]{1,0:T(8,128)(2,1)}, u32[]{:S(2)}, u32[]{:S(2)}) collective-permute-start(bf16[640,512]{1,0:T(8,128)(2,1)S(1)} %all_gather.3), channel_id=1, source_target_pairs={{0,32},{32,0},{64,96},{96,64},{128,160},{160,128},{192,224},{224,1... | collective-permute-start | bytes 1966088 | tf_op jit(solution)/shard_map/in_core/ppermute | solution.py:111
  104.3 4.9 %copy-start.5 = (f32[1,1,16]{2,1,0:T(1,128)S(1)}, f32[1,1,16]{2,1,0:T(1,128)}, u32[]{:S(2)}) copy-start(f32[1,1,16]{2,1,0:T(1,128)} %param.11) | copy-start | bytes 196
  105.7 14.5 %all-to-all-start.2 = ((bf16[4,160,512]{2,1,0:T(8,128)(2,1)}), bf16[4,160,512]{2,1,0:T(8,128)(2,1)S(1)}, u32[]{:S(2)}, u32[]{:S(2)}) async-start(bf16[4,160,512]{2,1,0:T(8,128)(2,1)} %bitcast.18), calls=%async_computation.2 | async-start | bytes 1310720 | tf_op jit(solution)/shard_map/sum_x/all_to_all | solution.py:87
  110.9 36.3 %copy-start.2 = (bf16[4,2,1,80,512]{4,3,2,1,0:T(8,128)(2,1)S(1)}, bf16[4,2,1,80,512]{4,3,2,1,0:T(8,128)(2,1)}, u32[]{:S(2)}) copy-start(bf16[4,2,1,80,512]{4,3,2,1,0:T(8,128)(2,1)} %copy-done.1) | copy-start | bytes 1966084
  120.2 29.6 %collective-permute-start.6 = (bf16[40,512]{1,0:T(8,128)(2,1)S(1)}, bf16[40,512]{1,0:T(8,128)(2,1)S(1)}, u32[]{:S(2)}, u32[]{:S(2)}) collective-permute-start(bf16[40,512]{1,0:T(8,128)(2,1)S(1)} %get-tuple-element.6), channel_id=1, source_target_pairs={{0,128},{32,160},{64,192},{96,224},{128,0},{160,32},{192,64},{224,... | collective-permute-start | bytes 122888 | tf_op jit(solution)/shard_map/sum_z/ppermute | solution.py:101
  133.2 17.3 %collective-permute-start.7 = (bf16[40,512]{1,0:T(8,128)(2,1)S(1)}, bf16[40,512]{1,0:T(8,128)(2,1)S(1)}, u32[]{:S(2)}, u32[]{:S(2)}) collective-permute-start(bf16[40,512]{1,0:T(8,128)(2,1)S(1)} %get-tuple-element.8), channel_id=1, source_target_pairs={{0,64},{32,96},{64,128},{96,160},{128,192},{160,224},{192,0},{224,... | collective-permute-start | bytes 122888 | tf_op jit(solution)/shard_map/sum_z/ppermute | solution.py:101
  139.7 17.7 %collective-permute-start.8 = (bf16[40,512]{1,0:T(8,128)(2,1)S(1)}, bf16[40,512]{1,0:T(8,128)(2,1)S(1)}, u32[]{:S(2)}, u32[]{:S(2)}) collective-permute-start(bf16[40,512]{1,0:T(8,128)(2,1)S(1)} %get-tuple-element.7), channel_id=1, source_target_pairs={{0,192},{32,224},{64,0},{96,32},{128,64},{160,96},{192,128},{224,1... | collective-permute-start | bytes 122888 | tf_op jit(solution)/shard_map/sum_z/ppermute | solution.py:101

commit v2 on v1

v2 whole, which is shorter than its diff:
```python
import jax
import jax.numpy as jnp
from jax import lax
from jax.experimental import pallas as pl
from jax.experimental.pallas import tpu as pltpu
from jax.sharding import PartitionSpec as P

code_max = 448.0
bf16 = jnp.bfloat16
f32 = jnp.float32


def row_of(x, h, c):
    return ((x % 4) * 4 + h % 4) * 2 + c % 2


def col_of(y, l):
    return (y % 4) * 8 + l


def row_pairs(dx, dh, dc):
    return [
        (row_of(x, h, c), row_of(x + dx, h + dh, c + dc)) for x in range(4) for h in range(4) for c in range(2)
    ]


def col_pairs(dy):
    return [(col_of(y, l), col_of(y + dy, l)) for y in range(4) for l in range(8)]


along_x = [[row_of(x, h, c) for x in range(4)] for h in range(4) for c in range(2)]
along_z = [[row_of(x, h, c) for h in range(4)] for x in range(4) for c in range(2)]
quads = [[col_of(y, 4 * s + k) for k in range(4)] for y in range(4) for s in range(2)]
halves = [(col_of(y, l), col_of(y, l ^ 4)) for y in range(4) for l in range(8)]


def restore_kernel(count_ref, slot_ref, values_ref, history_ref, restored_ref, updated_ref):
    slot = slot_ref[0, 0]
    history = history_ref[0]
    entry = lax.broadcasted_iota(jnp.int32, history.shape, 1)
    age = jnp.bitwise_and(slot - 1 - entry, history.shape[1] - 1)
    valid = age < count_ref[0]
    held = jnp.max(jnp.where(valid, history, 0.0), axis=1, keepdims=True)
    scale = code_max / held
    values = values_ref[...]
    codes = jnp.clip(values * scale, -code_max, code_max).astype(bf16)
    restored_ref[...] = (codes.astype(f32) / scale).astype(bf16)
    amax = jnp.max(jnp.max(jnp.abs(values), axis=0, keepdims=True), axis=1, keepdims=True)
    updated_ref[0] = jnp.where(entry == slot, amax, history)


def restore(values, history, slot, count):
    smem = pl.BlockSpec(memory_space=pltpu.SMEM)
    vmem = pl.BlockSpec(memory_space=pltpu.VMEM)
    return pl.pallas_call(
        restore_kernel,
        out_shape=(
            jax.ShapeDtypeStruct(values.shape, bf16),
            jax.ShapeDtypeStruct(history.shape, f32),
        ),
        in_specs=[smem, smem, vmem, vmem],
        out_specs=(vmem, vmem),
        compiler_params=pltpu.CompilerParams(vmem_limit_bytes=4 * 2**20),
        cost_estimate=pl.CostEstimate(flops=200000, bytes_accessed=130000, transcendentals=0),
    )(count, slot, values, history)


def call(kernel, outs, smem, vmem, scratch=()):
    place = [pl.BlockSpec(memory_space=pltpu.SMEM)] * len(smem) + [pl.BlockSpec(memory_space=pltpu.VMEM)] * len(vmem)
    return pl.pallas_call(
        kernel,
        out_shape=[jax.ShapeDtypeStruct(shape, kind) for shape, kind in outs],
        in_specs=place,
        out_specs=[pl.BlockSpec(memory_space=pltpu.VMEM)] * len(outs),
        scratch_shapes=scratch,
        compiler_params=pltpu.CompilerParams(vmem_limit_bytes=16 * 2**20),
        cost_estimate=pl.CostEstimate(flops=1024, bytes_accessed=1024, transcendentals=0),
    )(*smem, *vmem)


def other_kernel(y, core, d0, d1, d2, d3, weight, own, other, sent):
    for d, ref in enumerate((d0, d1, d2, d3)):
        at = jnp.bitwise_and(y[0] - d, 3)
        for k in range(2):
            own[at, k] = ref[k, core[0]]
            other[at, k] = ref[k, 1 - core[0]]
    rows = other[...].reshape(640, 512)
    sent[...] = jnp.dot(rows, weight[...], preferred_element_type=f32).astype(bf16)


def own_kernel(x, own, weight, got, e0, e1, e2, e3, held):
    total = jnp.dot(own[...], weight[...], preferred_element_type=f32) + got[...].astype(f32)
    held[...] = total.astype(bf16).reshape(4, 160, 512)
    for e, ref in enumerate((e0, e1, e2, e3)):
        ref[...] = held[jnp.bitwise_and(x[0] + e, 3)]


def line_kernel(e0, e1, e2, e3, blocks):
    total = e0[...].astype(f32)
    for ref in (e1, e2, e3):
        total += ref[...].astype(f32)
    for k in range(2):
        for s in range(2):
            at = 40 * (2 * k + s)
            blocks[2 * s + k] = total[at : at + 40].astype(bf16)


def outer_kernel(own, own_in, other, other_in, grad):
    contract = (((0,), (0,)), ((), ()))
    grad[...] = lax.dot_general(
        own[...], own_in[...], contract, preferred_element_type=f32
    ) + lax.dot_general(other[...], other_in[...], contract, preferred_element_type=f32)


def spread(block, axis_name, groups):
    n = len(groups[0])
    copies = jnp.broadcast_to(block[None], (n, *block.shape))
    return lax.all_to_all(copies, axis_name, 0, 0, axis_index_groups=groups)


def shards(saved_input, out_grad, weight, history_in, history_grad, slot_in, slot_grad, step_count):
    row = lax.axis_index("row")
    col = lax.axis_index("col")
    h = jnp.bitwise_and(row >> 1, 3)
    core = jnp.bitwise_and(row, 1)
    first = jnp.bitwise_and(col, 4) == 0

    grad, new_history_grad = restore(out_grad, history_grad, slot_grad, step_count)
    kept, new_history_in = restore(saved_input, history_in, slot_in, step_count)

    with jax.named_scope("grad_z"):
        far = lax.ppermute(grad, "col", halves)
        pair = jnp.stack([jnp.where(first, grad, far), jnp.where(first, far, grad)])
        line = spread(pair.reshape(80, 512), "col", quads)
    line, kept = lax.optimization_barrier((line, kept))
    with jax.named_scope("grad_y"):
        line = line.reshape(320, 512)
        passed = [lax.ppermute(line, "col", col_pairs(d)) for d in (1, 2, 3)]
    with jax.named_scope("in_z"):
        lines = spread(kept, "row", along_z)
        lines = lines.reshape(2, 2, 40, 512).swapaxes(0, 1).reshape(160, 512)
    half = ((4, 2, 80, 512), bf16)
    whole = ((640, 512), bf16)
    taken = [b.reshape(2, 2, 80, 512) for b in (line, *passed)]
    own, other, sent = call(
        other_kernel, [half, half, whole], [(col >> 3).reshape(1), core.reshape(1)], [*taken, weight]
    )
    own, other = own.reshape(640, 512), other.reshape(640, 512)

    with jax.named_scope("sum_core"):
        got = lax.ppermute(sent, "row", row_pairs(0, 0, 1))
    with jax.named_scope("sum_x"):
        parts = call(
            own_kernel,
            [((160, 512), bf16)] * 4,
            [(row >> 3).reshape(1)],
            [own, weight, got],
            [pltpu.VMEM((4, 160, 512), bf16)],
        )
        across = [lax.ppermute(parts[e], "row", row_pairs(e, 0, 0)) for e in (1, 2, 3)]
        (blocks,) = call(line_kernel, [((4, 40, 512), bf16)], [], [parts[0], *across])
    blocks, lines = lax.optimization_barrier((blocks, lines))
    with jax.named_scope("sum_z"):
        across = lax.all_to_all(blocks, "row", 0, 0, axis_index_groups=along_z)
        input_grad = jnp.sum(across.astype(f32), axis=0).astype(bf16)

    with jax.named_scope("in_x"):
        own_in = lax.all_gather(lines, "row", axis=0, tiled=True, axis_index_groups=along_x)
    with jax.named_scope("in_core"):
        other_in = lax.ppermute(own_in, "row", row_pairs(0, 0, 1))
    with jax.named_scope("outer"):
        (weight_grad,) = call(outer_kernel, [((512, 512), f32)], [], [own, own_in, other, other_in])
    return (weight_grad, input_grad, new_history_in, new_history_grad)


def solution(mesh):
    return jax.shard_map(
        shards,
        mesh=mesh,
        in_specs=(
            P("row", "col"),
            P("col", "row"),
            P("row", "col"),
            P("row", "col", None),
            P("row", "col", None),
            P("row", "col"),
            P("row", "col"),
            P(),
        ),
        out_specs=(P("row", "col"), P("row", "col"), P("row", "col", None), P("row", "col", None)),
        check_vma=False,
    )
```

time: 159 us -> 142 us (0.89)
  the two profiles are of different devices: /device:TPU:1 before, /device:TPU:42 now
where the time goes in v2:
time: 142 us
  starting transfers between devices  81.3 us (57%)
  waiting for transfers between devices  36.1 us (25%)
  blocking collectives  12.6 us (9%)
  Pallas kernels  5.85 us (4%)
  between operations  2.8 us (2%)
  local copies, waits for them, and re-layouts  2.33 us (2%)
    all_to_all x2, starting transfers between devices, spread(): return lax.all_to_all(copies, axis_name, 0, 0, axis_index_groups=groups)  31.4 us
    all_to_all x2, waiting for transfers between devices, spread(): return lax.all_to_all(copies, axis_name, 0, 0, axis_index_groups=groups)  18.2 us
    all_to_all x1, starting transfers between devices, shards(): across = lax.all_to_all(blocks, 'row', 0, 0, axis_index_groups=along_z)  15.9 us
    all_gather x1, blocking collectives, shards(): lax.all_gather(lines, 'row', axis=0, tiled=True, axis_index_groups=along_x)  12.6 us
    all_to_all x1, waiting for transfers between devices, shards(): across = lax.all_to_all(blocks, 'row', 0, 0, axis_index_groups=along_z)  11.6 us
    ppermute x3, starting transfers between devices, shards(): passed = [lax.ppermute(line, 'col', col_pairs(d)) for d in (1, 2, 3)]  10.6 us
    ppermute x3, starting transfers between devices, shards(): lax.ppermute(parts[e], 'row', row_pairs(e, 0, 0))  10.5 us
    ppermute x1, starting transfers between devices, shards(): far = lax.ppermute(grad, 'col', halves)  9.09 us
  transfers between devices with their start and end apart: 12, of which 6 were waited for; matrix products, arithmetic and copies ran while one was open for 0% of the time, Pallas kernels for 3%

profile of v2, /device:TPU:42, one launch (start us, length us, event | category | flops | bytes accessed | tf_op | source)
XLA Modules:
  0.0 141.7 jit_solution(6289247339871440987)
XLA Ops:
  2.0 0.9 copy-done.1
  3.4 9.1 %collective-permute-start = (bf16[40,512]{1,0:T(8,128)(2,1)S(1)}, bf16[40,512]{1,0:T(8,128)(2,1)S(1)}, u32[]{:S(2)}, u32[]{:S(2)}) collective-permute-start(bf16[40,512]{1,0:T(8,128)(2,1)S(1)} %get-tuple-element.19), channel_id=1, source_target_pairs={{0,4},{1,5},{2,6},{3,7},{4,0},{5,1},{6,2},{7,3},{8,12},{9,13},{10,... | collective-permute-start | bytes 122888 | tf_op jit(solution)/shard_map/grad_z/ppermute | solution.py:132
  12.5 2.0 %collective-permute-done = bf16[40,512]{1,0:T(8,128)(2,1)S(1)} collective-permute-done((bf16[40,512]{1,0:T(8,128)(2,1)S(1)}, bf16[40,512]{1,0:T(8,128)(2,1)S(1)}, u32[]{:S(2)}, u32[]{:S(2)}) %collective-permute-start) | collective-permute-done | bytes 40992 | tf_op jit(solution)/shard_map/grad_z/ppermute | solution.py:132
  14.5 0.7 broadcast_in_dim.14
  15.3 6.3 %all-to-all-start = ((bf16[4,80,512]{2,1,0:T(8,128)(2,1)}), bf16[4,80,512]{2,1,0:T(8,128)(2,1)S(1)}, u32[]{:S(2)}, u32[]{:S(2)}) async-start(bf16[4,80,512]{2,1,0:T(8,128)(2,1)} %broadcast_in_dim.14), calls=%async_computation | async-start | bytes 655360 | tf_op jit(solution)/shard_map/grad_z/all_to_all | solution.py:118
  22.9 6.8 %all-to-all-done = bf16[4,80,512]{2,1,0:T(8,128)(2,1)S(1)} async-done(((bf16[4,80,512]{2,1,0:T(8,128)(2,1)}), bf16[4,80,512]{2,1,0:T(8,128)(2,1)S(1)}, u32[]{:S(2)}, u32[]{:S(2)}) %all-to-all-start) | async-done | bytes 327712 | tf_op jit(solution)/shard_map/grad_z/all_to_all | solution.py:118
  29.7 2.3 %collective-permute-start.3 = (bf16[320,512]{1,0:T(8,128)(2,1)S(1)}, bf16[320,512]{1,0:T(8,128)(2,1)S(1)}, u32[]{:S(2)}, u32[]{:S(2)}) collective-permute-start(bf16[320,512]{1,0:T(8,128)(2,1)S(1)} %bitcast.21), channel_id=1, source_target_pairs={{0,24},{1,25},{2,26},{3,27},{4,28},{5,29},{6,30},{7,31},{8,0},{9,1... | collective-permute-start | bytes 983048 | tf_op jit(solution)/shard_map/grad_y/ppermute | solution.py:138
  32.0 4.5 %collective-permute-start.2 = (bf16[320,512]{1,0:T(8,128)(2,1)S(1)}, bf16[320,512]{1,0:T(8,128)(2,1)S(1)}, u32[]{:S(2)}, u32[]{:S(2)}) collective-permute-start(bf16[320,512]{1,0:T(8,128)(2,1)S(1)} %bitcast.22), channel_id=1, source_target_pairs={{0,16},{1,17},{2,18},{3,19},{4,20},{5,21},{6,22},{7,23},{8,24},{9,... | collective-permute-start | bytes 983048 | tf_op jit(solution)/shard_map/grad_y/ppermute | solution.py:138
  36.5 3.8 %collective-permute-start.1 = (bf16[320,512]{1,0:T(8,128)(2,1)S(1)}, bf16[320,512]{1,0:T(8,128)(2,1)S(1)}, u32[]{:S(2)}, u32[]{:S(2)}) collective-permute-start(bf16[320,512]{1,0:T(8,128)(2,1)S(1)} %bitcast.23), channel_id=1, source_target_pairs={{0,8},{1,9},{2,10},{3,11},{4,12},{5,13},{6,14},{7,15},{8,16},{9,17... | collective-permute-start | bytes 983048 | tf_op jit(solution)/shard_map/grad_y/ppermute | solution.py:138
  41.0 25.1 %all-to-all-start.1 = ((bf16[4,40,512]{2,1,0:T(8,128)(2,1)}), bf16[4,40,512]{2,1,0:T(8,128)(2,1)S(1)}, u32[]{:S(2)}, u32[]{:S(2)}) async-start(bf16[4,40,512]{2,1,0:T(8,128)(2,1)} %broadcast_in_dim.15), calls=%async_computation.1 | async-start | bytes 327680 | tf_op jit(solution)/shard_map/in_z/all_to_all | solution.py:118
  66.1 1.4 shard_map.113
  67.5 1.9 %collective-permute-start.4 = (bf16[640,512]{1,0:T(8,128)(2,1)}, bf16[640,512]{1,0:T(8,128)(2,1)S(1)}, u32[]{:S(2)}, u32[]{:S(2)}) collective-permute-start(bf16[640,512]{1,0:T(8,128)(2,1)} %get-tuple-element.23), channel_id=1, source_target_pairs={{0,32},{32,0},{64,96},{96,64},{128,160},{160,128},{192,224},{224,1... | collective-permute-start | bytes 1966088 | tf_op jit(solution)/shard_map/sum_core/ppermute | solution.py:151
  69.4 2.3 %collective-permute-done.4.got = bf16[640,512]{1,0:T(8,128)(2,1)S(1)} collective-permute-done((bf16[640,512]{1,0:T(8,128)(2,1)}, bf16[640,512]{1,0:T(8,128)(2,1)S(1)}, u32[]{:S(2)}, u32[]{:S(2)}) %collective-permute-start.4) | collective-permute-done | bytes 655392 | tf_op jit(solution)/shard_map/sum_core/ppermute | solution.py:151
  72.2 3.4 %collective-permute-start.5 = (bf16[160,512]{1,0:T(8,128)(2,1)S(1)}, bf16[160,512]{1,0:T(8,128)(2,1)S(1)}, u32[]{:S(2)}, u32[]{:S(2)}) collective-permute-start(bf16[160,512]{1,0:T(8,128)(2,1)S(1)} %get-tuple-element.25), channel_id=1, source_target_pairs={{0,256},{32,288},{64,320},{96,352},{128,384},{160,416},{192,448},{... | collective-permute-start | bytes 491528 | tf_op jit(solution)/shard_map/sum_x/ppermute | solution.py:160
  75.6 3.0 %collective-permute-start.6 = (bf16[160,512]{1,0:T(8,128)(2,1)S(1)}, bf16[160,512]{1,0:T(8,128)(2,1)S(1)}, u32[]{:S(2)}, u32[]{:S(2)}) collective-permute-start(bf16[160,512]{1,0:T(8,128)(2,1)S(1)} %get-tuple-element.26), channel_id=1, source_target_pairs={{0,512},{32,544},{64,576},{96,608},{128,640},{160,672},{192,704},{... | collective-permute-start | bytes 491528 | tf_op jit(solution)/shard_map/sum_x/ppermute | solution.py:160
  78.7 4.1 %collective-permute-start.7 = (bf16[160,512]{1,0:T(8,128)(2,1)S(1)}, bf16[160,512]{1,0:T(8,128)(2,1)S(1)}, u32[]{:S(2)}, u32[]{:S(2)}) collective-permute-start(bf16[160,512]{1,0:T(8,128)(2,1)S(1)} %get-tuple-element.27), channel_id=1, source_target_pairs={{0,768},{32,800},{64,832},{96,864},{128,896},{160,928},{192,960},{... | collective-permute-start | bytes 491528 | tf_op jit(solution)/shard_map/sum_x/ppermute | solution.py:160
  82.7 11.4 %all-to-all-done.1 = bf16[4,40,512]{2,1,0:T(8,128)(2,1)S(1)} async-done(((bf16[4,40,512]{2,1,0:T(8,128)(2,1)}), bf16[4,40,512]{2,1,0:T(8,128)(2,1)S(1)}, u32[]{:S(2)}, u32[]{:S(2)}) %all-to-all-start.1) | async-done | bytes 163872 | tf_op jit(solution)/shard_map/in_z/all_to_all | solution.py:118
  94.2 0.7 sum_x.3
  94.9 15.9 %all-to-all-start.2 = ((bf16[4,40,512]{2,1,0:T(8,128)(2,1)}), bf16[4,40,512]{2,1,0:T(8,128)(2,1)S(1)}, u32[]{:S(2)}, u32[]{:S(2)}) async-start(bf16[4,40,512]{2,1,0:T(8,128)(2,1)} %sum_x.3), calls=%async_computation.2 | async-start | bytes 327680 | tf_op jit(solution)/shard_map/sum_z/all_to_all | solution.py:164
  110.9 12.6 %all_gather.3.own_in = bf16[640,512]{1,0:T(8,128)(2,1)S(1)} all-gather(bf16[160,512]{1,0:T(8,128)(2,1)S(1)} %bitcast.30), channel_id=1, replica_groups={{0,256,512,768},{32,288,544,800},{64,320,576,832},{96,352,608,864},{128..., dimensions={0}, use_global_device_ids=true | all-gather | bytes 819200 | tf_op jit(solution)/shard_map/in_x/all_gather | solution.py:168
  123.5 1.9 %collective-permute-start.8 = (bf16[640,512]{1,0:T(8,128)(2,1)S(1)}, bf16[640,512]{1,0:T(8,128)(2,1)S(1)}, u32[]{:S(2)}, u32[]{:S(2)}) collective-permute-start(bf16[640,512]{1,0:T(8,128)(2,1)S(1)} %all_gather.3.own_in), channel_id=1, source_target_pairs={{0,32},{32,0},{64,96},{96,64},{128,160},{160,128},{192,224},{224,1... | collective-permute-start | bytes 1966088 | tf_op jit(solution)/shard_map/in_core/ppermute | solution.py:170
  125.4 2.1 %collective-permute-done.8.other_in = bf16[640,512]{1,0:T(8,128)(2,1)S(1)} collective-permute-done((bf16[640,512]{1,0:T(8,128)(2,1)S(1)}, bf16[640,512]{1,0:T(8,128)(2,1)S(1)}, u32[]{:S(2)}, u32[]{:S(2)}) %collective-permute-start.8) | collective-permute-done | bytes 655392 | tf_op jit(solution)/shard_map/in_core/ppermute | solution.py:170
  127.5 2.0 %outer.1 = f32[512,512]{1,0:T(8,128)} custom-call(bf16[640,512]{1,0:T(8,128)(2,1)S(1)} %bitcast.20, bf16[640,512]{1,0:T(8,128)(2,1)S(1)} %all_gather.3.own_in, bf16[640,512]{1,0:T(8,128)(2,1)S(1)} %bitcast.25, bf16[640,512]{1,0:T(8,128)(2,1)S(1)} %collective-permute-done.8.other_in), custom_call_target="tpu_custom_call" | custom-call | flops 1024 | bytes 1024 | tf_op jit(solution)/shard_map/outer/pallas_call | solution.py:70
  129.4 11.6 %all-to-all-done.2 = bf16[4,40,512]{2,1,0:T(8,128)(2,1)S(1)} async-done(((bf16[4,40,512]{2,1,0:T(8,128)(2,1)}), bf16[4,40,512]{2,1,0:T(8,128)(2,1)S(1)}, u32[]{:S(2)}, u32[]{:S(2)}) %all-to-all-start.2) | async-done | bytes 163872 | tf_op jit(solution)/shard_map/sum_z/all_to_all | solution.py:164
  (23 shorter events, 3.1 us)
Async XLA Ops:
  1.3 0.7 copy-start.3
  2.0 0.9 copy-start.1
  3.4 11.1 %collective-permute-start = (bf16[40,512]{1,0:T(8,128)(2,1)S(1)}, bf16[40,512]{1,0:T(8,128)(2,1)S(1)}, u32[]{:S(2)}, u32[]{:S(2)}) collective-permute-start(bf16[40,512]{1,0:T(8,128)(2,1)S(1)} %get-tuple-element.19), channel_id=1, source_target_pairs={{0,4},{1,5},{2,6},{3,7},{4,0},{5,1},{6,2},{7,3},{8,12},{9,13},{10,... | collective-permute-start | bytes 122888 | tf_op jit(solution)/shard_map/grad_z/ppermute | solution.py:132
  15.3 7.0 %copy-start.2 = (f32[40,512]{1,0:T(8,128)S(1)}, f32[40,512]{1,0:T(8,128)}, u32[]{:S(2)}) copy-start(f32[40,512]{1,0:T(8,128)} %values_ref.3) | copy-start | bytes 245764
  15.3 50.8 %copy-start = (bf16[512,512]{1,0:T(8,128)(2,1)S(1)}, bf16[512,512]{1,0:T(8,128)(2,1)}, u32[]{:S(2)}) copy-start(bf16[512,512]{1,0:T(8,128)(2,1)} %weight.3) | copy-start | bytes 1572868
  15.3 14.4 %all-to-all-start = ((bf16[4,80,512]{2,1,0:T(8,128)(2,1)}), bf16[4,80,512]{2,1,0:T(8,128)(2,1)S(1)}, u32[]{:S(2)}, u32[]{:S(2)}) async-start(bf16[4,80,512]{2,1,0:T(8,128)(2,1)} %broadcast_in_dim.14), calls=%async_computation | async-start | bytes 655360 | tf_op jit(solution)/shard_map/grad_z/all_to_all | solution.py:118
  21.6 0.7 copy-start.4
  29.7 36.4 %collective-permute-start.3 = (bf16[320,512]{1,0:T(8,128)(2,1)S(1)}, bf16[320,512]{1,0:T(8,128)(2,1)S(1)}, u32[]{:S(2)}, u32[]{:S(2)}) collective-permute-start(bf16[320,512]{1,0:T(8,128)(2,1)S(1)} %bitcast.21), channel_id=1, source_target_pairs={{0,24},{1,25},{2,26},{3,27},{4,28},{5,29},{6,30},{7,31},{8,0},{9,1... | collective-permute-start | bytes 983048 | tf_op jit(solution)/shard_map/grad_y/ppermute | solution.py:138
  32.0 34.1 %collective-permute-start.2 = (bf16[320,512]{1,0:T(8,128)(2,1)S(1)}, bf16[320,512]{1,0:T(8,128)(2,1)S(1)}, u32[]{:S(2)}, u32[]{:S(2)}) collective-permute-start(bf16[320,512]{1,0:T(8,128)(2,1)S(1)} %bitcast.22), channel_id=1, source_target_pairs={{0,16},{1,17},{2,18},{3,19},{4,20},{5,21},{6,22},{7,23},{8,24},{9,... | collective-permute-start | bytes 983048 | tf_op jit(solution)/shard_map/grad_y/ppermute | solution.py:138
  36.5 29.6 %collective-permute-start.1 = (bf16[320,512]{1,0:T(8,128)(2,1)S(1)}, bf16[320,512]{1,0:T(8,128)(2,1)S(1)}, u32[]{:S(2)}, u32[]{:S(2)}) collective-permute-start(bf16[320,512]{1,0:T(8,128)(2,1)S(1)} %bitcast.23), channel_id=1, source_target_pairs={{0,8},{1,9},{2,10},{3,11},{4,12},{5,13},{6,14},{7,15},{8,16},{9,17... | collective-permute-start | bytes 983048 | tf_op jit(solution)/shard_map/grad_y/ppermute | solution.py:138
  41.0 53.1 %all-to-all-start.1 = ((bf16[4,40,512]{2,1,0:T(8,128)(2,1)}), bf16[4,40,512]{2,1,0:T(8,128)(2,1)S(1)}, u32[]{:S(2)}, u32[]{:S(2)}) async-start(bf16[4,40,512]{2,1,0:T(8,128)(2,1)} %broadcast_in_dim.15), calls=%async_computation.1 | async-start | bytes 327680 | tf_op jit(solution)/shard_map/in_z/all_to_all | solution.py:118
  67.5 4.2 %collective-permute-start.4 = (bf16[640,512]{1,0:T(8,128)(2,1)}, bf16[640,512]{1,0:T(8,128)(2,1)S(1)}, u32[]{:S(2)}, u32[]{:S(2)}) collective-permute-start(bf16[640,512]{1,0:T(8,128)(2,1)} %get-tuple-element.23), channel_id=1, source_target_pairs={{0,32},{32,0},{64,96},{96,64},{128,160},{160,128},{192,224},{224,1... | collective-permute-start | bytes 1966088 | tf_op jit(solution)/shard_map/sum_core/ppermute | solution.py:151
  72.2 21.9 %collective-permute-start.5 = (bf16[160,512]{1,0:T(8,128)(2,1)S(1)}, bf16[160,512]{1,0:T(8,128)(2,1)S(1)}, u32[]{:S(2)}, u32[]{:S(2)}) collective-permute-start(bf16[160,512]{1,0:T(8,128)(2,1)S(1)} %get-tuple-element.25), channel_id=1, source_target_pairs={{0,256},{32,288},{64,320},{96,352},{128,384},{160,416},{192,448},{... | collective-permute-start | bytes 491528 | tf_op jit(solution)/shard_map/sum_x/ppermute | solution.py:160
  75.6 18.5 %collective-permute-start.6 = (bf16[160,512]{1,0:T(8,128)(2,1)S(1)}, bf16[160,512]{1,0:T(8,128)(2,1)S(1)}, u32[]{:S(2)}, u32[]{:S(2)}) collective-permute-start(bf16[160,512]{1,0:T(8,128)(2,1)S(1)} %get-tuple-element.26), channel_id=1, source_target_pairs={{0,512},{32,544},{64,576},{96,608},{128,640},{160,672},{192,704},{... | collective-permute-start | bytes 491528 | tf_op jit(solution)/shard_map/sum_x/ppermute | solution.py:160
  78.7 15.5 %collective-permute-start.7 = (bf16[160,512]{1,0:T(8,128)(2,1)S(1)}, bf16[160,512]{1,0:T(8,128)(2,1)S(1)}, u32[]{:S(2)}, u32[]{:S(2)}) collective-permute-start(bf16[160,512]{1,0:T(8,128)(2,1)S(1)} %get-tuple-element.27), channel_id=1, source_target_pairs={{0,768},{32,800},{64,832},{96,864},{128,896},{160,928},{192,960},{... | collective-permute-start | bytes 491528 | tf_op jit(solution)/shard_map/sum_x/ppermute | solution.py:160
  94.9 46.1 %all-to-all-start.2 = ((bf16[4,40,512]{2,1,0:T(8,128)(2,1)}), bf16[4,40,512]{2,1,0:T(8,128)(2,1)S(1)}, u32[]{:S(2)}, u32[]{:S(2)}) async-start(bf16[4,40,512]{2,1,0:T(8,128)(2,1)} %sum_x.3), calls=%async_computation.2 | async-start | bytes 327680 | tf_op jit(solution)/shard_map/sum_z/all_to_all | solution.py:164
  123.5 4.0 %collective-permute-start.8 = (bf16[640,512]{1,0:T(8,128)(2,1)S(1)}, bf16[640,512]{1,0:T(8,128)(2,1)S(1)}, u32[]{:S(2)}, u32[]{:S(2)}) collective-permute-start(bf16[640,512]{1,0:T(8,128)(2,1)S(1)} %all_gather.3.own_in), channel_id=1, source_target_pairs={{0,32},{32,0},{64,96},{96,64},{128,160},{160,128},{192,224},{224,1... | collective-permute-start | bytes 1966088 | tf_op jit(solution)/shard_map/in_core/ppermute | solution.py:170

commit v3 on v2

--- a/solution.py
+++ b/solution.py
@@ -18,18 +18,18 @@
     return (y % 4) * 8 + l
 
 
-def row_pairs(dx, dh, dc):
+def row_pairs(dc):
+    return [(row_of(x, h, c), row_of(x, h, c + dc)) for x in range(4) for h in range(4) for c in range(2)]
+
+
+def ring(step):
     return [
-        (row_of(x, h, c), row_of(x + dx, h + dh, c + dc)) for x in range(4) for h in range(4) for c in range(2)
+        (row_of(x, h, c), row_of(x, h + (step, -step)[c], c)) for x in range(4) for h in range(4) for c in range(2)
     ]
 
 
-def col_pairs(dy):
-    return [(col_of(y, l), col_of(y + dy, l)) for y in range(4) for l in range(8)]
-
-
 along_x = [[row_of(x, h, c) for x in range(4)] for h in range(4) for c in range(2)]
-along_z = [[row_of(x, h, c) for h in range(4)] for x in range(4) for c in range(2)]
+along_y = [[col_of(y, l) for y in range(4)] for l in range(8)]
 quads = [[col_of(y, 4 * s + k) for k in range(4)] for y in range(4) for s in range(2)]
 halves = [(col_of(y, l), col_of(y, l ^ 4)) for y in range(4) for l in range(8)]
 
@@ -78,31 +78,38 @@
     )(*smem, *vmem)
 
 
-def other_kernel(y, core, d0, d1, d2, d3, weight, own, other, sent):
-    for d, ref in enumerate((d0, d1, d2, d3)):
-        at = jnp.bitwise_and(y[0] - d, 3)
-        for k in range(2):
-            own[at, k] = ref[k, core[0]]
-            other[at, k] = ref[k, 1 - core[0]]
-    rows = other[...].reshape(640, 512)
-    sent[...] = jnp.dot(rows, weight[...], preferred_element_type=f32).astype(bf16)
-
-
-def own_kernel(x, own, weight, got, e0, e1, e2, e3, held):
+def sort_kernel(h, core, blocks, own, other):
+    for c, ref in ((core[0], own), (1 - core[0], other)):
+        turn = 1 - 2 * c
+        for p, (up, side) in enumerate(((turn, c), (turn, 1 - c), (2, c), (0, c))):
+            to = jnp.bitwise_and(h[0] + up, 3)
+            k = 2 * jnp.bitwise_and(to, 1) + side
+            for y in range(4):
+                ref[y, p] = blocks[y, k, to >> 1]
+
+
+def other_kernel(other, weight, sent):
+    sent[...] = jnp.dot(other[...], weight[...], preferred_element_type=f32).astype(bf16)
+
+
+def own_kernel(own, weight, got, part):
     total = jnp.dot(own[...], weight[...], preferred_element_type=f32) + got[...].astype(f32)
-    held[...] = total.astype(bf16).reshape(4, 160, 512)
-    for e, ref in enumerate((e0, e1, e2, e3)):
-        ref[...] = held[jnp.bitwise_and(x[0] + e, 3)]
-
-
-def line_kernel(e0, e1, e2, e3, blocks):
-    total = e0[...].astype(f32)
-    for ref in (e1, e2, e3):
-        total += ref[...].astype(f32)
-    for k in range(2):
-        for s in range(2):
-            at = 40 * (2 * k + s)
-            blocks[2 * s + k] = total[at : at + 40].astype(bf16)
+    part[...] = total.astype(bf16)
+
+
+def line_kernel(across, far, near, mine):
+    total = across[0].astype(f32)
+    for x in range(1, 4):
+        total += across[x].astype(f32)
+    near[0] = total[:40]
+    near[1] = total[40:80]
+    far[...] = total[80:120].astype(bf16)
+    mine[...] = total[120:]
+
+
+def near_kernel(near, got, sent):
+    sent[0] = (near[0] + got[...].astype(f32)).astype(bf16)
+    sent[1] = near[1].astype(bf16)
 
 
 def outer_kernel(own, own_in, other, other_in, grad):
@@ -121,8 +128,8 @@
 def shards(saved_input, out_grad, weight, history_in, history_grad, slot_in, slot_grad, step_count):
     row = lax.axis_index("row")
     col = lax.axis_index("col")
-    h = jnp.bitwise_and(row >> 1, 3)
-    core = jnp.bitwise_and(row, 1)
+    h = jnp.bitwise_and(row >> 1, 3).reshape(1)
+    core = jnp.bitwise_and(row, 1).reshape(1)
     first = jnp.bitwise_and(col, 4) == 0
 
     grad, new_history_grad = restore(out_grad, history_grad, slot_grad, step_count)
@@ -132,44 +139,48 @@
         far = lax.ppermute(grad, "col", halves)
         pair = jnp.stack([jnp.where(first, grad, far), jnp.where(first, far, grad)])
         line = spread(pair.reshape(80, 512), "col", quads)
-    line, kept = lax.optimization_barrier((line, kept))
+    with jax.named_scope("in_pair"):
+        both = jnp.concatenate([kept, lax.ppermute(kept, "row", row_pairs(1))])
+    line, both = lax.optimization_barrier((line, both))
     with jax.named_scope("grad_y"):
-        line = line.reshape(320, 512)
-        passed = [lax.ppermute(line, "col", col_pairs(d)) for d in (1, 2, 3)]
+        grads = spread(line.reshape(320, 512), "col", along_y)
     with jax.named_scope("in_z"):
-        lines = spread(kept, "row", along_z)
-        lines = lines.reshape(2, 2, 40, 512).swapaxes(0, 1).reshape(160, 512)
-    half = ((4, 2, 80, 512), bf16)
-    whole = ((640, 512), bf16)
-    taken = [b.reshape(2, 2, 80, 512) for b in (line, *passed)]
-    own, other, sent = call(
-        other_kernel, [half, half, whole], [(col >> 3).reshape(1), core.reshape(1)], [*taken, weight]
-    )
+        near_in = lax.ppermute(both, "row", ring(-1))
+
+    shared = ((4, 4, 40, 512), bf16)
+    own, other = call(sort_kernel, [shared, shared], [h, core], [grads.reshape(4, 4, 2, 40, 512)])
     own, other = own.reshape(640, 512), other.reshape(640, 512)
 
     with jax.named_scope("sum_core"):
-        got = lax.ppermute(sent, "row", row_pairs(0, 0, 1))
+        (sent,) = call(other_kernel, [((640, 512), bf16)], [], [other, weight])
+        sent, near_in = lax.optimization_barrier((sent, near_in))
+        got = lax.ppermute(sent, "row", row_pairs(1))
+        (part,) = call(own_kernel, [((640, 512), bf16)], [], [own, weight, got])
+    part, near_in = lax.optimization_barrier((part, near_in))
+    with jax.named_scope("in_z"):
+        far_in = lax.ppermute(near_in[:40], "row", ring(-1))
     with jax.named_scope("sum_x"):
-        parts = call(
-            own_kernel,
-            [((160, 512), bf16)] * 4,
-            [(row >> 3).reshape(1)],
-            [own, weight, got],
-            [pltpu.VMEM((4, 160, 512), bf16)],
+        across = lax.all_to_all(part.reshape(4, 160, 512), "row", 0, 0, axis_index_groups=along_x)
+        block = (40, 512)
+        far, near, mine = call(
+            line_kernel, [(block, bf16), ((2, *block), f32), (block, f32)], [], [across]
         )
-        across = [lax.ppermute(parts[e], "row", row_pairs(e, 0, 0)) for e in (1, 2, 3)]
-        (blocks,) = call(line_kernel, [((4, 40, 512), bf16)], [], [parts[0], *across])
-    blocks, lines = lax.optimization_barrier((blocks, lines))
+    far, kept = lax.optimization_barrier((far, kept))
+    with jax.named_scope("in_x"):
+        lines = jnp.concatenate([near_in, far_in, kept])
+        own_in = spread(lines, "row", along_x).reshape(640, 512)
     with jax.named_scope("sum_z"):
-        across = lax.all_to_all(blocks, "row", 0, 0, axis_index_groups=along_z)
-        input_grad = jnp.sum(across.astype(f32), axis=0).astype(bf16)
-
-    with jax.named_scope("in_x"):
-        own_in = lax.all_gather(lines, "row", axis=0, tiled=True, axis_index_groups=along_x)
+        (sent,) = call(near_kernel, [((2, *block), bf16)], [], [near, lax.ppermute(far, "row", ring(1))])
+        sent, own_in = lax.optimization_barrier((sent, own_in))
+        near = lax.ppermute(sent, "row", ring(1))
     with jax.named_scope("in_core"):
-        other_in = lax.ppermute(own_in, "row", row_pairs(0, 0, 1))
+        other_in = lax.ppermute(own_in, "row", row_pairs(1))
     with jax.named_scope("outer"):
         (weight_grad,) = call(outer_kernel, [((512, 512), f32)], [], [own, own_in, other, other_in])
+    with jax.named_scope("sum_z"):
+        near, weight_grad = lax.optimization_barrier((near, weight_grad))
+        got = lax.ppermute(near[1], "row", row_pairs(1))
+        input_grad = (mine + near[0].astype(f32) + got.astype(f32)).astype(bf16)
     return (weight_grad, input_grad, new_history_in, new_history_grad)
 
 

time: 142 us -> 137 us (0.965)
  the two profiles are of different devices: /device:TPU:42 before, /device:TPU:1 now
where the time goes in v3:
time: 137 us; the launch traced here: 135 us
  starting transfers between devices  101 us (74%)
  waiting for transfers between devices  21 us (15%)
  Pallas kernels  5.21 us (4%)
  local copies, waits for them, and re-layouts  4.37 us (3%)
  between operations  2.8 us (2%)
    all_to_all x3, starting transfers between devices, spread(): return lax.all_to_all(copies, axis_name, 0, 0, axis_index_groups=groups)  13.4 us
    ppermute x1, starting transfers between devices, shards(): lax.ppermute(far, 'row', ring(1))  12.9 us
    ppermute x1, starting transfers between devices, shards(): both = jnp.concatenate([kept, lax.ppermute(kept, 'row', row_pairs(1))])  12.8 us
    ppermute x1, starting transfers between devices, shards(): near = lax.ppermute(sent, 'row', ring(1))  12.4 us
    ppermute x1, starting transfers between devices, shards(): got = lax.ppermute(sent, 'row', row_pairs(1))  11.6 us
    ppermute x1, starting transfers between devices, shards(): near_in = lax.ppermute(both, 'row', ring(-1))  11 us
    ppermute x1, starting transfers between devices, shards(): far = lax.ppermute(grad, 'col', halves)  9.63 us
    ppermute x1, starting transfers between devices, shards(): far_in = lax.ppermute(near_in[:40], 'row', ring(-1))  6 us
  transfers between devices with their start and end apart: 13, of which 9 were waited for; matrix products, arithmetic and copies ran while one was open for 0% of the time, Pallas kernels for 2%

profile of v3, /device:TPU:1, one launch (start us, length us, event | category | flops | bytes accessed | tf_op | source)
XLA Modules:
  0.0 135.4 jit_solution(7346314178818630362)
XLA Ops:
  4.1 9.6 %collective-permute-start = (bf16[40,512]{1,0:T(8,128)(2,1)S(1)}, bf16[40,512]{1,0:T(8,128)(2,1)S(1)}, u32[]{:S(2)}, u32[]{:S(2)}) collective-permute-start(bf16[40,512]{1,0:T(8,128)(2,1)S(1)} %get-tuple-element.25), channel_id=1, source_target_pairs={{0,4},{1,5},{2,6},{3,7},{4,0},{5,1},{6,2},{7,3},{8,12},{9,13},{10,... | collective-permute-start | bytes 122888 | tf_op jit(solution)/shard_map/grad_z/ppermute | solution.py:139
  13.7 1.4 %collective-permute-done = bf16[40,512]{1,0:T(8,128)(2,1)S(1)} collective-permute-done((bf16[40,512]{1,0:T(8,128)(2,1)S(1)}, bf16[40,512]{1,0:T(8,128)(2,1)S(1)}, u32[]{:S(2)}, u32[]{:S(2)}) %collective-permute-start) | collective-permute-done | bytes 40992 | tf_op jit(solution)/shard_map/grad_z/ppermute | solution.py:139
  15.9 5.6 %all-to-all-start = ((bf16[4,80,512]{2,1,0:T(8,128)(2,1)}), bf16[4,80,512]{2,1,0:T(8,128)(2,1)S(1)}, u32[]{:S(2)}, u32[]{:S(2)}) async-start(bf16[4,80,512]{2,1,0:T(8,128)(2,1)} %broadcast_in_dim.21), calls=%async_computation | async-start | bytes 655360 | tf_op jit(solution)/shard_map/grad_z/all_to_all | solution.py:125
  22.8 12.8 %collective-permute-start.1 = (bf16[40,512]{1,0:T(8,128)(2,1)S(1)}, bf16[40,512]{1,0:T(8,128)(2,1)S(1)}, u32[]{:S(2)}, u32[]{:S(2)}) collective-permute-start(bf16[40,512]{1,0:T(8,128)(2,1)S(1)} %get-tuple-element.38), channel_id=1, source_target_pairs={{0,32},{32,0},{64,96},{96,64},{128,160},{160,128},{192,224},{224,1... | collective-permute-start | bytes 122888 | tf_op jit(solution)/shard_map/in_pair/ppermute | solution.py:143
  36.4 1.2 broadcast_in_dim.23
  37.6 3.5 %all-to-all-start.1 = ((bf16[4,320,512]{2,1,0:T(8,128)(2,1)}), bf16[4,320,512]{2,1,0:T(8,128)(2,1)S(1)}, u32[]{:S(2)}, u32[]{:S(2)}) async-start(bf16[4,320,512]{2,1,0:T(8,128)(2,1)} %broadcast_in_dim.23), calls=%async_computation.1 | async-start | bytes 2621440 | tf_op jit(solution)/shard_map/grad_y/all_to_all | solution.py:125
  41.2 11.0 %collective-permute-start.2 = (bf16[80,512]{1,0:T(8,128)(2,1)S(1)}, bf16[80,512]{1,0:T(8,128)(2,1)S(1)}, u32[]{:S(2)}, u32[]{:S(2)}) collective-permute-start(bf16[80,512]{1,0:T(8,128)(2,1)S(1)} %pad_maximum_fusion.2), channel_id=1, source_target_pairs={{0,192},{32,96},{64,0},{96,160},{128,64},{160,224},{192,128},{224,... | collective-permute-start | bytes 245768 | tf_op jit(solution)/shard_map/in_z/ppermute | solution.py:148
  52.2 3.4 %all-to-all-done.1 = bf16[4,320,512]{2,1,0:T(8,128)(2,1)S(1)} async-done(((bf16[4,320,512]{2,1,0:T(8,128)(2,1)}), bf16[4,320,512]{2,1,0:T(8,128)(2,1)S(1)}, u32[]{:S(2)}, u32[]{:S(2)}) %all-to-all-start.1) | async-done | bytes 1310752 | tf_op jit(solution)/shard_map/grad_y/all_to_all | solution.py:125
  56.2 11.6 %collective-permute-start.3 = (bf16[640,512]{1,0:T(8,128)(2,1)S(1)}, bf16[640,512]{1,0:T(8,128)(2,1)S(1)}, u32[]{:S(2)}, u32[]{:S(2)}) collective-permute-start(bf16[640,512]{1,0:T(8,128)(2,1)S(1)} %sum_core.2), channel_id=1, source_target_pairs={{0,32},{32,0},{64,96},{96,64},{128,160},{160,128},{192,224},{224,1... | collective-permute-start | bytes 1966088 | tf_op jit(solution)/shard_map/sum_core/ppermute | solution.py:157
  67.8 1.7 %collective-permute-done.3.got = bf16[640,512]{1,0:T(8,128)(2,1)S(1)} collective-permute-done((bf16[640,512]{1,0:T(8,128)(2,1)S(1)}, bf16[640,512]{1,0:T(8,128)(2,1)S(1)}, u32[]{:S(2)}, u32[]{:S(2)}) %collective-permute-start.3) | collective-permute-done | bytes 655392 | tf_op jit(solution)/shard_map/sum_core/ppermute | solution.py:157
  69.5 1.3 sum_core.3
  70.8 3.9 %all-to-all-start.2 = ((bf16[4,160,512]{2,1,0:T(8,128)(2,1)}), bf16[4,160,512]{2,1,0:T(8,128)(2,1)S(1)}, u32[]{:S(2)}, u32[]{:S(2)}) async-start(bf16[4,160,512]{2,1,0:T(8,128)(2,1)} %bitcast.9), calls=%async_computation.2 | async-start | bytes 1310720 | tf_op jit(solution)/shard_map/sum_x/all_to_all | solution.py:163
  74.8 6.0 %collective-permute-start.5 = (bf16[40,512]{1,0:T(8,128)(2,1)S(1)}, bf16[40,512]{1,0:T(8,128)(2,1)S(1)}, u32[]{:S(2)}, u32[]{:S(2)}) collective-permute-start(bf16[40,512]{1,0:T(8,128)(2,1)S(1)} %slice.9), channel_id=1, source_target_pairs={{0,192},{32,96},{64,0},{96,160},{128,64},{160,224},{192,128},{224,... | collective-permute-start | bytes 122888 | tf_op jit(solution)/shard_map/in_z/ppermute | solution.py:161
  80.8 4.3 %all-to-all-done.2.across = bf16[4,160,512]{2,1,0:T(8,128)(2,1)S(1)} async-done(((bf16[4,160,512]{2,1,0:T(8,128)(2,1)}), bf16[4,160,512]{2,1,0:T(8,128)(2,1)S(1)}, u32[]{:S(2)}, u32[]{:S(2)}) %all-to-all-start.2) | async-done | bytes 655392 | tf_op jit(solution)/shard_map/sum_x/all_to_all | solution.py:163
  85.1 3.8 %collective-permute-done.5 = bf16[40,512]{1,0:T(8,128)(2,1)S(1)} collective-permute-done((bf16[40,512]{1,0:T(8,128)(2,1)S(1)}, bf16[40,512]{1,0:T(8,128)(2,1)S(1)}, u32[]{:S(2)}, u32[]{:S(2)}) %collective-permute-start.5) | collective-permute-done | bytes 40992 | tf_op jit(solution)/shard_map/in_z/ppermute | solution.py:161
  89.8 4.2 %all-to-all-start.3 = ((bf16[4,160,512]{2,1,0:T(8,128)(2,1)}), bf16[4,160,512]{2,1,0:T(8,128)(2,1)S(1)}, u32[]{:S(2)}, u32[]{:S(2)}) async-start(bf16[4,160,512]{2,1,0:T(8,128)(2,1)} %broadcast_in_dim.24), calls=%async_computation.3 | async-start | bytes 1310720 | tf_op jit(solution)/shard_map/in_x/all_to_all | solution.py:125
  94.1 12.9 %collective-permute-start.4 = (bf16[40,512]{1,0:T(8,128)(2,1)S(1)}, bf16[40,512]{1,0:T(8,128)(2,1)S(1)}, u32[]{:S(2)}, u32[]{:S(2)}) collective-permute-start(bf16[40,512]{1,0:T(8,128)(2,1)S(1)} %get-tuple-element.36), channel_id=1, source_target_pairs={{0,64},{32,224},{64,128},{96,32},{128,192},{160,96},{192,0},{224,1... | collective-permute-start | bytes 122888 | tf_op jit(solution)/shard_map/sum_z/ppermute | solution.py:173
  107.0 1.8 %collective-permute-done.4.got = bf16[40,512]{1,0:T(8,128)(2,1)S(1)} collective-permute-done((bf16[40,512]{1,0:T(8,128)(2,1)S(1)}, bf16[40,512]{1,0:T(8,128)(2,1)S(1)}, u32[]{:S(2)}, u32[]{:S(2)}) %collective-permute-start.4) | collective-permute-done | bytes 40992 | tf_op jit(solution)/shard_map/sum_z/ppermute | solution.py:173
  108.8 5.8 %collective-permute-start.7 = (bf16[640,512]{1,0:T(8,128)(2,1)S(1)}, bf16[640,512]{1,0:T(8,128)(2,1)S(1)}, u32[]{:S(2)}, u32[]{:S(2)}) collective-permute-start(bf16[640,512]{1,0:T(8,128)(2,1)S(1)} %bitcast.21), channel_id=1, source_target_pairs={{0,32},{32,0},{64,96},{96,64},{128,160},{160,128},{192,224},{224,1... | collective-permute-start | bytes 1966088 | tf_op jit(solution)/shard_map/in_core/ppermute | solution.py:177
  114.6 12.4 %collective-permute-start.6 = (bf16[2,40,512]{2,1,0:T(8,128)(2,1)S(1)}, bf16[2,40,512]{2,1,0:T(8,128)(2,1)S(1)}, u32[]{:S(2)}, u32[]{:S(2)}) collective-permute-start(bf16[2,40,512]{2,1,0:T(8,128)(2,1)S(1)} %sum_z.1), channel_id=1, source_target_pairs={{0,64},{32,224},{64,128},{96,32},{128,192},{160,96},{192,0},{224,1... | collective-permute-start | bytes 245768 | tf_op jit(solution)/shard_map/sum_z/ppermute | solution.py:175
  127.0 2.0 %outer.1 = f32[512,512]{1,0:T(8,128)} custom-call(bf16[640,512]{1,0:T(8,128)(2,1)S(1)} %bitcast.24, bf16[640,512]{1,0:T(8,128)(2,1)S(1)} %bitcast.22, bf16[640,512]{1,0:T(8,128)(2,1)S(1)} %bitcast.20, bf16[640,512]{1,0:T(8,128)(2,1)S(1)} %collective-permute-done.7.other_in), custom_call_target="tpu_custom_call" | custom-call | flops 1024 | bytes 1024 | tf_op jit(solution)/shard_map/outer/pallas_call | solution.py:70
  129.0 2.7 %collective-permute-done.6 = bf16[2,40,512]{2,1,0:T(8,128)(2,1)S(1)} collective-permute-done((bf16[2,40,512]{2,1,0:T(8,128)(2,1)S(1)}, bf16[2,40,512]{2,1,0:T(8,128)(2,1)S(1)}, u32[]{:S(2)}, u32[]{:S(2)}) %collective-permute-start.6) | collective-permute-done | bytes 81952 | tf_op jit(solution)/shard_map/sum_z/ppermute | solution.py:175
  131.6 1.9 %collective-permute-start.8 = (bf16[40,512]{1,0:T(8,128)(2,1)S(1)}, bf16[40,512]{1,0:T(8,128)(2,1)S(1)}, u32[]{:S(2)}, u32[]{:S(2)}) collective-permute-start(bf16[40,512]{1,0:T(8,128)(2,1)S(1)} %slice_bitcast_fusion), channel_id=1, source_target_pairs={{0,32},{32,0},{64,96},{96,64},{128,160},{160,128},{192,224},{224,1... | collective-permute-start | bytes 122888 | tf_op jit(solution)/shard_map/sum_z/ppermute | solution.py:182
  133.6 1.2 collective-permute-done.8
  (30 shorter events, 6.6 us)
Async XLA Ops:
  0.6 21.5 %copy-start.4 = (f32[1,1,16]{2,1,0:T(1,128)S(1)}, f32[1,1,16]{2,1,0:T(1,128)}, u32[]{:S(2)}) copy-start(f32[1,1,16]{2,1,0:T(1,128)} %history_ref.3) | copy-start | bytes 196
  1.9 0.9 copy-start.1
  2.8 0.7 copy-start.3
  3.5 18.7 %copy-start.2 = (f32[40,512]{1,0:T(8,128)S(1)}, f32[40,512]{1,0:T(8,128)}, u32[]{:S(2)}) copy-start(f32[40,512]{1,0:T(8,128)} %values_ref.3) | copy-start | bytes 245764
  4.1 11.0 %collective-permute-start = (bf16[40,512]{1,0:T(8,128)(2,1)S(1)}, bf16[40,512]{1,0:T(8,128)(2,1)S(1)}, u32[]{:S(2)}, u32[]{:S(2)}) collective-permute-start(bf16[40,512]{1,0:T(8,128)(2,1)S(1)} %get-tuple-element.25), channel_id=1, source_target_pairs={{0,4},{1,5},{2,6},{3,7},{4,0},{5,1},{6,2},{7,3},{8,12},{9,13},{10,... | collective-permute-start | bytes 122888 | tf_op jit(solution)/shard_map/grad_z/ppermute | solution.py:139
  15.9 20.5 %all-to-all-start = ((bf16[4,80,512]{2,1,0:T(8,128)(2,1)}), bf16[4,80,512]{2,1,0:T(8,128)(2,1)S(1)}, u32[]{:S(2)}, u32[]{:S(2)}) async-start(bf16[4,80,512]{2,1,0:T(8,128)(2,1)} %broadcast_in_dim.21), calls=%async_computation | async-start | bytes 655360 | tf_op jit(solution)/shard_map/grad_z/all_to_all | solution.py:125
  22.8 13.6 %collective-permute-start.1 = (bf16[40,512]{1,0:T(8,128)(2,1)S(1)}, bf16[40,512]{1,0:T(8,128)(2,1)S(1)}, u32[]{:S(2)}, u32[]{:S(2)}) collective-permute-start(bf16[40,512]{1,0:T(8,128)(2,1)S(1)} %get-tuple-element.38), channel_id=1, source_target_pairs={{0,32},{32,0},{64,96},{96,64},{128,160},{160,128},{192,224},{224,1... | collective-permute-start | bytes 122888 | tf_op jit(solution)/shard_map/in_pair/ppermute | solution.py:143
  37.6 17.9 %all-to-all-start.1 = ((bf16[4,320,512]{2,1,0:T(8,128)(2,1)}), bf16[4,320,512]{2,1,0:T(8,128)(2,1)S(1)}, u32[]{:S(2)}, u32[]{:S(2)}) async-start(bf16[4,320,512]{2,1,0:T(8,128)(2,1)} %broadcast_in_dim.23), calls=%async_computation.1 | async-start | bytes 2621440 | tf_op jit(solution)/shard_map/grad_y/all_to_all | solution.py:125
  41.2 14.5 %copy-start = (bf16[512,512]{1,0:T(8,128)(2,1)S(1)}, bf16[512,512]{1,0:T(8,128)(2,1)}, u32[]{:S(2)}) copy-start(bf16[512,512]{1,0:T(8,128)(2,1)} %weight.3) | copy-start | bytes 1572868
  41.2 15.0 %collective-permute-start.2 = (bf16[80,512]{1,0:T(8,128)(2,1)S(1)}, bf16[80,512]{1,0:T(8,128)(2,1)S(1)}, u32[]{:S(2)}, u32[]{:S(2)}) collective-permute-start(bf16[80,512]{1,0:T(8,128)(2,1)S(1)} %pad_maximum_fusion.2), channel_id=1, source_target_pairs={{0,192},{32,96},{64,0},{96,160},{128,64},{160,224},{192,128},{224,... | collective-permute-start | bytes 245768 | tf_op jit(solution)/shard_map/in_z/ppermute | solution.py:148
  56.2 13.3 %collective-permute-start.3 = (bf16[640,512]{1,0:T(8,128)(2,1)S(1)}, bf16[640,512]{1,0:T(8,128)(2,1)S(1)}, u32[]{:S(2)}, u32[]{:S(2)}) collective-permute-start(bf16[640,512]{1,0:T(8,128)(2,1)S(1)} %sum_core.2), channel_id=1, source_target_pairs={{0,32},{32,0},{64,96},{96,64},{128,160},{160,128},{192,224},{224,1... | collective-permute-start | bytes 1966088 | tf_op jit(solution)/shard_map/sum_core/ppermute | solution.py:157
  70.8 14.2 %all-to-all-start.2 = ((bf16[4,160,512]{2,1,0:T(8,128)(2,1)}), bf16[4,160,512]{2,1,0:T(8,128)(2,1)S(1)}, u32[]{:S(2)}, u32[]{:S(2)}) async-start(bf16[4,160,512]{2,1,0:T(8,128)(2,1)} %bitcast.9), calls=%async_computation.2 | async-start | bytes 1310720 | tf_op jit(solution)/shard_map/sum_x/all_to_all | solution.py:163
  74.8 14.2 %collective-permute-start.5 = (bf16[40,512]{1,0:T(8,128)(2,1)S(1)}, bf16[40,512]{1,0:T(8,128)(2,1)S(1)}, u32[]{:S(2)}, u32[]{:S(2)}) collective-permute-start(bf16[40,512]{1,0:T(8,128)(2,1)S(1)} %slice.9), channel_id=1, source_target_pairs={{0,192},{32,96},{64,0},{96,160},{128,64},{160,224},{192,128},{224,... | collective-permute-start | bytes 122888 | tf_op jit(solution)/shard_map/in_z/ppermute | solution.py:161
  89.8 18.9 %all-to-all-start.3 = ((bf16[4,160,512]{2,1,0:T(8,128)(2,1)}), bf16[4,160,512]{2,1,0:T(8,128)(2,1)S(1)}, u32[]{:S(2)}, u32[]{:S(2)}) async-start(bf16[4,160,512]{2,1,0:T(8,128)(2,1)} %broadcast_in_dim.24), calls=%async_computation.3 | async-start | bytes 1310720 | tf_op jit(solution)/shard_map/in_x/all_to_all | solution.py:125
  94.1 14.7 %collective-permute-start.4 = (bf16[40,512]{1,0:T(8,128)(2,1)S(1)}, bf16[40,512]{1,0:T(8,128)(2,1)S(1)}, u32[]{:S(2)}, u32[]{:S(2)}) collective-permute-start(bf16[40,512]{1,0:T(8,128)(2,1)S(1)} %get-tuple-element.36), channel_id=1, source_target_pairs={{0,64},{32,224},{64,128},{96,32},{128,192},{160,96},{192,0},{224,1... | collective-permute-start | bytes 122888 | tf_op jit(solution)/shard_map/sum_z/ppermute | solution.py:173
  108.8 18.2 %collective-permute-start.7 = (bf16[640,512]{1,0:T(8,128)(2,1)S(1)}, bf16[640,512]{1,0:T(8,128)(2,1)S(1)}, u32[]{:S(2)}, u32[]{:S(2)}) collective-permute-start(bf16[640,512]{1,0:T(8,128)(2,1)S(1)} %bitcast.21), channel_id=1, source_target_pairs={{0,32},{32,0},{64,96},{96,64},{128,160},{160,128},{192,224},{224,1... | collective-permute-start | bytes 1966088 | tf_op jit(solution)/shard_map/in_core/ppermute | solution.py:177
  114.6 17.1 %collective-permute-start.6 = (bf16[2,40,512]{2,1,0:T(8,128)(2,1)S(1)}, bf16[2,40,512]{2,1,0:T(8,128)(2,1)S(1)}, u32[]{:S(2)}, u32[]{:S(2)}) collective-permute-start(bf16[2,40,512]{2,1,0:T(8,128)(2,1)S(1)} %sum_z.1), channel_id=1, source_target_pairs={{0,64},{32,224},{64,128},{96,32},{128,192},{160,96},{192,0},{224,1... | collective-permute-start | bytes 245768 | tf_op jit(solution)/shard_map/sum_z/ppermute | solution.py:175
  131.6 3.1 %collective-permute-start.8 = (bf16[40,512]{1,0:T(8,128)(2,1)S(1)}, bf16[40,512]{1,0:T(8,128)(2,1)S(1)}, u32[]{:S(2)}, u32[]{:S(2)}) collective-permute-start(bf16[40,512]{1,0:T(8,128)(2,1)S(1)} %slice_bitcast_fusion), channel_id=1, source_target_pairs={{0,32},{32,0},{64,96},{96,64},{128,160},{160,128},{192,224},{224,1... | collective-permute-start | bytes 122888 | tf_op jit(solution)/shard_map/sum_z/ppermute | solution.py:182

commit v4 on v3

--- a/solution.py
+++ b/solution.py
@@ -97,19 +97,24 @@
     part[...] = total.astype(bf16)
 
 
-def line_kernel(across, far, near, mine):
+def line_kernel(across, near_in, near, mine, sent):
     total = across[0].astype(f32)
     for x in range(1, 4):
         total += across[x].astype(f32)
     near[0] = total[:40]
     near[1] = total[40:80]
-    far[...] = total[80:120].astype(bf16)
     mine[...] = total[120:]
-
-
-def near_kernel(near, got, sent):
-    sent[0] = (near[0] + got[...].astype(f32)).astype(bf16)
+    sent[0] = total[80:120].astype(bf16)
+    sent[1] = near_in[0]
+
+
+def near_kernel(near, got, near_in, paired, sent, lines):
+    sent[0] = (near[0] + got[0].astype(f32)).astype(bf16)
     sent[1] = near[1].astype(bf16)
+    lines[0] = near_in[0]
+    lines[1] = near_in[1]
+    lines[2] = got[1]
+    lines[3] = paired[...]
 
 
 def outer_kernel(own, own_in, other, other_in, grad):
@@ -140,12 +145,13 @@
         pair = jnp.stack([jnp.where(first, grad, far), jnp.where(first, far, grad)])
         line = spread(pair.reshape(80, 512), "col", quads)
     with jax.named_scope("in_pair"):
-        both = jnp.concatenate([kept, lax.ppermute(kept, "row", row_pairs(1))])
+        paired = lax.ppermute(kept, "row", row_pairs(1))
+        both = jnp.stack([paired, kept])
     line, both = lax.optimization_barrier((line, both))
     with jax.named_scope("grad_y"):
         grads = spread(line.reshape(320, 512), "col", along_y)
     with jax.named_scope("in_z"):
-        near_in = lax.ppermute(both, "row", ring(-1))
+        near_in = lax.ppermute(both, "row", ring(1))
 
     shared = ((4, 4, 40, 512), bf16)
     own, other = call(sort_kernel, [shared, shared], [h, core], [grads.reshape(4, 4, 2, 40, 512)])
@@ -156,31 +162,28 @@
         sent, near_in = lax.optimization_barrier((sent, near_in))
         got = lax.ppermute(sent, "row", row_pairs(1))
         (part,) = call(own_kernel, [((640, 512), bf16)], [], [own, weight, got])
-    part, near_in = lax.optimization_barrier((part, near_in))
-    with jax.named_scope("in_z"):
-        far_in = lax.ppermute(near_in[:40], "row", ring(-1))
+    block = (40, 512)
     with jax.named_scope("sum_x"):
         across = lax.all_to_all(part.reshape(4, 160, 512), "row", 0, 0, axis_index_groups=along_x)
-        block = (40, 512)
-        far, near, mine = call(
-            line_kernel, [(block, bf16), ((2, *block), f32), (block, f32)], [], [across]
+        near, mine, sent = call(
+            line_kernel, [((2, *block), f32), (block, f32), ((2, *block), bf16)], [], [across, near_in]
         )
-    far, kept = lax.optimization_barrier((far, kept))
+    with jax.named_scope("sum_z"):
+        got = lax.ppermute(sent, "row", ring(1))
+        sent, lines = call(
+            near_kernel, [((2, *block), bf16), ((4, *block), bf16)], [], [near, got, near_in, paired]
+        )
+        near = lax.ppermute(sent, "row", ring(1))
     with jax.named_scope("in_x"):
-        lines = jnp.concatenate([near_in, far_in, kept])
-        own_in = spread(lines, "row", along_x).reshape(640, 512)
+        other_in = lax.all_gather(lines.reshape(160, 512), "row", axis=0, tiled=True, axis_index_groups=along_x)
+    near, other_in = lax.optimization_barrier((near, other_in))
     with jax.named_scope("sum_z"):
-        (sent,) = call(near_kernel, [((2, *block), bf16)], [], [near, lax.ppermute(far, "row", ring(1))])
-        sent, own_in = lax.optimization_barrier((sent, own_in))
-        near = lax.ppermute(sent, "row", ring(1))
+        got = lax.ppermute(near[1], "row", row_pairs(1))
+        input_grad = (mine + near[0].astype(f32) + got.astype(f32)).astype(bf16)
     with jax.named_scope("in_core"):
-        other_in = lax.ppermute(own_in, "row", row_pairs(1))
+        own_in = lax.ppermute(other_in, "row", row_pairs(1))
     with jax.named_scope("outer"):
         (weight_grad,) = call(outer_kernel, [((512, 512), f32)], [], [own, own_in, other, other_in])
-    with jax.named_scope("sum_z"):
-        near, weight_grad = lax.optimization_barrier((near, weight_grad))
-        got = lax.ppermute(near[1], "row", row_pairs(1))
-        input_grad = (mine + near[0].astype(f32) + got.astype(f32)).astype(bf16)
     return (weight_grad, input_grad, new_history_in, new_history_grad)
 
 

time: 137 us -> 135 us (0.985)
  blocking collectives: 0 us -> 23.9 us
  waiting for transfers between devices: 21 us -> 8.54 us
  starting transfers between devices: 101 us -> 90.8 us
    all_to_all x0 -> x1, blocking collectives: none -> 13.4 us  [shards(): lax.all_to_all(part.reshape(4, 160, 512), 'row', 0, 0, axis_index_groups=...]
    all_gather x0 -> x1, blocking collectives: none -> 10.5 us  [shards(): lax.all_gather(lines.reshape(160, 512), 'row', axis=0, tiled=True, axis_i...]
    ppermute x1, starting transfers between devices: 11.6 us -> 6.34 us  [shards(): got = lax.ppermute(sent, 'row', row_pairs(1))]
    all_to_all x1 -> x0, waiting for transfers between devices: 4.29 us -> none  [shards(): lax.all_to_all(part.reshape(4, 160, 512), 'row', 0, 0, axis_index_groups=...]
    all_to_all x3 -> x2, starting transfers between devices: 13.4 us -> 9.15 us  [spread(): return lax.all_to_all(copies, axis_name, 0, 0, axis_index_groups=groups)]
    all_to_all x1 -> x0, starting transfers between devices: 3.92 us -> none  [shards(): lax.all_to_all(part.reshape(4, 160, 512), 'row', 0, 0, axis_index_groups=...]
    ppermute x5 -> x4, waiting for transfers between devices: 6.43 us -> 2.6 us  [the longest x1 1.74 us: shards(): got = lax.ppermute(sent, 'row', ring(1))]
    ppermute x5 -> x4, starting transfers between devices: 48.4 us -> 51.4 us  [the longest x1 13 us: shards(): got = lax.ppermute(sent, 'row', ring(1))]
  transfers between devices with their start and end apart: 13 -> 10, of which waited for: 9 -> 6; matrix products, arithmetic and copies ran while one was open for 0% -> 0% of each run, Pallas kernels for 2% -> 1%
where the time goes in v4:
time: 135 us
  starting transfers between devices  90.8 us (67%)
  blocking collectives  23.9 us (18%)
  waiting for transfers between devices  8.54 us (6%)
  Pallas kernels  4.38 us (3%)
  local copies, waits for them, and re-layouts  3.48 us (3%)
  between operations  2.79 us (2%)
    all_to_all x1, blocking collectives, shards(): lax.all_to_all(part.reshape(4, 160, 512), 'row', 0, 0, axis_index_groups=...  13.4 us
    ppermute x1, starting transfers between devices, shards(): got = lax.ppermute(sent, 'row', ring(1))  13 us
    ppermute x1, starting transfers between devices, shards(): own_in = lax.ppermute(other_in, 'row', row_pairs(1))  12.9 us
    ppermute x1, starting transfers between devices, shards(): paired = lax.ppermute(kept, 'row', row_pairs(1))  12.8 us
    ppermute x1, starting transfers between devices, shards(): near_in = lax.ppermute(both, 'row', ring(1))  12.7 us
    ppermute x1, starting transfers between devices, shards(): near = lax.ppermute(sent, 'row', ring(1))  12.4 us
    all_gather x1, blocking collectives, shards(): lax.all_gather(lines.reshape(160, 512), 'row', axis=0, tiled=True, axis_i...  10.5 us
    ppermute x1, starting transfers between devices, shards(): far = lax.ppermute(grad, 'col', halves)  9.63 us
  transfers between devices with their start and end apart: 10, of which 6 were waited for; matrix products, arithmetic and copies ran while one was open for 0% of the time, Pallas kernels for 1%

profile of v4, /device:TPU:1, one launch (start us, length us, event | category | flops | bytes accessed | tf_op | source)
XLA Modules:
  0.0 134.5 jit_solution(14683445427966090768)
XLA Ops:
  2.0 0.9 copy-done.1
  2.8 0.7 copy-done.3
  4.1 9.6 %collective-permute-start = (bf16[40,512]{1,0:T(8,128)(2,1)S(1)}, bf16[40,512]{1,0:T(8,128)(2,1)S(1)}, u32[]{:S(2)}, u32[]{:S(2)}) collective-permute-start(bf16[40,512]{1,0:T(8,128)(2,1)S(1)} %get-tuple-element.21), channel_id=1, source_target_pairs={{0,4},{1,5},{2,6},{3,7},{4,0},{5,1},{6,2},{7,3},{8,12},{9,13},{10,... | collective-permute-start | bytes 122888 | tf_op jit(solution)/shard_map/grad_z/ppermute | solution.py:144
  13.7 1.4 %collective-permute-done = bf16[40,512]{1,0:T(8,128)(2,1)S(1)} collective-permute-done((bf16[40,512]{1,0:T(8,128)(2,1)S(1)}, bf16[40,512]{1,0:T(8,128)(2,1)S(1)}, u32[]{:S(2)}, u32[]{:S(2)}) %collective-permute-start) | collective-permute-done | bytes 40992 | tf_op jit(solution)/shard_map/grad_z/ppermute | solution.py:144
  15.1 0.7 broadcast_in_dim.15
  15.9 5.6 %all-to-all-start = ((bf16[4,80,512]{2,1,0:T(8,128)(2,1)}), bf16[4,80,512]{2,1,0:T(8,128)(2,1)S(1)}, u32[]{:S(2)}, u32[]{:S(2)}) async-start(bf16[4,80,512]{2,1,0:T(8,128)(2,1)} %broadcast_in_dim.15), calls=%async_computation | async-start | bytes 655360 | tf_op jit(solution)/shard_map/grad_z/all_to_all | solution.py:130
  22.8 12.8 %collective-permute-start.1 = (bf16[40,512]{1,0:T(8,128)(2,1)S(1)}, bf16[40,512]{1,0:T(8,128)(2,1)S(1)}, u32[]{:S(2)}, u32[]{:S(2)}) collective-permute-start(bf16[40,512]{1,0:T(8,128)(2,1)S(1)} %get-tuple-element.22), channel_id=1, source_target_pairs={{0,32},{32,0},{64,96},{96,64},{128,160},{160,128},{192,224},{224,1... | collective-permute-start | bytes 122888 | tf_op jit(solution)/shard_map/in_pair/ppermute | solution.py:148
  35.6 0.8 collective-permute-done.1.paired
  36.4 1.2 broadcast_in_dim.17
  37.6 3.5 %all-to-all-start.1 = ((bf16[4,320,512]{2,1,0:T(8,128)(2,1)}), bf16[4,320,512]{2,1,0:T(8,128)(2,1)S(1)}, u32[]{:S(2)}, u32[]{:S(2)}) async-start(bf16[4,320,512]{2,1,0:T(8,128)(2,1)} %broadcast_in_dim.17), calls=%async_computation.1 | async-start | bytes 2621440 | tf_op jit(solution)/shard_map/grad_y/all_to_all | solution.py:130
  41.2 12.7 %collective-permute-start.2 = (bf16[2,40,512]{2,1,0:T(8,128)(2,1)S(1)}, bf16[2,40,512]{2,1,0:T(8,128)(2,1)S(1)}, u32[]{:S(2)}, u32[]{:S(2)}) collective-permute-start(bf16[2,40,512]{2,1,0:T(8,128)(2,1)S(1)} %pad_maximum_fusion.1), channel_id=1, source_target_pairs={{0,64},{32,224},{64,128},{96,32},{128,192},{160,96},{192,0},{224,1... | collective-permute-start | bytes 245768 | tf_op jit(solution)/shard_map/in_z/ppermute | solution.py:154
  53.9 1.7 %all-to-all-done.1 = bf16[4,320,512]{2,1,0:T(8,128)(2,1)S(1)} async-done(((bf16[4,320,512]{2,1,0:T(8,128)(2,1)}), bf16[4,320,512]{2,1,0:T(8,128)(2,1)S(1)}, u32[]{:S(2)}, u32[]{:S(2)}) %all-to-all-start.1) | async-done | bytes 1310752 | tf_op jit(solution)/shard_map/grad_y/all_to_all | solution.py:130
  56.2 6.3 %collective-permute-start.3 = (bf16[640,512]{1,0:T(8,128)(2,1)S(1)}, bf16[640,512]{1,0:T(8,128)(2,1)S(1)}, u32[]{:S(2)}, u32[]{:S(2)}) collective-permute-start(bf16[640,512]{1,0:T(8,128)(2,1)S(1)} %sum_core.2), channel_id=1, source_target_pairs={{0,32},{32,0},{64,96},{96,64},{128,160},{160,128},{192,224},{224,1... | collective-permute-start | bytes 1966088 | tf_op jit(solution)/shard_map/sum_core/ppermute | solution.py:163
  62.5 1.7 %collective-permute-done.3.got = bf16[640,512]{1,0:T(8,128)(2,1)S(1)} collective-permute-done((bf16[640,512]{1,0:T(8,128)(2,1)S(1)}, bf16[640,512]{1,0:T(8,128)(2,1)S(1)}, u32[]{:S(2)}, u32[]{:S(2)}) %collective-permute-start.3) | collective-permute-done | bytes 655392 | tf_op jit(solution)/shard_map/sum_core/ppermute | solution.py:163
  64.7 13.4 %all_to_all.15.across = bf16[4,160,512]{2,1,0:T(8,128)(2,1)S(1)} all-to-all(bf16[4,160,512]{2,1,0:T(8,128)(2,1)S(1)} %bitcast.25), channel_id=1, replica_groups={{0,256,512,768},{32,288,544,800},{64,320,576,832},{96,352,608,864},{128..., dimensions={0} | all-to-all | bytes 1310720 | tf_op jit(solution)/shard_map/sum_x/all_to_all | solution.py:167
  78.3 13.0 %collective-permute-start.4 = (bf16[2,40,512]{2,1,0:T(8,128)(2,1)S(1)}, bf16[2,40,512]{2,1,0:T(8,128)(2,1)S(1)}, u32[]{:S(2)}, u32[]{:S(2)}) collective-permute-start(bf16[2,40,512]{2,1,0:T(8,128)(2,1)S(1)} %get-tuple-element.30), channel_id=1, source_target_pairs={{0,64},{32,224},{64,128},{96,32},{128,192},{160,96},{192,0},{224,1... | collective-permute-start | bytes 245768 | tf_op jit(solution)/shard_map/sum_z/ppermute | solution.py:172
  91.3 1.7 %collective-permute-done.4.got = bf16[2,40,512]{2,1,0:T(8,128)(2,1)S(1)} collective-permute-done((bf16[2,40,512]{2,1,0:T(8,128)(2,1)S(1)}, bf16[2,40,512]{2,1,0:T(8,128)(2,1)S(1)}, u32[]{:S(2)}, u32[]{:S(2)}) %collective-permute-start.4) | collective-permute-done | bytes 81952 | tf_op jit(solution)/shard_map/sum_z/ppermute | solution.py:172
  93.0 12.4 %collective-permute-start.5 = (bf16[2,40,512]{2,1,0:T(8,128)(2,1)S(1)}, bf16[2,40,512]{2,1,0:T(8,128)(2,1)S(1)}, u32[]{:S(2)}, u32[]{:S(2)}) collective-permute-start(bf16[2,40,512]{2,1,0:T(8,128)(2,1)S(1)} %get-tuple-element.31), channel_id=1, source_target_pairs={{0,64},{32,224},{64,128},{96,32},{128,192},{160,96},{192,0},{224,1... | collective-permute-start | bytes 245768 | tf_op jit(solution)/shard_map/sum_z/ppermute | solution.py:176
  105.4 10.5 %all_gather.3.other_in = bf16[640,512]{1,0:T(8,128)(2,1)S(1)} all-gather(bf16[160,512]{1,0:T(8,128)(2,1)S(1)} %bitcast.26), channel_id=1, replica_groups={{0,256,512,768},{32,288,544,800},{64,320,576,832},{96,352,608,864},{128..., dimensions={0}, use_global_device_ids=true | all-gather | bytes 819200 | tf_op jit(solution)/shard_map/in_x/all_gather | solution.py:178
  115.9 12.9 %collective-permute-start.6 = (bf16[640,512]{1,0:T(8,128)(2,1)S(1)}, bf16[640,512]{1,0:T(8,128)(2,1)S(1)}, u32[]{:S(2)}, u32[]{:S(2)}) collective-permute-start(bf16[640,512]{1,0:T(8,128)(2,1)S(1)} %all_gather.3.other_in), channel_id=1, source_target_pairs={{0,32},{32,0},{64,96},{96,64},{128,160},{160,128},{192,224},{224,1... | collective-permute-start | bytes 1966088 | tf_op jit(solution)/shard_map/in_core/ppermute | solution.py:184
  128.8 1.9 %collective-permute-start.7 = (bf16[40,512]{1,0:T(8,128)(2,1)S(1)}, bf16[40,512]{1,0:T(8,128)(2,1)S(1)}, u32[]{:S(2)}, u32[]{:S(2)}) collective-permute-start(bf16[40,512]{1,0:T(8,128)(2,1)S(1)} %slice_bitcast_fusion), channel_id=1, source_target_pairs={{0,32},{32,0},{64,96},{96,64},{128,160},{160,128},{192,224},{224,1... | collective-permute-start | bytes 122888 | tf_op jit(solution)/shard_map/sum_z/ppermute | solution.py:181
  130.7 1.2 collective-permute-done.7
  131.9 0.6 fusion.1
  132.6 2.0 %outer.1 = f32[512,512]{1,0:T(8,128)} custom-call(bf16[640,512]{1,0:T(8,128)(2,1)S(1)} %bitcast.24, bf16[640,512]{1,0:T(8,128)(2,1)S(1)} %collective-permute-done.6.own_in, bf16[640,512]{1,0:T(8,128)(2,1)S(1)} %bitcast.22, bf16[640,512]{1,0:T(8,128)(2,1)S(1)} %all_gather.3.other_in), custom_call_target="tpu_custom_call" | custom-call | flops 1024 | bytes 1024 | tf_op jit(solution)/shard_map/outer/pallas_call | solution.py:70
  (23 shorter events, 2.5 us)
Async XLA Ops:
  0.6 21.5 %copy-start.4 = (f32[1,1,16]{2,1,0:T(1,128)S(1)}, f32[1,1,16]{2,1,0:T(1,128)}, u32[]{:S(2)}) copy-start(f32[1,1,16]{2,1,0:T(1,128)} %history_ref.3) | copy-start | bytes 196
  1.9 0.9 copy-start.1
  2.8 0.7 copy-start.3
  3.5 18.7 %copy-start.2 = (f32[40,512]{1,0:T(8,128)S(1)}, f32[40,512]{1,0:T(8,128)}, u32[]{:S(2)}) copy-start(f32[40,512]{1,0:T(8,128)} %values_ref.3) | copy-start | bytes 245764
  4.1 11.0 %collective-permute-start = (bf16[40,512]{1,0:T(8,128)(2,1)S(1)}, bf16[40,512]{1,0:T(8,128)(2,1)S(1)}, u32[]{:S(2)}, u32[]{:S(2)}) collective-permute-start(bf16[40,512]{1,0:T(8,128)(2,1)S(1)} %get-tuple-element.21), channel_id=1, source_target_pairs={{0,4},{1,5},{2,6},{3,7},{4,0},{5,1},{6,2},{7,3},{8,12},{9,13},{10,... | collective-permute-start | bytes 122888 | tf_op jit(solution)/shard_map/grad_z/ppermute | solution.py:144
  15.9 20.5 %all-to-all-start = ((bf16[4,80,512]{2,1,0:T(8,128)(2,1)}), bf16[4,80,512]{2,1,0:T(8,128)(2,1)S(1)}, u32[]{:S(2)}, u32[]{:S(2)}) async-start(bf16[4,80,512]{2,1,0:T(8,128)(2,1)} %broadcast_in_dim.15), calls=%async_computation | async-start | bytes 655360 | tf_op jit(solution)/shard_map/grad_z/all_to_all | solution.py:130
  22.8 13.6 %collective-permute-start.1 = (bf16[40,512]{1,0:T(8,128)(2,1)S(1)}, bf16[40,512]{1,0:T(8,128)(2,1)S(1)}, u32[]{:S(2)}, u32[]{:S(2)}) collective-permute-start(bf16[40,512]{1,0:T(8,128)(2,1)S(1)} %get-tuple-element.22), channel_id=1, source_target_pairs={{0,32},{32,0},{64,96},{96,64},{128,160},{160,128},{192,224},{224,1... | collective-permute-start | bytes 122888 | tf_op jit(solution)/shard_map/in_pair/ppermute | solution.py:148
  37.6 17.9 %all-to-all-start.1 = ((bf16[4,320,512]{2,1,0:T(8,128)(2,1)}), bf16[4,320,512]{2,1,0:T(8,128)(2,1)S(1)}, u32[]{:S(2)}, u32[]{:S(2)}) async-start(bf16[4,320,512]{2,1,0:T(8,128)(2,1)} %broadcast_in_dim.17), calls=%async_computation.1 | async-start | bytes 2621440 | tf_op jit(solution)/shard_map/grad_y/all_to_all | solution.py:130
  41.2 14.5 %copy-start = (bf16[512,512]{1,0:T(8,128)(2,1)S(1)}, bf16[512,512]{1,0:T(8,128)(2,1)}, u32[]{:S(2)}) copy-start(bf16[512,512]{1,0:T(8,128)(2,1)} %weight.3) | copy-start | bytes 1572868
  41.2 15.0 %collective-permute-start.2 = (bf16[2,40,512]{2,1,0:T(8,128)(2,1)S(1)}, bf16[2,40,512]{2,1,0:T(8,128)(2,1)S(1)}, u32[]{:S(2)}, u32[]{:S(2)}) collective-permute-start(bf16[2,40,512]{2,1,0:T(8,128)(2,1)S(1)} %pad_maximum_fusion.1), channel_id=1, source_target_pairs={{0,64},{32,224},{64,128},{96,32},{128,192},{160,96},{192,0},{224,1... | collective-permute-start | bytes 245768 | tf_op jit(solution)/shard_map/in_z/ppermute | solution.py:154
  56.2 8.1 %collective-permute-start.3 = (bf16[640,512]{1,0:T(8,128)(2,1)S(1)}, bf16[640,512]{1,0:T(8,128)(2,1)S(1)}, u32[]{:S(2)}, u32[]{:S(2)}) collective-permute-start(bf16[640,512]{1,0:T(8,128)(2,1)S(1)} %sum_core.2), channel_id=1, source_target_pairs={{0,32},{32,0},{64,96},{96,64},{128,160},{160,128},{192,224},{224,1... | collective-permute-start | bytes 1966088 | tf_op jit(solution)/shard_map/sum_core/ppermute | solution.py:163
  78.3 14.8 %collective-permute-start.4 = (bf16[2,40,512]{2,1,0:T(8,128)(2,1)S(1)}, bf16[2,40,512]{2,1,0:T(8,128)(2,1)S(1)}, u32[]{:S(2)}, u32[]{:S(2)}) collective-permute-start(bf16[2,40,512]{2,1,0:T(8,128)(2,1)S(1)} %get-tuple-element.30), channel_id=1, source_target_pairs={{0,64},{32,224},{64,128},{96,32},{128,192},{160,96},{192,0},{224,1... | collective-permute-start | bytes 245768 | tf_op jit(solution)/shard_map/sum_z/ppermute | solution.py:172
  93.0 22.8 %collective-permute-start.5 = (bf16[2,40,512]{2,1,0:T(8,128)(2,1)S(1)}, bf16[2,40,512]{2,1,0:T(8,128)(2,1)S(1)}, u32[]{:S(2)}, u32[]{:S(2)}) collective-permute-start(bf16[2,40,512]{2,1,0:T(8,128)(2,1)S(1)} %get-tuple-element.31), channel_id=1, source_target_pairs={{0,64},{32,224},{64,128},{96,32},{128,192},{160,96},{192,0},{224,1... | collective-permute-start | bytes 245768 | tf_op jit(solution)/shard_map/sum_z/ppermute | solution.py:176
  115.9 16.7 %collective-permute-start.6 = (bf16[640,512]{1,0:T(8,128)(2,1)S(1)}, bf16[640,512]{1,0:T(8,128)(2,1)S(1)}, u32[]{:S(2)}, u32[]{:S(2)}) collective-permute-start(bf16[640,512]{1,0:T(8,128)(2,1)S(1)} %all_gather.3.other_in), channel_id=1, source_target_pairs={{0,32},{32,0},{64,96},{96,64},{128,160},{160,128},{192,224},{224,1... | collective-permute-start | bytes 1966088 | tf_op jit(solution)/shard_map/in_core/ppermute | solution.py:184
  128.8 3.1 %collective-permute-start.7 = (bf16[40,512]{1,0:T(8,128)(2,1)S(1)}, bf16[40,512]{1,0:T(8,128)(2,1)S(1)}, u32[]{:S(2)}, u32[]{:S(2)}) collective-permute-start(bf16[40,512]{1,0:T(8,128)(2,1)S(1)} %slice_bitcast_fusion), channel_id=1, source_target_pairs={{0,32},{32,0},{64,96},{96,64},{128,160},{160,128},{192,224},{224,1... | collective-permute-start | bytes 122888 | tf_op jit(solution)/shard_map/sum_z/ppermute | solution.py:181

commit v5 on v4

--- a/solution.py
+++ b/solution.py
@@ -81,7 +81,7 @@
 def sort_kernel(h, core, blocks, own, other):
     for c, ref in ((core[0], own), (1 - core[0], other)):
         turn = 1 - 2 * c
-        for p, (up, side) in enumerate(((turn, c), (turn, 1 - c), (2, c), (0, c))):
+        for p, (up, side) in enumerate(((turn, c), (turn, 1 - c), (0, c), (2, c))):
             to = jnp.bitwise_and(h[0] + up, 3)
             k = 2 * jnp.bitwise_and(to, 1) + side
             for y in range(4):
@@ -97,24 +97,24 @@
     part[...] = total.astype(bf16)
 
 
-def line_kernel(across, near_in, near, mine, sent):
+def line_kernel(across, near_in, paired, near, mine, sent, lines):
     total = across[0].astype(f32)
     for x in range(1, 4):
         total += across[x].astype(f32)
     near[0] = total[:40]
     near[1] = total[40:80]
-    mine[...] = total[120:]
-    sent[0] = total[80:120].astype(bf16)
+    mine[...] = total[80:120]
+    sent[0] = total[120:].astype(bf16)
     sent[1] = near_in[0]
-
-
-def near_kernel(near, got, near_in, paired, sent, lines):
+    lines[0] = near_in[0]
+    lines[1] = near_in[1]
+    lines[2] = paired[...]
+
+
+def near_kernel(near, got, sent, far):
     sent[0] = (near[0] + got[0].astype(f32)).astype(bf16)
     sent[1] = near[1].astype(bf16)
-    lines[0] = near_in[0]
-    lines[1] = near_in[1]
-    lines[2] = got[1]
-    lines[3] = paired[...]
+    far[...] = got[1]
 
 
 def outer_kernel(own, own_in, other, other_in, grad):
@@ -165,23 +165,28 @@
     block = (40, 512)
     with jax.named_scope("sum_x"):
         across = lax.all_to_all(part.reshape(4, 160, 512), "row", 0, 0, axis_index_groups=along_x)
-        near, mine, sent = call(
-            line_kernel, [((2, *block), f32), (block, f32), ((2, *block), bf16)], [], [across, near_in]
+        near, mine, sent, lines = call(
+            line_kernel,
+            [((2, *block), f32), (block, f32), ((2, *block), bf16), ((3, *block), bf16)],
+            [],
+            [across, near_in, paired],
         )
+    with jax.named_scope("in_x"):
+        most_in = lax.all_gather(lines, "row", axis=0, axis_index_groups=along_x)
     with jax.named_scope("sum_z"):
         got = lax.ppermute(sent, "row", ring(1))
-        sent, lines = call(
-            near_kernel, [((2, *block), bf16), ((4, *block), bf16)], [], [near, got, near_in, paired]
-        )
+        sent, last_in = call(near_kernel, [((2, *block), bf16), (block, bf16)], [], [near, got])
+        sent, most_in = lax.optimization_barrier((sent, most_in))
         near = lax.ppermute(sent, "row", ring(1))
     with jax.named_scope("in_x"):
-        other_in = lax.all_gather(lines.reshape(160, 512), "row", axis=0, tiled=True, axis_index_groups=along_x)
+        last_in = lax.all_gather(last_in, "row", axis=0, axis_index_groups=along_x)
+        other_in = jnp.concatenate([most_in, last_in[:, None]], axis=1).reshape(640, 512)
     near, other_in = lax.optimization_barrier((near, other_in))
+    with jax.named_scope("in_core"):
+        own_in = lax.ppermute(other_in, "row", row_pairs(1))
     with jax.named_scope("sum_z"):
         got = lax.ppermute(near[1], "row", row_pairs(1))
         input_grad = (mine + near[0].astype(f32) + got.astype(f32)).astype(bf16)
-    with jax.named_scope("in_core"):
-        own_in = lax.ppermute(other_in, "row", row_pairs(1))
     with jax.named_scope("outer"):
         (weight_grad,) = call(outer_kernel, [((512, 512), f32)], [], [own, own_in, other, other_in])
     return (weight_grad, input_grad, new_history_in, new_history_grad)

time: 135 us -> 146 us (1.081); the launches traced: 135 us -> 144 us
  blocking collectives: 23.9 us -> 33.7 us
  starting transfers between devices: 90.8 us -> 89.1 us
    all_gather x1 -> x2, blocking collectives: 10.5 us -> 20.3 us  [the longest x1 11.1 us: shards(): most_in = lax.all_gather(lines, 'row', axis=0, axis_index_groups=along_x)]
    ppermute x1, waiting for transfers between devices: 0.01 us -> 2.84 us  [shards(): near = lax.ppermute(sent, 'row', ring(1))]
    ppermute x1, waiting for transfers between devices: 1.74 us -> 0.01 us  [shards(): got = lax.ppermute(sent, 'row', ring(1))]
where the time goes in v5:
time: 146 us; the launch traced here: 144 us
  starting transfers between devices  89.1 us (61%)
  blocking collectives  33.7 us (23%)
  waiting for transfers between devices  9.64 us (7%)
  Pallas kernels  4.37 us (3%)
  local copies, waits for them, and re-layouts  3.48 us (2%)
  between operations  2.8 us (2%)
    all_to_all x1, blocking collectives, shards(): lax.all_to_all(part.reshape(4, 160, 512), 'row', 0, 0, axis_index_groups=...  13.4 us
    ppermute x1, starting transfers between devices, shards(): got = lax.ppermute(sent, 'row', ring(1))  13 us
    ppermute x1, starting transfers between devices, shards(): paired = lax.ppermute(kept, 'row', row_pairs(1))  12.8 us
    ppermute x1, starting transfers between devices, shards(): near_in = lax.ppermute(both, 'row', ring(1))  12.7 us
    ppermute x1, starting transfers between devices, shards(): own_in = lax.ppermute(other_in, 'row', row_pairs(1))  12.4 us
    ppermute x1, starting transfers between devices, shards(): near = lax.ppermute(sent, 'row', ring(1))  11.2 us
    all_gather x1, blocking collectives, shards(): most_in = lax.all_gather(lines, 'row', axis=0, axis_index_groups=along_x)  11.1 us
    ppermute x1, starting transfers between devices, shards(): far = lax.ppermute(grad, 'col', halves)  9.63 us
  transfers between devices with their start and end apart: 10, of which 6 were waited for; matrix products, arithmetic and copies ran while one was open for 0% of the time, Pallas kernels for 1%

profile of v5, /device:TPU:1, one launch (start us, length us, event | category | flops | bytes accessed | tf_op | source)
XLA Modules:
  0.0 143.8 jit_solution(6944557083529166203)
XLA Ops:
  2.0 0.9 copy-done.1
  2.8 0.7 copy-done.3
  4.1 9.6 %collective-permute-start = (bf16[40,512]{1,0:T(8,128)(2,1)S(1)}, bf16[40,512]{1,0:T(8,128)(2,1)S(1)}, u32[]{:S(2)}, u32[]{:S(2)}) collective-permute-start(bf16[40,512]{1,0:T(8,128)(2,1)S(1)} %get-tuple-element.24), channel_id=1, source_target_pairs={{0,4},{1,5},{2,6},{3,7},{4,0},{5,1},{6,2},{7,3},{8,12},{9,13},{10,... | collective-permute-start | bytes 122888 | tf_op jit(solution)/shard_map/grad_z/ppermute | solution.py:144
  13.7 1.4 collective-permute-done
  15.1 0.7 broadcast_in_dim.18
  15.9 5.6 %all-to-all-start = ((bf16[4,80,512]{2,1,0:T(8,128)(2,1)}), bf16[4,80,512]{2,1,0:T(8,128)(2,1)S(1)}, u32[]{:S(2)}, u32[]{:S(2)}) async-start(bf16[4,80,512]{2,1,0:T(8,128)(2,1)} %broadcast_in_dim.18), calls=%async_computation | async-start | bytes 655360 | tf_op jit(solution)/shard_map/grad_z/all_to_all | solution.py:130
  22.8 12.8 %collective-permute-start.1 = (bf16[40,512]{1,0:T(8,128)(2,1)S(1)}, bf16[40,512]{1,0:T(8,128)(2,1)S(1)}, u32[]{:S(2)}, u32[]{:S(2)}) collective-permute-start(bf16[40,512]{1,0:T(8,128)(2,1)S(1)} %get-tuple-element.25), channel_id=1, source_target_pairs={{0,32},{32,0},{64,96},{96,64},{128,160},{160,128},{192,224},{224,1... | collective-permute-start | bytes 122888 | tf_op jit(solution)/shard_map/in_pair/ppermute | solution.py:148
  35.6 0.8 collective-permute-done.1.paired
  36.4 1.2 broadcast_in_dim.20
  37.6 3.5 %all-to-all-start.1 = ((bf16[4,320,512]{2,1,0:T(8,128)(2,1)}), bf16[4,320,512]{2,1,0:T(8,128)(2,1)S(1)}, u32[]{:S(2)}, u32[]{:S(2)}) async-start(bf16[4,320,512]{2,1,0:T(8,128)(2,1)} %broadcast_in_dim.20), calls=%async_computation.1 | async-start | bytes 2621440 | tf_op jit(solution)/shard_map/grad_y/all_to_all | solution.py:130
  41.2 12.7 %collective-permute-start.2 = (bf16[2,40,512]{2,1,0:T(8,128)(2,1)S(1)}, bf16[2,40,512]{2,1,0:T(8,128)(2,1)S(1)}, u32[]{:S(2)}, u32[]{:S(2)}) collective-permute-start(bf16[2,40,512]{2,1,0:T(8,128)(2,1)S(1)} %pad_maximum_fusion.2), channel_id=1, source_target_pairs={{0,64},{32,224},{64,128},{96,32},{128,192},{160,96},{192,0},{224,1... | collective-permute-start | bytes 245768 | tf_op jit(solution)/shard_map/in_z/ppermute | solution.py:154
  53.9 1.7 %all-to-all-done.1 = bf16[4,320,512]{2,1,0:T(8,128)(2,1)S(1)} async-done(((bf16[4,320,512]{2,1,0:T(8,128)(2,1)}), bf16[4,320,512]{2,1,0:T(8,128)(2,1)S(1)}, u32[]{:S(2)}, u32[]{:S(2)}) %all-to-all-start.1) | async-done | bytes 1310752 | tf_op jit(solution)/shard_map/grad_y/all_to_all | solution.py:130
  56.2 6.3 %collective-permute-start.3 = (bf16[640,512]{1,0:T(8,128)(2,1)S(1)}, bf16[640,512]{1,0:T(8,128)(2,1)S(1)}, u32[]{:S(2)}, u32[]{:S(2)}) collective-permute-start(bf16[640,512]{1,0:T(8,128)(2,1)S(1)} %sum_core.2), channel_id=1, source_target_pairs={{0,32},{32,0},{64,96},{96,64},{128,160},{160,128},{192,224},{224,1... | collective-permute-start | bytes 1966088 | tf_op jit(solution)/shard_map/sum_core/ppermute | solution.py:163
  62.5 1.7 %collective-permute-done.3.got = bf16[640,512]{1,0:T(8,128)(2,1)S(1)} collective-permute-done((bf16[640,512]{1,0:T(8,128)(2,1)S(1)}, bf16[640,512]{1,0:T(8,128)(2,1)S(1)}, u32[]{:S(2)}, u32[]{:S(2)}) %collective-permute-start.3) | collective-permute-done | bytes 655392 | tf_op jit(solution)/shard_map/sum_core/ppermute | solution.py:163
  64.7 13.4 %all_to_all.15.across = bf16[4,160,512]{2,1,0:T(8,128)(2,1)S(1)} all-to-all(bf16[4,160,512]{2,1,0:T(8,128)(2,1)S(1)} %bitcast.31), channel_id=1, replica_groups={{0,256,512,768},{32,288,544,800},{64,320,576,832},{96,352,608,864},{128..., dimensions={0} | all-to-all | bytes 1310720 | tf_op jit(solution)/shard_map/sum_x/all_to_all | solution.py:167
  78.3 13.0 %collective-permute-start.4 = (bf16[2,40,512]{2,1,0:T(8,128)(2,1)S(1)}, bf16[2,40,512]{2,1,0:T(8,128)(2,1)S(1)}, u32[]{:S(2)}, u32[]{:S(2)}) collective-permute-start(bf16[2,40,512]{2,1,0:T(8,128)(2,1)S(1)} %get-tuple-element.33), channel_id=1, source_target_pairs={{0,64},{32,224},{64,128},{96,32},{128,192},{160,96},{192,0},{224,1... | collective-permute-start | bytes 245768 | tf_op jit(solution)/shard_map/sum_z/ppermute | solution.py:177
  91.3 11.1 %all-gather = bf16[12,40,512]{2,1,0:T(8,128)(2,1)S(1)} all-gather(bf16[3,40,512]{2,1,0:T(8,128)(2,1)S(1)} %get-tuple-element.35), channel_id=2, replica_groups={{0,256,512,768},{32,288,544,800},{64,320,576,832},{96,352,608,864},{128..., dimensions={0}, use_global_device_ids=true | all-gather | bytes 614400 | tf_op jit(solution)/shard_map/in_x/all_gather | solution.py:175
  102.4 9.2 %all-gather.1 = bf16[160,512]{1,0:T(8,128)(2,1)S(1)} all-gather(bf16[40,512]{1,0:T(8,128)(2,1)S(1)} %get-tuple-element.38), channel_id=3, replica_groups={{0,256,512,768},{32,288,544,800},{64,320,576,832},{96,352,608,864},{128..., dimensions={0}, use_global_device_ids=true | all-gather | bytes 204800 | tf_op jit(solution)/shard_map/in_x/all_gather | solution.py:182
  111.6 11.2 %collective-permute-start.5 = (bf16[2,40,512]{2,1,0:T(8,128)(2,1)S(1)}, bf16[2,40,512]{2,1,0:T(8,128)(2,1)S(1)}, u32[]{:S(2)}, u32[]{:S(2)}) collective-permute-start(bf16[2,40,512]{2,1,0:T(8,128)(2,1)S(1)} %get-tuple-element.36), channel_id=1, source_target_pairs={{0,64},{32,224},{64,128},{96,32},{128,192},{160,96},{192,0},{224,1... | collective-permute-start | bytes 245768 | tf_op jit(solution)/shard_map/sum_z/ppermute | solution.py:180
  122.8 2.8 %collective-permute-done.5 = bf16[2,40,512]{2,1,0:T(8,128)(2,1)S(1)} collective-permute-done((bf16[2,40,512]{2,1,0:T(8,128)(2,1)S(1)}, bf16[2,40,512]{2,1,0:T(8,128)(2,1)S(1)}, u32[]{:S(2)}, u32[]{:S(2)}) %collective-permute-start.5) | collective-permute-done | bytes 81952 | tf_op jit(solution)/shard_map/sum_z/ppermute | solution.py:180
  125.7 12.4 %collective-permute-start.6 = (bf16[640,512]{1,0:T(8,128)(2,1)S(1)}, bf16[640,512]{1,0:T(8,128)(2,1)S(1)}, u32[]{:S(2)}, u32[]{:S(2)}) collective-permute-start(bf16[640,512]{1,0:T(8,128)(2,1)S(1)} %bitcast.27), channel_id=1, source_target_pairs={{0,32},{32,0},{64,96},{96,64},{128,160},{160,128},{192,224},{224,1... | collective-permute-start | bytes 1966088 | tf_op jit(solution)/shard_map/in_core/ppermute | solution.py:186
  138.1 1.9 %collective-permute-start.7 = (bf16[40,512]{1,0:T(8,128)(2,1)S(1)}, bf16[40,512]{1,0:T(8,128)(2,1)S(1)}, u32[]{:S(2)}, u32[]{:S(2)}) collective-permute-start(bf16[40,512]{1,0:T(8,128)(2,1)S(1)} %slice_bitcast_fusion), channel_id=1, source_target_pairs={{0,32},{32,0},{64,96},{96,64},{128,160},{160,128},{192,224},{224,1... | collective-permute-start | bytes 122888 | tf_op jit(solution)/shard_map/sum_z/ppermute | solution.py:188
  140.0 1.2 collective-permute-done.7
  141.9 2.0 %outer.1 = f32[512,512]{1,0:T(8,128)} custom-call(bf16[640,512]{1,0:T(8,128)(2,1)S(1)} %bitcast.30, bf16[640,512]{1,0:T(8,128)(2,1)S(1)} %collective-permute-done.6.own_in, bf16[640,512]{1,0:T(8,128)(2,1)S(1)} %bitcast.26, bf16[640,512]{1,0:T(8,128)(2,1)S(1)} %bitcast.28), custom_call_target="tpu_custom_call" | custom-call | flops 1024 | bytes 1024 | tf_op jit(solution)/shard_map/outer/pallas_call | solution.py:70
  (25 shorter events, 3.2 us)
Async XLA Ops:
  0.6 21.5 %copy-start.4 = (f32[1,1,16]{2,1,0:T(1,128)S(1)}, f32[1,1,16]{2,1,0:T(1,128)}, u32[]{:S(2)}) copy-start(f32[1,1,16]{2,1,0:T(1,128)} %history_ref.3) | copy-start | bytes 196
  1.9 0.9 copy-start.1
  2.8 0.7 copy-start.3
  3.5 18.7 %copy-start.2 = (f32[40,512]{1,0:T(8,128)S(1)}, f32[40,512]{1,0:T(8,128)}, u32[]{:S(2)}) copy-start(f32[40,512]{1,0:T(8,128)} %values_ref.3) | copy-start | bytes 245764
  4.1 11.0 %collective-permute-start = (bf16[40,512]{1,0:T(8,128)(2,1)S(1)}, bf16[40,512]{1,0:T(8,128)(2,1)S(1)}, u32[]{:S(2)}, u32[]{:S(2)}) collective-permute-start(bf16[40,512]{1,0:T(8,128)(2,1)S(1)} %get-tuple-element.24), channel_id=1, source_target_pairs={{0,4},{1,5},{2,6},{3,7},{4,0},{5,1},{6,2},{7,3},{8,12},{9,13},{10,... | collective-permute-start | bytes 122888 | tf_op jit(solution)/shard_map/grad_z/ppermute | solution.py:144
  15.9 20.5 %all-to-all-start = ((bf16[4,80,512]{2,1,0:T(8,128)(2,1)}), bf16[4,80,512]{2,1,0:T(8,128)(2,1)S(1)}, u32[]{:S(2)}, u32[]{:S(2)}) async-start(bf16[4,80,512]{2,1,0:T(8,128)(2,1)} %broadcast_in_dim.18), calls=%async_computation | async-start | bytes 655360 | tf_op jit(solution)/shard_map/grad_z/all_to_all | solution.py:130
  22.8 13.6 %collective-permute-start.1 = (bf16[40,512]{1,0:T(8,128)(2,1)S(1)}, bf16[40,512]{1,0:T(8,128)(2,1)S(1)}, u32[]{:S(2)}, u32[]{:S(2)}) collective-permute-start(bf16[40,512]{1,0:T(8,128)(2,1)S(1)} %get-tuple-element.25), channel_id=1, source_target_pairs={{0,32},{32,0},{64,96},{96,64},{128,160},{160,128},{192,224},{224,1... | collective-permute-start | bytes 122888 | tf_op jit(solution)/shard_map/in_pair/ppermute | solution.py:148
  37.6 17.9 %all-to-all-start.1 = ((bf16[4,320,512]{2,1,0:T(8,128)(2,1)}), bf16[4,320,512]{2,1,0:T(8,128)(2,1)S(1)}, u32[]{:S(2)}, u32[]{:S(2)}) async-start(bf16[4,320,512]{2,1,0:T(8,128)(2,1)} %broadcast_in_dim.20), calls=%async_computation.1 | async-start | bytes 2621440 | tf_op jit(solution)/shard_map/grad_y/all_to_all | solution.py:130
  41.2 14.5 %copy-start = (bf16[512,512]{1,0:T(8,128)(2,1)S(1)}, bf16[512,512]{1,0:T(8,128)(2,1)}, u32[]{:S(2)}) copy-start(bf16[512,512]{1,0:T(8,128)(2,1)} %weight.3) | copy-start | bytes 1572868
  41.2 15.0 %collective-permute-start.2 = (bf16[2,40,512]{2,1,0:T(8,128)(2,1)S(1)}, bf16[2,40,512]{2,1,0:T(8,128)(2,1)S(1)}, u32[]{:S(2)}, u32[]{:S(2)}) collective-permute-start(bf16[2,40,512]{2,1,0:T(8,128)(2,1)S(1)} %pad_maximum_fusion.2), channel_id=1, source_target_pairs={{0,64},{32,224},{64,128},{96,32},{128,192},{160,96},{192,0},{224,1... | collective-permute-start | bytes 245768 | tf_op jit(solution)/shard_map/in_z/ppermute | solution.py:154
  56.2 8.1 %collective-permute-start.3 = (bf16[640,512]{1,0:T(8,128)(2,1)S(1)}, bf16[640,512]{1,0:T(8,128)(2,1)S(1)}, u32[]{:S(2)}, u32[]{:S(2)}) collective-permute-start(bf16[640,512]{1,0:T(8,128)(2,1)S(1)} %sum_core.2), channel_id=1, source_target_pairs={{0,32},{32,0},{64,96},{96,64},{128,160},{160,128},{192,224},{224,1... | collective-permute-start | bytes 1966088 | tf_op jit(solution)/shard_map/sum_core/ppermute | solution.py:163
  78.3 24.1 %collective-permute-start.4 = (bf16[2,40,512]{2,1,0:T(8,128)(2,1)S(1)}, bf16[2,40,512]{2,1,0:T(8,128)(2,1)S(1)}, u32[]{:S(2)}, u32[]{:S(2)}) collective-permute-start(bf16[2,40,512]{2,1,0:T(8,128)(2,1)S(1)} %get-tuple-element.33), channel_id=1, source_target_pairs={{0,64},{32,224},{64,128},{96,32},{128,192},{160,96},{192,0},{224,1... | collective-permute-start | bytes 245768 | tf_op jit(solution)/shard_map/sum_z/ppermute | solution.py:177
  111.6 14.1 %collective-permute-start.5 = (bf16[2,40,512]{2,1,0:T(8,128)(2,1)S(1)}, bf16[2,40,512]{2,1,0:T(8,128)(2,1)S(1)}, u32[]{:S(2)}, u32[]{:S(2)}) collective-permute-start(bf16[2,40,512]{2,1,0:T(8,128)(2,1)S(1)} %get-tuple-element.36), channel_id=1, source_target_pairs={{0,64},{32,224},{64,128},{96,32},{128,192},{160,96},{192,0},{224,1... | collective-permute-start | bytes 245768 | tf_op jit(solution)/shard_map/sum_z/ppermute | solution.py:180
  125.7 16.2 %collective-permute-start.6 = (bf16[640,512]{1,0:T(8,128)(2,1)S(1)}, bf16[640,512]{1,0:T(8,128)(2,1)S(1)}, u32[]{:S(2)}, u32[]{:S(2)}) collective-permute-start(bf16[640,512]{1,0:T(8,128)(2,1)S(1)} %bitcast.27), channel_id=1, source_target_pairs={{0,32},{32,0},{64,96},{96,64},{128,160},{160,128},{192,224},{224,1... | collective-permute-start | bytes 1966088 | tf_op jit(solution)/shard_map/in_core/ppermute | solution.py:186
  138.1 3.1 %collective-permute-start.7 = (bf16[40,512]{1,0:T(8,128)(2,1)S(1)}, bf16[40,512]{1,0:T(8,128)(2,1)S(1)}, u32[]{:S(2)}, u32[]{:S(2)}) collective-permute-start(bf16[40,512]{1,0:T(8,128)(2,1)S(1)} %slice_bitcast_fusion), channel_id=1, source_target_pairs={{0,32},{32,0},{64,96},{96,64},{128,160},{160,128},{192,224},{224,1... | collective-permute-start | bytes 122888 | tf_op jit(solution)/shard_map/sum_z/ppermute | solution.py:188

commit v6 on v3

--- a/solution.py
+++ b/solution.py
@@ -97,19 +97,26 @@
     part[...] = total.astype(bf16)
 
 
-def line_kernel(across, far, near, mine):
+def line_kernel(across, near, mine, sent):
     total = across[0].astype(f32)
     for x in range(1, 4):
         total += across[x].astype(f32)
     near[0] = total[:40]
     near[1] = total[40:80]
-    far[...] = total[80:120].astype(bf16)
     mine[...] = total[120:]
+    sent[...] = total[80:120].astype(bf16)
 
 
 def near_kernel(near, got, sent):
     sent[0] = (near[0] + got[...].astype(f32)).astype(bf16)
     sent[1] = near[1].astype(bf16)
+
+
+def lines_kernel(near_in, far_in, paired, lines):
+    lines[0] = near_in[0]
+    lines[1] = near_in[1]
+    lines[2] = far_in[...]
+    lines[3] = paired[...]
 
 
 def outer_kernel(own, own_in, other, other_in, grad):
@@ -140,12 +147,13 @@
         pair = jnp.stack([jnp.where(first, grad, far), jnp.where(first, far, grad)])
         line = spread(pair.reshape(80, 512), "col", quads)
     with jax.named_scope("in_pair"):
-        both = jnp.concatenate([kept, lax.ppermute(kept, "row", row_pairs(1))])
+        paired = lax.ppermute(kept, "row", row_pairs(1))
+        both = jnp.stack([paired, kept])
     line, both = lax.optimization_barrier((line, both))
     with jax.named_scope("grad_y"):
         grads = spread(line.reshape(320, 512), "col", along_y)
     with jax.named_scope("in_z"):
-        near_in = lax.ppermute(both, "row", ring(-1))
+        near_in = lax.ppermute(both, "row", ring(1))
 
     shared = ((4, 4, 40, 512), bf16)
     own, other = call(sort_kernel, [shared, shared], [h, core], [grads.reshape(4, 4, 2, 40, 512)])
@@ -156,25 +164,24 @@
         sent, near_in = lax.optimization_barrier((sent, near_in))
         got = lax.ppermute(sent, "row", row_pairs(1))
         (part,) = call(own_kernel, [((640, 512), bf16)], [], [own, weight, got])
+    block = (40, 512)
     part, near_in = lax.optimization_barrier((part, near_in))
     with jax.named_scope("in_z"):
-        far_in = lax.ppermute(near_in[:40], "row", ring(-1))
+        far_in = lax.ppermute(near_in[0], "row", ring(1))
     with jax.named_scope("sum_x"):
         across = lax.all_to_all(part.reshape(4, 160, 512), "row", 0, 0, axis_index_groups=along_x)
-        block = (40, 512)
-        far, near, mine = call(
-            line_kernel, [(block, bf16), ((2, *block), f32), (block, f32)], [], [across]
-        )
-    far, kept = lax.optimization_barrier((far, kept))
+        near, mine, sent = call(line_kernel, [((2, *block), f32), (block, f32), (block, bf16)], [], [across])
+    sent, paired = lax.optimization_barrier((sent, paired))
     with jax.named_scope("in_x"):
-        lines = jnp.concatenate([near_in, far_in, kept])
-        own_in = spread(lines, "row", along_x).reshape(640, 512)
+        (lines,) = call(lines_kernel, [((4, *block), bf16)], [], [near_in, far_in, paired])
+        other_in = lax.all_gather(lines.reshape(160, 512), "row", axis=0, tiled=True, axis_index_groups=along_x)
     with jax.named_scope("sum_z"):
-        (sent,) = call(near_kernel, [((2, *block), bf16)], [], [near, lax.ppermute(far, "row", ring(1))])
-        sent, own_in = lax.optimization_barrier((sent, own_in))
+        got = lax.ppermute(sent, "row", ring(1))
+        (sent,) = call(near_kernel, [((2, *block), bf16)], [], [near, got])
+        sent, other_in = lax.optimization_barrier((sent, other_in))
         near = lax.ppermute(sent, "row", ring(1))
     with jax.named_scope("in_core"):
-        other_in = lax.ppermute(own_in, "row", row_pairs(1))
+        own_in = lax.ppermute(other_in, "row", row_pairs(1))
     with jax.named_scope("outer"):
         (weight_grad,) = call(outer_kernel, [((512, 512), f32)], [], [own, own_in, other, other_in])
     with jax.named_scope("sum_z"):

time: 137 us -> 136 us (level)
  blocking collectives: 0 us -> 12.1 us
  starting transfers between devices: 101 us -> 92.3 us
  waiting for transfers between devices: 21 us -> 16.9 us
    all_gather x0 -> x1, blocking collectives: none -> 12.1 us  [shards(): lax.all_gather(lines.reshape(160, 512), 'row', axis=0, tiled=True, axis_i...]
    ppermute x1, waiting for transfers between devices: 2.66 us -> 10.4 us  [shards(): near = lax.ppermute(sent, 'row', ring(1))]
    ppermute x5, starting transfers between devices: 48.4 us -> 55.5 us  [the longest x1 13 us: shards(): far_in = lax.ppermute(near_in[0], 'row', ring(1))]
    ppermute x1, starting transfers between devices: 12.4 us -> 5.42 us  [shards(): near = lax.ppermute(sent, 'row', ring(1))]
    ppermute x5, waiting for transfers between devices: 6.43 us -> 0.86 us  [the longest x1 0.85 us: shards(): paired = lax.ppermute(kept, 'row', row_pairs(1))]
    ppermute x1, starting transfers between devices: 11.6 us -> 6.34 us  [shards(): got = lax.ppermute(sent, 'row', row_pairs(1))]
    all_to_all x1, waiting for transfers between devices: 4.29 us -> 0.01 us  [shards(): lax.all_to_all(part.reshape(4, 160, 512), 'row', 0, 0, axis_index_groups=...]
    all_to_all x3 -> x2, starting transfers between devices: 13.4 us -> 9.15 us  [spread(): return lax.all_to_all(copies, axis_name, 0, 0, axis_index_groups=groups)]
  transfers between devices with their start and end apart: 13 -> 12, of which waited for: 9 -> 6; matrix products, arithmetic and copies ran while one was open for 0% -> 0% of each run, Pallas kernels for 2% -> 2%
where the time goes in v6:
time: 136 us; the launch traced here: 133 us
  starting transfers between devices  92.3 us (68%)
  waiting for transfers between devices  16.9 us (12%)
  blocking collectives  12.1 us (9%)
  Pallas kernels  5.21 us (4%)
  local copies, waits for them, and re-layouts  3.47 us (3%)
  between operations  2.82 us (2%)
    ppermute x1, starting transfers between devices, shards(): far_in = lax.ppermute(near_in[0], 'row', ring(1))  13 us
    ppermute x1, starting transfers between devices, shards(): paired = lax.ppermute(kept, 'row', row_pairs(1))  12.8 us
    ppermute x1, starting transfers between devices, shards(): near_in = lax.ppermute(both, 'row', ring(1))  12.7 us
    all_gather x1, blocking collectives, shards(): lax.all_gather(lines.reshape(160, 512), 'row', axis=0, tiled=True, axis_i...  12.1 us
    ppermute x1, starting transfers between devices, shards(): got = lax.ppermute(sent, 'row', ring(1))  11.7 us
    ppermute x1, waiting for transfers between devices, shards(): near = lax.ppermute(sent, 'row', ring(1))  10.4 us
    ppermute x1, starting transfers between devices, shards(): far = lax.ppermute(grad, 'col', halves)  9.63 us
    all_to_all x2, starting transfers between devices, spread(): return lax.all_to_all(copies, axis_name, 0, 0, axis_index_groups=groups)  9.15 us
  transfers between devices with their start and end apart: 12, of which 6 were waited for; matrix products, arithmetic and copies ran while one was open for 0% of the time, Pallas kernels for 2%

profile of v6, /device:TPU:1, one launch (start us, length us, event | category | flops | bytes accessed | tf_op | source)
XLA Modules:
  0.0 133.4 jit_solution(13424159308673474218)
XLA Ops:
  2.0 0.9 copy-done.1
  4.1 9.6 %collective-permute-start = (bf16[40,512]{1,0:T(8,128)(2,1)S(1)}, bf16[40,512]{1,0:T(8,128)(2,1)S(1)}, u32[]{:S(2)}, u32[]{:S(2)}) collective-permute-start(bf16[40,512]{1,0:T(8,128)(2,1)S(1)} %get-tuple-element.25), channel_id=1, source_target_pairs={{0,4},{1,5},{2,6},{3,7},{4,0},{5,1},{6,2},{7,3},{8,12},{9,13},{10,... | collective-permute-start | bytes 122888 | tf_op jit(solution)/shard_map/grad_z/ppermute | solution.py:146
  13.7 1.4 %collective-permute-done = bf16[40,512]{1,0:T(8,128)(2,1)S(1)} collective-permute-done((bf16[40,512]{1,0:T(8,128)(2,1)S(1)}, bf16[40,512]{1,0:T(8,128)(2,1)S(1)}, u32[]{:S(2)}, u32[]{:S(2)}) %collective-permute-start) | collective-permute-done | bytes 40992 | tf_op jit(solution)/shard_map/grad_z/ppermute | solution.py:146
  15.1 0.7 broadcast_in_dim.15
  15.9 5.6 %all-to-all-start = ((bf16[4,80,512]{2,1,0:T(8,128)(2,1)}), bf16[4,80,512]{2,1,0:T(8,128)(2,1)S(1)}, u32[]{:S(2)}, u32[]{:S(2)}) async-start(bf16[4,80,512]{2,1,0:T(8,128)(2,1)} %broadcast_in_dim.15), calls=%async_computation | async-start | bytes 655360 | tf_op jit(solution)/shard_map/grad_z/all_to_all | solution.py:132
  22.8 12.8 %collective-permute-start.1 = (bf16[40,512]{1,0:T(8,128)(2,1)S(1)}, bf16[40,512]{1,0:T(8,128)(2,1)S(1)}, u32[]{:S(2)}, u32[]{:S(2)}) collective-permute-start(bf16[40,512]{1,0:T(8,128)(2,1)S(1)} %get-tuple-element.26), channel_id=1, source_target_pairs={{0,32},{32,0},{64,96},{96,64},{128,160},{160,128},{192,224},{224,1... | collective-permute-start | bytes 122888 | tf_op jit(solution)/shard_map/in_pair/ppermute | solution.py:150
  35.6 0.8 collective-permute-done.1.paired
  36.4 1.2 broadcast_in_dim.17
  37.6 3.5 %all-to-all-start.1 = ((bf16[4,320,512]{2,1,0:T(8,128)(2,1)}), bf16[4,320,512]{2,1,0:T(8,128)(2,1)S(1)}, u32[]{:S(2)}, u32[]{:S(2)}) async-start(bf16[4,320,512]{2,1,0:T(8,128)(2,1)} %broadcast_in_dim.17), calls=%async_computation.1 | async-start | bytes 2621440 | tf_op jit(solution)/shard_map/grad_y/all_to_all | solution.py:132
  41.2 12.7 %collective-permute-start.2 = (bf16[2,40,512]{2,1,0:T(8,128)(2,1)S(1)}, bf16[2,40,512]{2,1,0:T(8,128)(2,1)S(1)}, u32[]{:S(2)}, u32[]{:S(2)}) collective-permute-start(bf16[2,40,512]{2,1,0:T(8,128)(2,1)S(1)} %pad_maximum_fusion.1), channel_id=1, source_target_pairs={{0,64},{32,224},{64,128},{96,32},{128,192},{160,96},{192,0},{224,1... | collective-permute-start | bytes 245768 | tf_op jit(solution)/shard_map/in_z/ppermute | solution.py:156
  53.9 1.7 %all-to-all-done.1 = bf16[4,320,512]{2,1,0:T(8,128)(2,1)S(1)} async-done(((bf16[4,320,512]{2,1,0:T(8,128)(2,1)}), bf16[4,320,512]{2,1,0:T(8,128)(2,1)S(1)}, u32[]{:S(2)}, u32[]{:S(2)}) %all-to-all-start.1) | async-done | bytes 1310752 | tf_op jit(solution)/shard_map/grad_y/all_to_all | solution.py:132
  56.2 6.3 %collective-permute-start.3 = (bf16[640,512]{1,0:T(8,128)(2,1)S(1)}, bf16[640,512]{1,0:T(8,128)(2,1)S(1)}, u32[]{:S(2)}, u32[]{:S(2)}) collective-permute-start(bf16[640,512]{1,0:T(8,128)(2,1)S(1)} %sum_core.2), channel_id=1, source_target_pairs={{0,32},{32,0},{64,96},{96,64},{128,160},{160,128},{192,224},{224,1... | collective-permute-start | bytes 1966088 | tf_op jit(solution)/shard_map/sum_core/ppermute | solution.py:165
  62.5 1.7 %collective-permute-done.3.got = bf16[640,512]{1,0:T(8,128)(2,1)S(1)} collective-permute-done((bf16[640,512]{1,0:T(8,128)(2,1)S(1)}, bf16[640,512]{1,0:T(8,128)(2,1)S(1)}, u32[]{:S(2)}, u32[]{:S(2)}) %collective-permute-start.3) | collective-permute-done | bytes 655392 | tf_op jit(solution)/shard_map/sum_core/ppermute | solution.py:165
  64.2 1.3 %sum_core.3 = bf16[640,512]{1,0:T(8,128)(2,1)} custom-call(bf16[640,512]{1,0:T(8,128)(2,1)S(1)} %bitcast.25, bf16[512,512]{1,0:T(8,128)(2,1)S(1)} %copy-done, bf16[640,512]{1,0:T(8,128)(2,1)S(1)} %collective-permute-done.3.got), custom_call_target="tpu_custom_call" | custom-call | flops 1024 | bytes 1024 | tf_op jit(solution)/shard_map/sum_core/pallas_call | solution.py:70
  65.6 3.6 %all-to-all-start.2 = ((bf16[4,160,512]{2,1,0:T(8,128)(2,1)}), bf16[4,160,512]{2,1,0:T(8,128)(2,1)S(1)}, u32[]{:S(2)}, u32[]{:S(2)}) async-start(bf16[4,160,512]{2,1,0:T(8,128)(2,1)} %bitcast.11), calls=%async_computation.2 | async-start | bytes 1310720 | tf_op jit(solution)/shard_map/sum_x/all_to_all | solution.py:172
  69.2 13.0 %collective-permute-start.5 = (bf16[40,512]{1,0:T(8,128)(2,1)S(1)}, bf16[40,512]{1,0:T(8,128)(2,1)S(1)}, u32[]{:S(2)}, u32[]{:S(2)}) collective-permute-start(bf16[40,512]{1,0:T(8,128)(2,1)S(1)} %slice_bitcast_fusion.1), channel_id=1, source_target_pairs={{0,64},{32,224},{64,128},{96,32},{128,192},{160,96},{192,0},{224,1... | collective-permute-start | bytes 122888 | tf_op jit(solution)/shard_map/in_z/ppermute | solution.py:170
  82.3 11.7 %collective-permute-start.4 = (bf16[40,512]{1,0:T(8,128)(2,1)S(1)}, bf16[40,512]{1,0:T(8,128)(2,1)S(1)}, u32[]{:S(2)}, u32[]{:S(2)}) collective-permute-start(bf16[40,512]{1,0:T(8,128)(2,1)S(1)} %get-tuple-element.36), channel_id=1, source_target_pairs={{0,64},{32,224},{64,128},{96,32},{128,192},{160,96},{192,0},{224,1... | collective-permute-start | bytes 122888 | tf_op jit(solution)/shard_map/sum_z/ppermute | solution.py:179
  94.0 12.1 %all_gather.3.other_in = bf16[640,512]{1,0:T(8,128)(2,1)S(1)} all-gather(bf16[160,512]{1,0:T(8,128)(2,1)S(1)} %bitcast.27), channel_id=1, replica_groups={{0,256,512,768},{32,288,544,800},{64,320,576,832},{96,352,608,864},{128..., dimensions={0}, use_global_device_ids=true | all-gather | bytes 819200 | tf_op jit(solution)/shard_map/in_x/all_gather | solution.py:177
  106.1 5.4 %collective-permute-start.7 = (bf16[640,512]{1,0:T(8,128)(2,1)S(1)}, bf16[640,512]{1,0:T(8,128)(2,1)S(1)}, u32[]{:S(2)}, u32[]{:S(2)}) collective-permute-start(bf16[640,512]{1,0:T(8,128)(2,1)S(1)} %all_gather.3.other_in), channel_id=1, source_target_pairs={{0,32},{32,0},{64,96},{96,64},{128,160},{160,128},{192,224},{224,1... | collective-permute-start | bytes 1966088 | tf_op jit(solution)/shard_map/in_core/ppermute | solution.py:184
  111.5 5.4 %collective-permute-start.6 = (bf16[2,40,512]{2,1,0:T(8,128)(2,1)S(1)}, bf16[2,40,512]{2,1,0:T(8,128)(2,1)S(1)}, u32[]{:S(2)}, u32[]{:S(2)}) collective-permute-start(bf16[2,40,512]{2,1,0:T(8,128)(2,1)S(1)} %sum_z.1), channel_id=1, source_target_pairs={{0,64},{32,224},{64,128},{96,32},{128,192},{160,96},{192,0},{224,1... | collective-permute-start | bytes 245768 | tf_op jit(solution)/shard_map/sum_z/ppermute | solution.py:182
  117.0 2.0 %outer.1 = f32[512,512]{1,0:T(8,128)} custom-call(bf16[640,512]{1,0:T(8,128)(2,1)S(1)} %bitcast.26, bf16[640,512]{1,0:T(8,128)(2,1)S(1)} %collective-permute-done.7.own_in, bf16[640,512]{1,0:T(8,128)(2,1)S(1)} %bitcast.24, bf16[640,512]{1,0:T(8,128)(2,1)S(1)} %all_gather.3.other_in), custom_call_target="tpu_custom_call" | custom-call | flops 1024 | bytes 1024 | tf_op jit(solution)/shard_map/outer/pallas_call | solution.py:70
  118.9 10.4 %collective-permute-done.6 = bf16[2,40,512]{2,1,0:T(8,128)(2,1)S(1)} collective-permute-done((bf16[2,40,512]{2,1,0:T(8,128)(2,1)S(1)}, bf16[2,40,512]{2,1,0:T(8,128)(2,1)S(1)}, u32[]{:S(2)}, u32[]{:S(2)}) %collective-permute-start.6) | collective-permute-done | bytes 81952 | tf_op jit(solution)/shard_map/sum_z/ppermute | solution.py:182
  129.4 2.6 %collective-permute-start.8 = (bf16[40,512]{1,0:T(8,128)(2,1)S(1)}, bf16[40,512]{1,0:T(8,128)(2,1)S(1)}, u32[]{:S(2)}, u32[]{:S(2)}) collective-permute-start(bf16[40,512]{1,0:T(8,128)(2,1)S(1)} %slice_bitcast_fusion), channel_id=1, source_target_pairs={{0,32},{32,0},{64,96},{96,64},{128,160},{160,128},{192,224},{224,1... | collective-permute-start | bytes 122888 | tf_op jit(solution)/shard_map/sum_z/ppermute | solution.py:189
  132.0 0.8 collective-permute-done.8
  (28 shorter events, 3.3 us)
Async XLA Ops:
  0.6 21.5 %copy-start.4 = (f32[1,1,16]{2,1,0:T(1,128)S(1)}, f32[1,1,16]{2,1,0:T(1,128)}, u32[]{:S(2)}) copy-start(f32[1,1,16]{2,1,0:T(1,128)} %history_ref.3) | copy-start | bytes 196
  1.9 0.9 copy-start.1
  2.8 0.7 copy-start.3
  3.5 18.7 %copy-start.2 = (f32[40,512]{1,0:T(8,128)S(1)}, f32[40,512]{1,0:T(8,128)}, u32[]{:S(2)}) copy-start(f32[40,512]{1,0:T(8,128)} %values_ref.3) | copy-start | bytes 245764
  4.1 11.0 %collective-permute-start = (bf16[40,512]{1,0:T(8,128)(2,1)S(1)}, bf16[40,512]{1,0:T(8,128)(2,1)S(1)}, u32[]{:S(2)}, u32[]{:S(2)}) collective-permute-start(bf16[40,512]{1,0:T(8,128)(2,1)S(1)} %get-tuple-element.25), channel_id=1, source_target_pairs={{0,4},{1,5},{2,6},{3,7},{4,0},{5,1},{6,2},{7,3},{8,12},{9,13},{10,... | collective-permute-start | bytes 122888 | tf_op jit(solution)/shard_map/grad_z/ppermute | solution.py:146
  15.9 20.5 %all-to-all-start = ((bf16[4,80,512]{2,1,0:T(8,128)(2,1)}), bf16[4,80,512]{2,1,0:T(8,128)(2,1)S(1)}, u32[]{:S(2)}, u32[]{:S(2)}) async-start(bf16[4,80,512]{2,1,0:T(8,128)(2,1)} %broadcast_in_dim.15), calls=%async_computation | async-start | bytes 655360 | tf_op jit(solution)/shard_map/grad_z/all_to_all | solution.py:132
  22.8 13.6 %collective-permute-start.1 = (bf16[40,512]{1,0:T(8,128)(2,1)S(1)}, bf16[40,512]{1,0:T(8,128)(2,1)S(1)}, u32[]{:S(2)}, u32[]{:S(2)}) collective-permute-start(bf16[40,512]{1,0:T(8,128)(2,1)S(1)} %get-tuple-element.26), channel_id=1, source_target_pairs={{0,32},{32,0},{64,96},{96,64},{128,160},{160,128},{192,224},{224,1... | collective-permute-start | bytes 122888 | tf_op jit(solution)/shard_map/in_pair/ppermute | solution.py:150
  37.6 17.9 %all-to-all-start.1 = ((bf16[4,320,512]{2,1,0:T(8,128)(2,1)}), bf16[4,320,512]{2,1,0:T(8,128)(2,1)S(1)}, u32[]{:S(2)}, u32[]{:S(2)}) async-start(bf16[4,320,512]{2,1,0:T(8,128)(2,1)} %broadcast_in_dim.17), calls=%async_computation.1 | async-start | bytes 2621440 | tf_op jit(solution)/shard_map/grad_y/all_to_all | solution.py:132
  41.2 14.5 %copy-start = (bf16[512,512]{1,0:T(8,128)(2,1)S(1)}, bf16[512,512]{1,0:T(8,128)(2,1)}, u32[]{:S(2)}) copy-start(bf16[512,512]{1,0:T(8,128)(2,1)} %weight.3) | copy-start | bytes 1572868
  41.2 15.0 %collective-permute-start.2 = (bf16[2,40,512]{2,1,0:T(8,128)(2,1)S(1)}, bf16[2,40,512]{2,1,0:T(8,128)(2,1)S(1)}, u32[]{:S(2)}, u32[]{:S(2)}) collective-permute-start(bf16[2,40,512]{2,1,0:T(8,128)(2,1)S(1)} %pad_maximum_fusion.1), channel_id=1, source_target_pairs={{0,64},{32,224},{64,128},{96,32},{128,192},{160,96},{192,0},{224,1... | collective-permute-start | bytes 245768 | tf_op jit(solution)/shard_map/in_z/ppermute | solution.py:156
  56.2 8.1 %collective-permute-start.3 = (bf16[640,512]{1,0:T(8,128)(2,1)S(1)}, bf16[640,512]{1,0:T(8,128)(2,1)S(1)}, u32[]{:S(2)}, u32[]{:S(2)}) collective-permute-start(bf16[640,512]{1,0:T(8,128)(2,1)S(1)} %sum_core.2), channel_id=1, source_target_pairs={{0,32},{32,0},{64,96},{96,64},{128,160},{160,128},{192,224},{224,1... | collective-permute-start | bytes 1966088 | tf_op jit(solution)/shard_map/sum_core/ppermute | solution.py:165
  65.6 16.6 %all-to-all-start.2 = ((bf16[4,160,512]{2,1,0:T(8,128)(2,1)}), bf16[4,160,512]{2,1,0:T(8,128)(2,1)S(1)}, u32[]{:S(2)}, u32[]{:S(2)}) async-start(bf16[4,160,512]{2,1,0:T(8,128)(2,1)} %bitcast.11), calls=%async_computation.2 | async-start | bytes 1310720 | tf_op jit(solution)/shard_map/sum_x/all_to_all | solution.py:172
  69.2 24.8 %collective-permute-start.5 = (bf16[40,512]{1,0:T(8,128)(2,1)S(1)}, bf16[40,512]{1,0:T(8,128)(2,1)S(1)}, u32[]{:S(2)}, u32[]{:S(2)}) collective-permute-start(bf16[40,512]{1,0:T(8,128)(2,1)S(1)} %slice_bitcast_fusion.1), channel_id=1, source_target_pairs={{0,64},{32,224},{64,128},{96,32},{128,192},{160,96},{192,0},{224,1... | collective-permute-start | bytes 122888 | tf_op jit(solution)/shard_map/in_z/ppermute | solution.py:170
  82.3 23.8 %collective-permute-start.4 = (bf16[40,512]{1,0:T(8,128)(2,1)S(1)}, bf16[40,512]{1,0:T(8,128)(2,1)S(1)}, u32[]{:S(2)}, u32[]{:S(2)}) collective-permute-start(bf16[40,512]{1,0:T(8,128)(2,1)S(1)} %get-tuple-element.36), channel_id=1, source_target_pairs={{0,64},{32,224},{64,128},{96,32},{128,192},{160,96},{192,0},{224,1... | collective-permute-start | bytes 122888 | tf_op jit(solution)/shard_map/sum_z/ppermute | solution.py:179
  106.1 10.8 %collective-permute-start.7 = (bf16[640,512]{1,0:T(8,128)(2,1)S(1)}, bf16[640,512]{1,0:T(8,128)(2,1)S(1)}, u32[]{:S(2)}, u32[]{:S(2)}) collective-permute-start(bf16[640,512]{1,0:T(8,128)(2,1)S(1)} %all_gather.3.other_in), channel_id=1, source_target_pairs={{0,32},{32,0},{64,96},{96,64},{128,160},{160,128},{192,224},{224,1... | collective-permute-start | bytes 1966088 | tf_op jit(solution)/shard_map/in_core/ppermute | solution.py:184
  111.5 17.9 %collective-permute-start.6 = (bf16[2,40,512]{2,1,0:T(8,128)(2,1)S(1)}, bf16[2,40,512]{2,1,0:T(8,128)(2,1)S(1)}, u32[]{:S(2)}, u32[]{:S(2)}) collective-permute-start(bf16[2,40,512]{2,1,0:T(8,128)(2,1)S(1)} %sum_z.1), channel_id=1, source_target_pairs={{0,64},{32,224},{64,128},{96,32},{128,192},{160,96},{192,0},{224,1... | collective-permute-start | bytes 245768 | tf_op jit(solution)/shard_map/sum_z/ppermute | solution.py:182
  129.4 3.4 %collective-permute-start.8 = (bf16[40,512]{1,0:T(8,128)(2,1)S(1)}, bf16[40,512]{1,0:T(8,128)(2,1)S(1)}, u32[]{:S(2)}, u32[]{:S(2)}) collective-permute-start(bf16[40,512]{1,0:T(8,128)(2,1)S(1)} %slice_bitcast_fusion), channel_id=1, source_target_pairs={{0,32},{32,0},{64,96},{96,64},{128,160},{160,128},{192,224},{224,1... | collective-permute-start | bytes 122888 | tf_op jit(solution)/shard_map/sum_z/ppermute | solution.py:189

commit v7 on v6

--- a/solution.py
+++ b/solution.py
@@ -29,6 +29,7 @@
 
 
 along_x = [[row_of(x, h, c) for x in range(4)] for h in range(4) for c in range(2)]
+along_core = [[row_of(x, h, c) for c in range(2)] for x in range(4) for h in range(4)]
 along_y = [[col_of(y, l) for y in range(4)] for l in range(8)]
 quads = [[col_of(y, 4 * s + k) for k in range(4)] for y in range(4) for s in range(2)]
 halves = [(col_of(y, l), col_of(y, l ^ 4)) for y in range(4) for l in range(8)]
@@ -119,11 +120,15 @@
     lines[3] = paired[...]
 
 
-def outer_kernel(own, own_in, other, other_in, grad):
+def outer_kernel(core, own, other, front, back, grad):
     contract = (((0,), (0,)), ((), ()))
-    grad[...] = lax.dot_general(
-        own[...], own_in[...], contract, preferred_element_type=f32
-    ) + lax.dot_general(other[...], other_in[...], contract, preferred_element_type=f32)
+    total = jnp.zeros(grad.shape, f32)
+    for ref, at in ((own, 1 - core[0]), (other, core[0])):
+        for i, part in enumerate((front, back)):
+            total += lax.dot_general(
+                ref[320 * i : 320 * (i + 1)], part[at], contract, preferred_element_type=f32
+            )
+    grad[...] = total
 
 
 def spread(block, axis_name, groups):
@@ -142,13 +147,14 @@
     grad, new_history_grad = restore(out_grad, history_grad, slot_grad, step_count)
     kept, new_history_in = restore(saved_input, history_in, slot_in, step_count)
 
+    with jax.named_scope("in_pair"):
+        paired = lax.ppermute(kept, "row", row_pairs(1))
     with jax.named_scope("grad_z"):
         far = lax.ppermute(grad, "col", halves)
+        far, paired = lax.optimization_barrier((far, paired))
         pair = jnp.stack([jnp.where(first, grad, far), jnp.where(first, far, grad)])
         line = spread(pair.reshape(80, 512), "col", quads)
-    with jax.named_scope("in_pair"):
-        paired = lax.ppermute(kept, "row", row_pairs(1))
-        both = jnp.stack([paired, kept])
+    both = jnp.stack([paired, kept])
     line, both = lax.optimization_barrier((line, both))
     with jax.named_scope("grad_y"):
         grads = spread(line.reshape(320, 512), "col", along_y)
@@ -181,12 +187,16 @@
         sent, other_in = lax.optimization_barrier((sent, other_in))
         near = lax.ppermute(sent, "row", ring(1))
     with jax.named_scope("in_core"):
-        own_in = lax.ppermute(other_in, "row", row_pairs(1))
+        front, back = (
+            lax.all_gather(half, "row", axis=0, axis_index_groups=along_core)
+            for half in (other_in[:320], other_in[320:])
+        )
     with jax.named_scope("outer"):
-        (weight_grad,) = call(outer_kernel, [((512, 512), f32)], [], [own, own_in, other, other_in])
+        (weight_grad,) = call(outer_kernel, [((512, 512), f32)], [core], [own, other, front, back])
     with jax.named_scope("sum_z"):
         near, weight_grad = lax.optimization_barrier((near, weight_grad))
-        got = lax.ppermute(near[1], "row", row_pairs(1))
+        got = lax.all_gather(near[1], "row", axis=0, axis_index_groups=along_core)
+        got = jnp.where(core[0] == 0, got[1], got[0])
         input_grad = (mine + near[0].astype(f32) + got.astype(f32)).astype(bf16)
     return (weight_grad, input_grad, new_history_in, new_history_grad)
 

time: 136 us -> 131 us (0.963); the launches traced: 133 us -> 130 us
  starting transfers between devices: 92.3 us -> 82.2 us
  blocking collectives: 12.1 us -> 21.6 us
  waiting for transfers between devices: 16.9 us -> 12.1 us
  local copies, waits for them, and re-layouts: 3.47 us -> 5.05 us
    ppermute x1, waiting for transfers between devices: 10.4 us -> 0.01 us  [shards(): near = lax.ppermute(sent, 'row', ring(1))]
    all_gather x0 -> x3, blocking collectives: none -> 9.55 us  [the longest x2 7.67 us: shards(): lax.all_gather(half, 'row', axis=0, axis_index_groups=along_core)]
    ppermute x2 -> x0, starting transfers between devices: 7.94 us -> none  [the longest x1 5.37 us: shards(): own_in = lax.ppermute(other_in, 'row', row_pairs(1))]
    all_to_all x2, waiting for transfers between devices: 1.69 us -> 6.18 us  [spread(): return lax.all_to_all(copies, axis_name, 0, 0, axis_index_groups=groups)]
    ppermute x1, starting transfers between devices: 12.8 us -> 8.32 us  [shards(): paired = lax.ppermute(kept, 'row', row_pairs(1))]
    ppermute x1, starting transfers between devices: 5.42 us -> 9.84 us  [shards(): near = lax.ppermute(sent, 'row', ring(1))]
    ppermute x1, waiting for transfers between devices: 0.01 us -> 3.42 us  [shards(): near_in = lax.ppermute(both, 'row', ring(1))]
    ppermute x1, starting transfers between devices: 12.7 us -> 15.2 us  [shards(): near_in = lax.ppermute(both, 'row', ring(1))]
  transfers between devices with their start and end apart: 12 -> 10, of which waited for: 6 -> 4; matrix products, arithmetic and copies ran while one was open for 0% -> 0% of each run, Pallas kernels for 2% -> 3%
where the time goes in v7:
time: 131 us; the launch traced here: 130 us
  starting transfers between devices  82.2 us (63%)
  blocking collectives  21.6 us (16%)
  waiting for transfers between devices  12.1 us (9%)
  Pallas kernels  5.5 us (4%)
  local copies, waits for them, and re-layouts  5.05 us (4%)
  between operations  2.8 us (2%)
    ppermute x1, starting transfers between devices, shards(): near_in = lax.ppermute(both, 'row', ring(1))  15.2 us
    all_gather x1, blocking collectives, shards(): lax.all_gather(lines.reshape(160, 512), 'row', axis=0, tiled=True, axis_i...  12.1 us
    ppermute x1, starting transfers between devices, shards(): far_in = lax.ppermute(near_in[0], 'row', ring(1))  11.3 us
    ppermute x1, starting transfers between devices, shards(): got = lax.ppermute(sent, 'row', ring(1))  11 us
    ppermute x1, starting transfers between devices, shards(): near = lax.ppermute(sent, 'row', ring(1))  9.84 us
    ppermute x1, starting transfers between devices, shards(): far = lax.ppermute(grad, 'col', halves)  9.63 us
    ppermute x1, starting transfers between devices, shards(): paired = lax.ppermute(kept, 'row', row_pairs(1))  8.32 us
    all_gather x2, blocking collectives, shards(): lax.all_gather(half, 'row', axis=0, axis_index_groups=along_core)  7.67 us
  transfers between devices with their start and end apart: 10, of which 4 were waited for; matrix products, arithmetic and copies ran while one was open for 0% of the time, Pallas kernels for 3%

profile of v7, /device:TPU:1, one launch (start us, length us, event | category | flops | bytes accessed | tf_op | source)
XLA Modules:
  0.0 130.0 jit_solution(15843735135130560930)
XLA Ops:
  1.9 0.9 copy-done.1
  4.1 9.6 %collective-permute-start = (bf16[40,512]{1,0:T(8,128)(2,1)S(1)}, bf16[40,512]{1,0:T(8,128)(2,1)S(1)}, u32[]{:S(2)}, u32[]{:S(2)}) collective-permute-start(bf16[40,512]{1,0:T(8,128)(2,1)S(1)} %get-tuple-element.27), channel_id=1, source_target_pairs={{0,4},{1,5},{2,6},{3,7},{4,0},{5,1},{6,2},{7,3},{8,12},{9,13},{10,... | collective-permute-start | bytes 122888 | tf_op jit(solution)/shard_map/grad_z/ppermute | solution.py:153
  14.4 0.9 copy-done.2
  16.5 8.3 %collective-permute-start.1 = (bf16[40,512]{1,0:T(8,128)(2,1)S(1)}, bf16[40,512]{1,0:T(8,128)(2,1)S(1)}, u32[]{:S(2)}, u32[]{:S(2)}) collective-permute-start(bf16[40,512]{1,0:T(8,128)(2,1)S(1)} %get-tuple-element.28), channel_id=1, source_target_pairs={{0,32},{32,0},{64,96},{96,64},{128,160},{160,128},{192,224},{224,1... | collective-permute-start | bytes 122888 | tf_op jit(solution)/shard_map/in_pair/ppermute | solution.py:151
  24.9 0.8 collective-permute-done.1.paired
  25.7 0.7 broadcast_in_dim.15
  26.5 3.5 %all-to-all-start = ((bf16[4,80,512]{2,1,0:T(8,128)(2,1)}), bf16[4,80,512]{2,1,0:T(8,128)(2,1)S(1)}, u32[]{:S(2)}, u32[]{:S(2)}) async-start(bf16[4,80,512]{2,1,0:T(8,128)(2,1)} %broadcast_in_dim.15), calls=%async_computation | async-start | bytes 655360 | tf_op jit(solution)/shard_map/grad_z/all_to_all | solution.py:137
  30.0 6.2 %all-to-all-done = bf16[4,80,512]{2,1,0:T(8,128)(2,1)S(1)} async-done(((bf16[4,80,512]{2,1,0:T(8,128)(2,1)}), bf16[4,80,512]{2,1,0:T(8,128)(2,1)S(1)}, u32[]{:S(2)}, u32[]{:S(2)}) %all-to-all-start) | async-done | bytes 327712 | tf_op jit(solution)/shard_map/grad_z/all_to_all | solution.py:137
  36.1 1.2 broadcast_in_dim.17
  37.3 3.5 %all-to-all-start.1 = ((bf16[4,320,512]{2,1,0:T(8,128)(2,1)}), bf16[4,320,512]{2,1,0:T(8,128)(2,1)S(1)}, u32[]{:S(2)}, u32[]{:S(2)}) async-start(bf16[4,320,512]{2,1,0:T(8,128)(2,1)} %broadcast_in_dim.17), calls=%async_computation.1 | async-start | bytes 2621440 | tf_op jit(solution)/shard_map/grad_y/all_to_all | solution.py:137
  40.9 15.2 %collective-permute-start.2 = (bf16[2,40,512]{2,1,0:T(8,128)(2,1)S(1)}, bf16[2,40,512]{2,1,0:T(8,128)(2,1)S(1)}, u32[]{:S(2)}, u32[]{:S(2)}) collective-permute-start(bf16[2,40,512]{2,1,0:T(8,128)(2,1)S(1)} %pad_maximum_fusion.1), channel_id=1, source_target_pairs={{0,64},{32,224},{64,128},{96,32},{128,192},{160,96},{192,0},{224,1... | collective-permute-start | bytes 245768 | tf_op jit(solution)/shard_map/in_z/ppermute | solution.py:162
  56.7 3.4 %collective-permute-done.2.near_in = bf16[2,40,512]{2,1,0:T(8,128)(2,1)S(1)} collective-permute-done((bf16[2,40,512]{2,1,0:T(8,128)(2,1)S(1)}, bf16[2,40,512]{2,1,0:T(8,128)(2,1)S(1)}, u32[]{:S(2)}, u32[]{:S(2)}) %collective-permute-start.2) | collective-permute-done | bytes 81952 | tf_op jit(solution)/shard_map/in_z/ppermute | solution.py:162
  60.2 4.1 %collective-permute-start.3 = (bf16[640,512]{1,0:T(8,128)(2,1)S(1)}, bf16[640,512]{1,0:T(8,128)(2,1)S(1)}, u32[]{:S(2)}, u32[]{:S(2)}) collective-permute-start(bf16[640,512]{1,0:T(8,128)(2,1)S(1)} %sum_core.2), channel_id=1, source_target_pairs={{0,32},{32,0},{64,96},{96,64},{128,160},{160,128},{192,224},{224,1... | collective-permute-start | bytes 1966088 | tf_op jit(solution)/shard_map/sum_core/ppermute | solution.py:171
  64.3 1.7 %collective-permute-done.3.got = bf16[640,512]{1,0:T(8,128)(2,1)S(1)} collective-permute-done((bf16[640,512]{1,0:T(8,128)(2,1)S(1)}, bf16[640,512]{1,0:T(8,128)(2,1)S(1)}, u32[]{:S(2)}, u32[]{:S(2)}) %collective-permute-start.3) | collective-permute-done | bytes 655392 | tf_op jit(solution)/shard_map/sum_core/ppermute | solution.py:171
  66.0 1.3 %sum_core.3 = bf16[640,512]{1,0:T(8,128)(2,1)} custom-call(bf16[640,512]{1,0:T(8,128)(2,1)S(1)} %bitcast.30, bf16[512,512]{1,0:T(8,128)(2,1)S(1)} %copy-done, bf16[640,512]{1,0:T(8,128)(2,1)S(1)} %collective-permute-done.3.got), custom_call_target="tpu_custom_call" | custom-call | flops 1024 | bytes 1024 | tf_op jit(solution)/shard_map/sum_core/pallas_call | solution.py:71
  67.3 5.8 %all-to-all-start.2 = ((bf16[4,160,512]{2,1,0:T(8,128)(2,1)}), bf16[4,160,512]{2,1,0:T(8,128)(2,1)S(1)}, u32[]{:S(2)}, u32[]{:S(2)}) async-start(bf16[4,160,512]{2,1,0:T(8,128)(2,1)} %bitcast.11), calls=%async_computation.2 | async-start | bytes 1310720 | tf_op jit(solution)/shard_map/sum_x/all_to_all | solution.py:178
  73.1 11.3 %collective-permute-start.5 = (bf16[40,512]{1,0:T(8,128)(2,1)S(1)}, bf16[40,512]{1,0:T(8,128)(2,1)S(1)}, u32[]{:S(2)}, u32[]{:S(2)}) collective-permute-start(bf16[40,512]{1,0:T(8,128)(2,1)S(1)} %slice_bitcast_fusion), channel_id=1, source_target_pairs={{0,64},{32,224},{64,128},{96,32},{128,192},{160,96},{192,0},{224,1... | collective-permute-start | bytes 122888 | tf_op jit(solution)/shard_map/in_z/ppermute | solution.py:176
  84.5 11.0 %collective-permute-start.4 = (bf16[40,512]{1,0:T(8,128)(2,1)S(1)}, bf16[40,512]{1,0:T(8,128)(2,1)S(1)}, u32[]{:S(2)}, u32[]{:S(2)}) collective-permute-start(bf16[40,512]{1,0:T(8,128)(2,1)S(1)} %get-tuple-element.40), channel_id=1, source_target_pairs={{0,64},{32,224},{64,128},{96,32},{128,192},{160,96},{192,0},{224,1... | collective-permute-start | bytes 122888 | tf_op jit(solution)/shard_map/sum_z/ppermute | solution.py:185
  95.6 12.1 %all_gather.18 = bf16[640,512]{1,0:T(8,128)(2,1)S(1)} all-gather(bf16[160,512]{1,0:T(8,128)(2,1)S(1)} %bitcast.34), channel_id=1, replica_groups={{0,256,512,768},{32,288,544,800},{64,320,576,832},{96,352,608,864},{128..., dimensions={0}, use_global_device_ids=true | all-gather | bytes 819200 | tf_op jit(solution)/shard_map/in_x/all_gather | solution.py:183
  107.7 9.8 %collective-permute-start.6 = (bf16[2,40,512]{2,1,0:T(8,128)(2,1)S(1)}, bf16[2,40,512]{2,1,0:T(8,128)(2,1)S(1)}, u32[]{:S(2)}, u32[]{:S(2)}) collective-permute-start(bf16[2,40,512]{2,1,0:T(8,128)(2,1)S(1)} %sum_z.1), channel_id=1, source_target_pairs={{0,64},{32,224},{64,128},{96,32},{128,192},{160,96},{192,0},{224,1... | collective-permute-start | bytes 245768 | tf_op jit(solution)/shard_map/sum_z/ppermute | solution.py:188
  117.6 5.4 %all-gather = bf16[640,512]{1,0:T(8,128)(2,1)S(1)} all-gather(bf16[320,512]{1,0:T(8,128)(2,1)S(1)} %get-tuple-element.51), channel_id=2, replica_groups={{0,32},{64,96},{128,160},{192,224},{256,288},{320,352},{384,416},{448,4..., dimensions={0}, use_global_device_ids=true | all-gather | bytes 983040 | tf_op jit(solution)/shard_map/in_core/all_gather | solution.py:191
  123.0 2.3 %all-gather.1 = bf16[640,512]{1,0:T(8,128)(2,1)S(1)} all-gather(bf16[320,512]{1,0:T(8,128)(2,1)S(1)} %get-tuple-element.50), channel_id=3, replica_groups={{0,32},{64,96},{128,160},{192,224},{256,288},{320,352},{384,416},{448,4..., dimensions={0}, use_global_device_ids=true | all-gather | bytes 983040 | tf_op jit(solution)/shard_map/in_core/all_gather | solution.py:191
  125.3 2.2 %outer.1 = f32[512,512]{1,0:T(8,128)} custom-call(s32[1]{0:T(128)} %bitcast.1.core, bf16[640,512]{1,0:T(8,128)(2,1)S(1)} %bitcast.31, bf16[640,512]{1,0:T(8,128)(2,1)S(1)} %bitcast.29, bf16[2,320,512]{2,1,0:T(8,128)(2,1)S(1)} %bitcast.32, bf16[2,320,512]{2,1,0:T(8,128)(2,1)S(1)} %bitcast.33), custom_call_target="tpu_custom_call" | custom-call | flops 1024 | bytes 1024 | tf_op jit(solution)/shard_map/outer/pallas_call | solution.py:71
  127.5 1.9 %all_gather.23 = bf16[2,40,512]{2,1,0:T(8,128)(2,1)S(1)} all-gather(bf16[1,40,512]{2,1,0:T(8,128)(2,1)S(1)} %slice.25), channel_id=1, replica_groups={{0,32},{64,96},{128,160},{192,224},{256,288},{320,352},{384,416},{448,4..., dimensions={0}, use_global_device_ids=true | all-gather | bytes 122880 | tf_op jit(solution)/shard_map/sum_z/all_gather | solution.py:198
  (28 shorter events, 4.0 us)
Async XLA Ops:
  1.9 0.9 copy-start.1
  2.8 0.7 copy-start.3
  4.1 20.8 %collective-permute-start = (bf16[40,512]{1,0:T(8,128)(2,1)S(1)}, bf16[40,512]{1,0:T(8,128)(2,1)S(1)}, u32[]{:S(2)}, u32[]{:S(2)}) collective-permute-start(bf16[40,512]{1,0:T(8,128)(2,1)S(1)} %get-tuple-element.27), channel_id=1, source_target_pairs={{0,4},{1,5},{2,6},{3,7},{4,0},{5,1},{6,2},{7,3},{8,12},{9,13},{10,... | collective-permute-start | bytes 122888 | tf_op jit(solution)/shard_map/grad_z/ppermute | solution.py:153
  14.4 0.9 copy-start.2
  15.3 0.7 copy-start.4
  16.5 9.2 %collective-permute-start.1 = (bf16[40,512]{1,0:T(8,128)(2,1)S(1)}, bf16[40,512]{1,0:T(8,128)(2,1)S(1)}, u32[]{:S(2)}, u32[]{:S(2)}) collective-permute-start(bf16[40,512]{1,0:T(8,128)(2,1)S(1)} %get-tuple-element.28), channel_id=1, source_target_pairs={{0,32},{32,0},{64,96},{96,64},{128,160},{160,128},{192,224},{224,1... | collective-permute-start | bytes 122888 | tf_op jit(solution)/shard_map/in_pair/ppermute | solution.py:151
  26.5 9.7 %all-to-all-start = ((bf16[4,80,512]{2,1,0:T(8,128)(2,1)}), bf16[4,80,512]{2,1,0:T(8,128)(2,1)S(1)}, u32[]{:S(2)}, u32[]{:S(2)}) async-start(bf16[4,80,512]{2,1,0:T(8,128)(2,1)} %broadcast_in_dim.15), calls=%async_computation | async-start | bytes 655360 | tf_op jit(solution)/shard_map/grad_z/all_to_all | solution.py:137
  37.3 18.8 %all-to-all-start.1 = ((bf16[4,320,512]{2,1,0:T(8,128)(2,1)}), bf16[4,320,512]{2,1,0:T(8,128)(2,1)S(1)}, u32[]{:S(2)}, u32[]{:S(2)}) async-start(bf16[4,320,512]{2,1,0:T(8,128)(2,1)} %broadcast_in_dim.17), calls=%async_computation.1 | async-start | bytes 2621440 | tf_op jit(solution)/shard_map/grad_y/all_to_all | solution.py:137
  40.9 15.4 %copy-start = (bf16[512,512]{1,0:T(8,128)(2,1)S(1)}, bf16[512,512]{1,0:T(8,128)(2,1)}, u32[]{:S(2)}) copy-start(bf16[512,512]{1,0:T(8,128)(2,1)} %weight.3) | copy-start | bytes 1572868
  40.9 19.3 %collective-permute-start.2 = (bf16[2,40,512]{2,1,0:T(8,128)(2,1)S(1)}, bf16[2,40,512]{2,1,0:T(8,128)(2,1)S(1)}, u32[]{:S(2)}, u32[]{:S(2)}) collective-permute-start(bf16[2,40,512]{2,1,0:T(8,128)(2,1)S(1)} %pad_maximum_fusion.1), channel_id=1, source_target_pairs={{0,64},{32,224},{64,128},{96,32},{128,192},{160,96},{192,0},{224,1... | collective-permute-start | bytes 245768 | tf_op jit(solution)/shard_map/in_z/ppermute | solution.py:162
  60.2 5.8 %collective-permute-start.3 = (bf16[640,512]{1,0:T(8,128)(2,1)S(1)}, bf16[640,512]{1,0:T(8,128)(2,1)S(1)}, u32[]{:S(2)}, u32[]{:S(2)}) collective-permute-start(bf16[640,512]{1,0:T(8,128)(2,1)S(1)} %sum_core.2), channel_id=1, source_target_pairs={{0,32},{32,0},{64,96},{96,64},{128,160},{160,128},{192,224},{224,1... | collective-permute-start | bytes 1966088 | tf_op jit(solution)/shard_map/sum_core/ppermute | solution.py:171
  67.3 17.1 %all-to-all-start.2 = ((bf16[4,160,512]{2,1,0:T(8,128)(2,1)}), bf16[4,160,512]{2,1,0:T(8,128)(2,1)S(1)}, u32[]{:S(2)}, u32[]{:S(2)}) async-start(bf16[4,160,512]{2,1,0:T(8,128)(2,1)} %bitcast.11), calls=%async_computation.2 | async-start | bytes 1310720 | tf_op jit(solution)/shard_map/sum_x/all_to_all | solution.py:178
  73.1 22.5 %collective-permute-start.5 = (bf16[40,512]{1,0:T(8,128)(2,1)S(1)}, bf16[40,512]{1,0:T(8,128)(2,1)S(1)}, u32[]{:S(2)}, u32[]{:S(2)}) collective-permute-start(bf16[40,512]{1,0:T(8,128)(2,1)S(1)} %slice_bitcast_fusion), channel_id=1, source_target_pairs={{0,64},{32,224},{64,128},{96,32},{128,192},{160,96},{192,0},{224,1... | collective-permute-start | bytes 122888 | tf_op jit(solution)/shard_map/in_z/ppermute | solution.py:176
  84.5 23.2 %collective-permute-start.4 = (bf16[40,512]{1,0:T(8,128)(2,1)S(1)}, bf16[40,512]{1,0:T(8,128)(2,1)S(1)}, u32[]{:S(2)}, u32[]{:S(2)}) collective-permute-start(bf16[40,512]{1,0:T(8,128)(2,1)S(1)} %get-tuple-element.40), channel_id=1, source_target_pairs={{0,64},{32,224},{64,128},{96,32},{128,192},{160,96},{192,0},{224,1... | collective-permute-start | bytes 122888 | tf_op jit(solution)/shard_map/sum_z/ppermute | solution.py:185
  107.7 19.8 %collective-permute-start.6 = (bf16[2,40,512]{2,1,0:T(8,128)(2,1)S(1)}, bf16[2,40,512]{2,1,0:T(8,128)(2,1)S(1)}, u32[]{:S(2)}, u32[]{:S(2)}) collective-permute-start(bf16[2,40,512]{2,1,0:T(8,128)(2,1)S(1)} %sum_z.1), channel_id=1, source_target_pairs={{0,64},{32,224},{64,128},{96,32},{128,192},{160,96},{192,0},{224,1... | collective-permute-start | bytes 245768 | tf_op jit(solution)/shard_map/sum_z/ppermute | solution.py:188

commit v8 on v7

--- a/solution.py
+++ b/solution.py
@@ -32,7 +32,7 @@
 along_core = [[row_of(x, h, c) for c in range(2)] for x in range(4) for h in range(4)]
 along_y = [[col_of(y, l) for y in range(4)] for l in range(8)]
 quads = [[col_of(y, 4 * s + k) for k in range(4)] for y in range(4) for s in range(2)]
-halves = [(col_of(y, l), col_of(y, l ^ 4)) for y in range(4) for l in range(8)]
+halves = [[col_of(y, k), col_of(y, k + 4)] for y in range(4) for k in range(4)]
 
 
 def restore_kernel(count_ref, slot_ref, values_ref, history_ref, restored_ref, updated_ref):
@@ -139,22 +139,18 @@
 
 def shards(saved_input, out_grad, weight, history_in, history_grad, slot_in, slot_grad, step_count):
     row = lax.axis_index("row")
-    col = lax.axis_index("col")
     h = jnp.bitwise_and(row >> 1, 3).reshape(1)
     core = jnp.bitwise_and(row, 1).reshape(1)
-    first = jnp.bitwise_and(col, 4) == 0
 
     grad, new_history_grad = restore(out_grad, history_grad, slot_grad, step_count)
     kept, new_history_in = restore(saved_input, history_in, slot_in, step_count)
 
+    with jax.named_scope("grad_z"):
+        pair = lax.all_gather(grad, "col", axis=0, axis_index_groups=halves)
+        line = spread(pair.reshape(80, 512), "col", quads)
     with jax.named_scope("in_pair"):
         paired = lax.ppermute(kept, "row", row_pairs(1))
-    with jax.named_scope("grad_z"):
-        far = lax.ppermute(grad, "col", halves)
-        far, paired = lax.optimization_barrier((far, paired))
-        pair = jnp.stack([jnp.where(first, grad, far), jnp.where(first, far, grad)])
-        line = spread(pair.reshape(80, 512), "col", quads)
-    both = jnp.stack([paired, kept])
+        both = jnp.stack([paired, kept])
     line, both = lax.optimization_barrier((line, both))
     with jax.named_scope("grad_y"):
         grads = spread(line.reshape(320, 512), "col", along_y)

time: 131 us -> 132 us (level)
  the two profiles are of different devices: /device:TPU:1 before, /device:TPU:9 now
where the time goes in v8:
time: 132 us; the launch traced here: 131 us
  starting transfers between devices  75.3 us (57%)
  blocking collectives  36 us (27%)
  waiting for transfers between devices  7.04 us (5%)
  Pallas kernels  5.49 us (4%)
  local copies, waits for them, and re-layouts  4.17 us (3%)
  between operations  2.74 us (2%)
    all_to_all x2, starting transfers between devices, spread(): return lax.all_to_all(copies, axis_name, 0, 0, axis_index_groups=groups)  16.2 us
    ppermute x1, starting transfers between devices, shards(): near_in = lax.ppermute(both, 'row', ring(1))  12.7 us
    ppermute x1, starting transfers between devices, shards(): got = lax.ppermute(sent, 'row', ring(1))  12.4 us
    ppermute x1, starting transfers between devices, shards(): far_in = lax.ppermute(near_in[0], 'row', ring(1))  12.3 us
    all_gather x1, blocking collectives, shards(): lax.all_gather(lines.reshape(160, 512), 'row', axis=0, tiled=True, axis_i...  12.1 us
    all_gather x1, blocking collectives, shards(): pair = lax.all_gather(grad, 'col', axis=0, axis_index_groups=halves)  8.94 us
    ppermute x1, starting transfers between devices, shards(): near = lax.ppermute(sent, 'row', ring(1))  8.92 us
    all_gather x2, blocking collectives, shards(): lax.all_gather(half, 'row', axis=0, axis_index_groups=along_core)  8.61 us
  transfers between devices with their start and end apart: 9, of which 4 were waited for; matrix products, arithmetic and copies ran while one was open for 0% of the time, Pallas kernels for 3%

profile of v8, /device:TPU:9, one launch (start us, length us, event | category | flops | bytes accessed | tf_op | source)
XLA Modules:
  0.0 131.4 jit_solution(7869924717215995853)
XLA Ops:
  1.9 0.9 copy-done.1
  2.8 0.7 copy-done.3
  4.1 8.9 %all-gather = bf16[80,512]{1,0:T(8,128)(2,1)S(1)} all-gather(bf16[40,512]{1,0:T(8,128)(2,1)S(1)} %get-tuple-element.25), channel_id=2, replica_groups={{0,4},{1,5},{2,6},{3,7},{8,12},{9,13},{10,14},{11,15},{16,20},{17,21},{..., dimensions={0}, use_global_device_ids=true | all-gather | bytes 122880 | tf_op jit(solution)/shard_map/grad_z/all_gather | solution.py:149
  13.0 0.7 broadcast_in_dim.15
  13.8 6.7 %all-to-all-start = ((bf16[4,80,512]{2,1,0:T(8,128)(2,1)}), bf16[4,80,512]{2,1,0:T(8,128)(2,1)S(1)}, u32[]{:S(2)}, u32[]{:S(2)}) async-start(bf16[4,80,512]{2,1,0:T(8,128)(2,1)} %broadcast_in_dim.15), calls=%async_computation | async-start | bytes 655360 | tf_op jit(solution)/shard_map/grad_z/all_to_all | solution.py:137
  22.4 2.8 %collective-permute-start = (bf16[40,512]{1,0:T(8,128)(2,1)S(1)}, bf16[40,512]{1,0:T(8,128)(2,1)S(1)}, u32[]{:S(2)}, u32[]{:S(2)}) collective-permute-start(bf16[40,512]{1,0:T(8,128)(2,1)S(1)} %get-tuple-element.26), channel_id=1, source_target_pairs={{0,32},{32,0},{64,96},{96,64},{128,160},{160,128},{192,224},{224,1... | collective-permute-start | bytes 122888 | tf_op jit(solution)/shard_map/in_pair/ppermute | solution.py:152
  25.2 0.8 collective-permute-done.paired
  26.1 3.0 %all-to-all-done = bf16[4,80,512]{2,1,0:T(8,128)(2,1)S(1)} async-done(((bf16[4,80,512]{2,1,0:T(8,128)(2,1)}), bf16[4,80,512]{2,1,0:T(8,128)(2,1)S(1)}, u32[]{:S(2)}, u32[]{:S(2)}) %all-to-all-start) | async-done | bytes 327712 | tf_op jit(solution)/shard_map/grad_z/all_to_all | solution.py:137
  29.1 1.2 broadcast_in_dim.17
  30.3 9.6 %all-to-all-start.1 = ((bf16[4,320,512]{2,1,0:T(8,128)(2,1)}), bf16[4,320,512]{2,1,0:T(8,128)(2,1)S(1)}, u32[]{:S(2)}, u32[]{:S(2)}) async-start(bf16[4,320,512]{2,1,0:T(8,128)(2,1)} %broadcast_in_dim.17), calls=%async_computation.1 | async-start | bytes 2621440 | tf_op jit(solution)/shard_map/grad_y/all_to_all | solution.py:137
  39.8 12.7 %collective-permute-start.1 = (bf16[2,40,512]{2,1,0:T(8,128)(2,1)S(1)}, bf16[2,40,512]{2,1,0:T(8,128)(2,1)S(1)}, u32[]{:S(2)}, u32[]{:S(2)}) collective-permute-start(bf16[2,40,512]{2,1,0:T(8,128)(2,1)S(1)} %pad_maximum_fusion), channel_id=1, source_target_pairs={{0,64},{32,224},{64,128},{96,32},{128,192},{160,96},{192,0},{224,1... | collective-permute-start | bytes 245768 | tf_op jit(solution)/shard_map/in_z/ppermute | solution.py:158
  52.6 1.5 %all-to-all-done.1 = bf16[4,320,512]{2,1,0:T(8,128)(2,1)S(1)} async-done(((bf16[4,320,512]{2,1,0:T(8,128)(2,1)}), bf16[4,320,512]{2,1,0:T(8,128)(2,1)S(1)}, u32[]{:S(2)}, u32[]{:S(2)}) %all-to-all-start.1) | async-done | bytes 1310752 | tf_op jit(solution)/shard_map/grad_y/all_to_all | solution.py:137
  54.7 5.8 %collective-permute-start.2 = (bf16[640,512]{1,0:T(8,128)(2,1)S(1)}, bf16[640,512]{1,0:T(8,128)(2,1)S(1)}, u32[]{:S(2)}, u32[]{:S(2)}) collective-permute-start(bf16[640,512]{1,0:T(8,128)(2,1)S(1)} %sum_core.2), channel_id=1, source_target_pairs={{0,32},{32,0},{64,96},{96,64},{128,160},{160,128},{192,224},{224,1... | collective-permute-start | bytes 1966088 | tf_op jit(solution)/shard_map/sum_core/ppermute | solution.py:167
  60.5 1.7 %collective-permute-done.2.got = bf16[640,512]{1,0:T(8,128)(2,1)S(1)} collective-permute-done((bf16[640,512]{1,0:T(8,128)(2,1)S(1)}, bf16[640,512]{1,0:T(8,128)(2,1)S(1)}, u32[]{:S(2)}, u32[]{:S(2)}) %collective-permute-start.2) | collective-permute-done | bytes 655392 | tf_op jit(solution)/shard_map/sum_core/ppermute | solution.py:167
  62.2 1.3 %sum_core.3 = bf16[640,512]{1,0:T(8,128)(2,1)} custom-call(bf16[640,512]{1,0:T(8,128)(2,1)S(1)} %bitcast.25, bf16[512,512]{1,0:T(8,128)(2,1)S(1)} %copy-done, bf16[640,512]{1,0:T(8,128)(2,1)S(1)} %collective-permute-done.2.got), custom_call_target="tpu_custom_call" | custom-call | flops 1024 | bytes 1024 | tf_op jit(solution)/shard_map/sum_core/pallas_call | solution.py:71
  63.5 4.0 %all-to-all-start.2 = ((bf16[4,160,512]{2,1,0:T(8,128)(2,1)}), bf16[4,160,512]{2,1,0:T(8,128)(2,1)S(1)}, u32[]{:S(2)}, u32[]{:S(2)}) async-start(bf16[4,160,512]{2,1,0:T(8,128)(2,1)} %bitcast.8), calls=%async_computation.2 | async-start | bytes 1310720 | tf_op jit(solution)/shard_map/sum_x/all_to_all | solution.py:174
  67.6 12.3 %collective-permute-start.4 = (bf16[40,512]{1,0:T(8,128)(2,1)S(1)}, bf16[40,512]{1,0:T(8,128)(2,1)S(1)}, u32[]{:S(2)}, u32[]{:S(2)}) collective-permute-start(bf16[40,512]{1,0:T(8,128)(2,1)S(1)} %slice_bitcast_fusion), channel_id=1, source_target_pairs={{0,64},{32,224},{64,128},{96,32},{128,192},{160,96},{192,0},{224,1... | collective-permute-start | bytes 122888 | tf_op jit(solution)/shard_map/in_z/ppermute | solution.py:172
  80.0 12.4 %collective-permute-start.3 = (bf16[40,512]{1,0:T(8,128)(2,1)S(1)}, bf16[40,512]{1,0:T(8,128)(2,1)S(1)}, u32[]{:S(2)}, u32[]{:S(2)}) collective-permute-start(bf16[40,512]{1,0:T(8,128)(2,1)S(1)} %get-tuple-element.36), channel_id=1, source_target_pairs={{0,64},{32,224},{64,128},{96,32},{128,192},{160,96},{192,0},{224,1... | collective-permute-start | bytes 122888 | tf_op jit(solution)/shard_map/sum_z/ppermute | solution.py:181
  92.4 12.1 %all_gather.26 = bf16[640,512]{1,0:T(8,128)(2,1)S(1)} all-gather(bf16[160,512]{1,0:T(8,128)(2,1)S(1)} %bitcast.29), channel_id=1, replica_groups={{0,256,512,768},{32,288,544,800},{64,320,576,832},{96,352,608,864},{128..., dimensions={0}, use_global_device_ids=true | all-gather | bytes 819200 | tf_op jit(solution)/shard_map/in_x/all_gather | solution.py:179
  104.5 8.9 %collective-permute-start.5 = (bf16[2,40,512]{2,1,0:T(8,128)(2,1)S(1)}, bf16[2,40,512]{2,1,0:T(8,128)(2,1)S(1)}, u32[]{:S(2)}, u32[]{:S(2)}) collective-permute-start(bf16[2,40,512]{2,1,0:T(8,128)(2,1)S(1)} %sum_z.1), channel_id=1, source_target_pairs={{0,64},{32,224},{64,128},{96,32},{128,192},{160,96},{192,0},{224,1... | collective-permute-start | bytes 245768 | tf_op jit(solution)/shard_map/sum_z/ppermute | solution.py:184
  113.5 6.3 %all-gather.1 = bf16[640,512]{1,0:T(8,128)(2,1)S(1)} all-gather(bf16[320,512]{1,0:T(8,128)(2,1)S(1)} %get-tuple-element.47), channel_id=3, replica_groups={{0,32},{64,96},{128,160},{192,224},{256,288},{320,352},{384,416},{448,4..., dimensions={0}, use_global_device_ids=true | all-gather | bytes 983040 | tf_op jit(solution)/shard_map/in_core/all_gather | solution.py:187
  119.8 2.3 %all-gather.2 = bf16[640,512]{1,0:T(8,128)(2,1)S(1)} all-gather(bf16[320,512]{1,0:T(8,128)(2,1)S(1)} %get-tuple-element.46), channel_id=4, replica_groups={{0,32},{64,96},{128,160},{192,224},{256,288},{320,352},{384,416},{448,4..., dimensions={0}, use_global_device_ids=true | all-gather | bytes 983040 | tf_op jit(solution)/shard_map/in_core/all_gather | solution.py:187
  122.1 2.2 %outer.1 = f32[512,512]{1,0:T(8,128)} custom-call(s32[1]{0:T(128)} %bitcast.1.core, bf16[640,512]{1,0:T(8,128)(2,1)S(1)} %bitcast.26, bf16[640,512]{1,0:T(8,128)(2,1)S(1)} %bitcast.24, bf16[2,320,512]{2,1,0:T(8,128)(2,1)S(1)} %bitcast.27, bf16[2,320,512]{2,1,0:T(8,128)(2,1)S(1)} %bitcast.28), custom_call_target="tpu_custom_call" | custom-call | flops 1024 | bytes 1024 | tf_op jit(solution)/shard_map/outer/pallas_call | solution.py:71
  124.3 6.4 %all_gather.31 = bf16[2,40,512]{2,1,0:T(8,128)(2,1)S(1)} all-gather(bf16[1,40,512]{2,1,0:T(8,128)(2,1)S(1)} %slice.25), channel_id=1, replica_groups={{0,32},{64,96},{128,160},{192,224},{256,288},{320,352},{384,416},{448,4..., dimensions={0}, use_global_device_ids=true | all-gather | bytes 122880 | tf_op jit(solution)/shard_map/sum_z/all_gather | solution.py:194
  (25 shorter events, 3.3 us)
Async XLA Ops:
  1.9 0.9 copy-start.1
  2.8 0.7 copy-start.3
  3.5 17.6 %copy-start.2 = (f32[40,512]{1,0:T(8,128)S(1)}, f32[40,512]{1,0:T(8,128)}, u32[]{:S(2)}) copy-start(f32[40,512]{1,0:T(8,128)} %values_ref.3) | copy-start | bytes 245764
  13.8 15.4 %all-to-all-start = ((bf16[4,80,512]{2,1,0:T(8,128)(2,1)}), bf16[4,80,512]{2,1,0:T(8,128)(2,1)S(1)}, u32[]{:S(2)}, u32[]{:S(2)}) async-start(bf16[4,80,512]{2,1,0:T(8,128)(2,1)} %broadcast_in_dim.15), calls=%async_computation | async-start | bytes 655360 | tf_op jit(solution)/shard_map/grad_z/all_to_all | solution.py:137
  21.1 0.7 copy-start.4
  22.4 3.7 %collective-permute-start = (bf16[40,512]{1,0:T(8,128)(2,1)S(1)}, bf16[40,512]{1,0:T(8,128)(2,1)S(1)}, u32[]{:S(2)}, u32[]{:S(2)}) collective-permute-start(bf16[40,512]{1,0:T(8,128)(2,1)S(1)} %get-tuple-element.26), channel_id=1, source_target_pairs={{0,32},{32,0},{64,96},{96,64},{128,160},{160,128},{192,224},{224,1... | collective-permute-start | bytes 122888 | tf_op jit(solution)/shard_map/in_pair/ppermute | solution.py:152
  30.3 23.7 %all-to-all-start.1 = ((bf16[4,320,512]{2,1,0:T(8,128)(2,1)}), bf16[4,320,512]{2,1,0:T(8,128)(2,1)S(1)}, u32[]{:S(2)}, u32[]{:S(2)}) async-start(bf16[4,320,512]{2,1,0:T(8,128)(2,1)} %broadcast_in_dim.17), calls=%async_computation.1 | async-start | bytes 2621440 | tf_op jit(solution)/shard_map/grad_y/all_to_all | solution.py:137
  39.8 14.3 %copy-start = (bf16[512,512]{1,0:T(8,128)(2,1)S(1)}, bf16[512,512]{1,0:T(8,128)(2,1)}, u32[]{:S(2)}) copy-start(bf16[512,512]{1,0:T(8,128)(2,1)} %weight.3) | copy-start | bytes 1572868
  39.8 14.8 %collective-permute-start.1 = (bf16[2,40,512]{2,1,0:T(8,128)(2,1)S(1)}, bf16[2,40,512]{2,1,0:T(8,128)(2,1)S(1)}, u32[]{:S(2)}, u32[]{:S(2)}) collective-permute-start(bf16[2,40,512]{2,1,0:T(8,128)(2,1)S(1)} %pad_maximum_fusion), channel_id=1, source_target_pairs={{0,64},{32,224},{64,128},{96,32},{128,192},{160,96},{192,0},{224,1... | collective-permute-start | bytes 245768 | tf_op jit(solution)/shard_map/in_z/ppermute | solution.py:158
  54.7 7.5 %collective-permute-start.2 = (bf16[640,512]{1,0:T(8,128)(2,1)S(1)}, bf16[640,512]{1,0:T(8,128)(2,1)S(1)}, u32[]{:S(2)}, u32[]{:S(2)}) collective-permute-start(bf16[640,512]{1,0:T(8,128)(2,1)S(1)} %sum_core.2), channel_id=1, source_target_pairs={{0,32},{32,0},{64,96},{96,64},{128,160},{160,128},{192,224},{224,1... | collective-permute-start | bytes 1966088 | tf_op jit(solution)/shard_map/sum_core/ppermute | solution.py:167
  63.5 16.4 %all-to-all-start.2 = ((bf16[4,160,512]{2,1,0:T(8,128)(2,1)}), bf16[4,160,512]{2,1,0:T(8,128)(2,1)S(1)}, u32[]{:S(2)}, u32[]{:S(2)}) async-start(bf16[4,160,512]{2,1,0:T(8,128)(2,1)} %bitcast.8), calls=%async_computation.2 | async-start | bytes 1310720 | tf_op jit(solution)/shard_map/sum_x/all_to_all | solution.py:174
  67.6 24.8 %collective-permute-start.4 = (bf16[40,512]{1,0:T(8,128)(2,1)S(1)}, bf16[40,512]{1,0:T(8,128)(2,1)S(1)}, u32[]{:S(2)}, u32[]{:S(2)}) collective-permute-start(bf16[40,512]{1,0:T(8,128)(2,1)S(1)} %slice_bitcast_fusion), channel_id=1, source_target_pairs={{0,64},{32,224},{64,128},{96,32},{128,192},{160,96},{192,0},{224,1... | collective-permute-start | bytes 122888 | tf_op jit(solution)/shard_map/in_z/ppermute | solution.py:172
  80.0 24.5 %collective-permute-start.3 = (bf16[40,512]{1,0:T(8,128)(2,1)S(1)}, bf16[40,512]{1,0:T(8,128)(2,1)S(1)}, u32[]{:S(2)}, u32[]{:S(2)}) collective-permute-start(bf16[40,512]{1,0:T(8,128)(2,1)S(1)} %get-tuple-element.36), channel_id=1, source_target_pairs={{0,64},{32,224},{64,128},{96,32},{128,192},{160,96},{192,0},{224,1... | collective-permute-start | bytes 122888 | tf_op jit(solution)/shard_map/sum_z/ppermute | solution.py:181
  104.5 19.8 %collective-permute-start.5 = (bf16[2,40,512]{2,1,0:T(8,128)(2,1)S(1)}, bf16[2,40,512]{2,1,0:T(8,128)(2,1)S(1)}, u32[]{:S(2)}, u32[]{:S(2)}) collective-permute-start(bf16[2,40,512]{2,1,0:T(8,128)(2,1)S(1)} %sum_z.1), channel_id=1, source_target_pairs={{0,64},{32,224},{64,128},{96,32},{128,192},{160,96},{192,0},{224,1... | collective-permute-start | bytes 245768 | tf_op jit(solution)/shard_map/sum_z/ppermute | solution.py:184
